TPU v7x, 256 devices: a whole 4x4x8 slice. The times are simulated.
256 devices in a mesh: axial: 16 (over z, core), depth: 16 (over x, y).
Axes of the slice: x: 4, y: 4, z: 8, core: 2. Of those that a mesh axis runs over, the one named last changes fastest.
Arguments:
- kelvin_before_step: float32 [256, 128, 2048], P('axial', 'depth'), may hold values from -3 to 3
- unburnt_resin_share: float32 [256, 128, 2048], P('axial', 'depth'), may hold values from 0.2 to 1
- deposited_energy_amount: float32 [256, 128, 2048], P('axial', 'depth'), may hold values from -6 to 6
- material_label: int32 [256, 128, 2048], P('axial', 'depth'), may hold values from 0 to 7
- zonal_diffusivity: float32 [8], replicated, may hold values from 0.5 to 2
- zonal_storage_coefficient: float32 [8], replicated, may hold values from 0.05 to 0.5
- frequency_coefficient: float32 [8], replicated, may hold values from 0.2 to 2
- arrhenius_barrier: float32 [8], replicated, may hold values from 1 to 4
- stream_keeper: int32 [256, 2048], P('axial', 'depth'), may hold values from 0 to 15, as said below
- keeper_position: int32 [256, 2048], P('axial', 'depth'), may hold values from 0 to 4095, as said below
Outputs:
- kelvin_after_step: float32 [256, 128, 2048], P('axial', 'depth')
- delivered_blowing: float32 [1048576], P(('axial', 'depth'))
Inputs may be any that keep to these rules, and one draw needn't show every extreme that they name: `stream_keeper`: each flow owner takes the surface faces of one contiguous range of axial rows, the same at every azimuth; different owners take different ranges; every owner holds at least 8 rows and at most 32, and one owner holds exactly 32. `keeper_position`: within one azimuth slice of 128 columns, the faces of one owner hold the distinct slots 0 to their count - 1, in an order unrelated to position.
All inputs are finite; a program needn't handle non-finite values.
Results may differ from a plain program's by a relative error of at most 0.00014.
Values sent between devices are 32-bit elements; how exact they have to be, the bound alone decides.
No kernel may reach another device: no remote copies, remote signals or barrier semaphores. Data moves between devices by JAX's collectives and lax.ppermute only.
A program may use at most 128 MiB of HBM per device.

v0:
```python
import jax
import jax.numpy as jnp
from jax import lax
from jax.sharding import PartitionSpec as P

NEWTON = 3
SWEEPS = 4


lengthwise_coupling_table = 1.0
circumferential_coupling_table = 1.0
layerwise_coupling_table = 2.0
charring_enthalpy = 0.5
outgassing_advection_enthalpy = 4.0


def carried_in(part, axis, combine, identity):
    count = lax.axis_size(axis)
    place = lax.axis_index(axis)
    ahead = count - 1 - place
    gathered = lax.all_gather(part, axis)
    state = jnp.zeros_like(part) + jnp.asarray(identity, part.dtype)

    def one(turn, state):
        source = count - 1 - turn
        return combine(state, lax.dynamic_index_in_dim(gathered, source, 0, False))

    return lax.fori_loop(0, ahead, one, state)


def extended(cells, sides, width):
    for axis, dim in sides:
        count = lax.axis_size(axis)
        ends = count - 1
        head = lax.slice_in_dim(cells, 0, width, axis=dim)
        tail = lax.slice_in_dim(cells, cells.shape[dim] - width, cells.shape[dim], axis=dim)
        cells = jnp.concatenate(
            [
                lax.ppermute(tail, axis, [(i, (i + 1) % count) for i in range(ends)]),
                cells,
                lax.ppermute(head, axis, [((i + 1) % count, i) for i in range(ends)]),
            ],
            axis=dim,
        )
    return cells


def lookup(material_label, table):
    result = jnp.zeros(material_label.shape, jnp.float32)
    for number in range(table.shape[0]):
        result = jnp.where(material_label == number, table[number], result)
    return result


def combine_sum(earlier, later):
    return earlier + later


def coupling_components(bordered_kelvin_values):
    interior_portion = bordered_kelvin_values[1:-1, 1:-1]
    lengthwise_couple = bordered_kelvin_values[2:, 1:-1] + bordered_kelvin_values[:-2, 1:-1]
    circumferential_couple = jnp.roll(interior_portion, 1, axis=2) + jnp.roll(
        interior_portion, -1, axis=2
    )
    return (
        lengthwise_couple,
        circumferential_couple,
        bordered_kelvin_values[1:-1, 2:],
        bordered_kelvin_values[1:-1, :-2],
    )


def charring_production(
    kelvin_after_step, frequency_coefficient_grid, arrhenius_barrier_grid, unburnt_resin_share
):
    smoothed_kelvin_values = 1.0 + jnp.abs(kelvin_after_step)
    charring_speed = (
        frequency_coefficient_grid
        * unburnt_resin_share
        * jnp.exp(arrhenius_barrier_grid * kelvin_after_step / smoothed_kelvin_values)
    )
    speed_sensitivity = (
        charring_speed * arrhenius_barrier_grid / (smoothed_kelvin_values * smoothed_kelvin_values)
    )
    return (charring_speed, speed_sensitivity)


def sweep_value(iterative_mismatch, diagonal, transfer_coefficient, gas_term, padded_update):
    pair_a, pair_z, deeper_up, shallower_up = coupling_components(padded_update)
    return (
        -iterative_mismatch
        + transfer_coefficient
        * (
            lengthwise_coupling_table * pair_a
            + circumferential_coupling_table * pair_z
            + layerwise_coupling_table * (deeper_up + shallower_up)
        )
        + gas_term * deeper_up
    ) / diagonal


def shards(
    kelvin_before_step,
    unburnt_resin_share,
    deposited_energy_amount,
    material_label,
    zonal_diffusivity,
    zonal_storage_coefficient,
    frequency_coefficient,
    arrhenius_barrier,
    stream_keeper,
    keeper_position,
):
    transfer_coefficient = lookup(material_label, zonal_diffusivity)
    storage_coefficient = lookup(material_label, zonal_storage_coefficient)
    frequency_coefficient_grid = lookup(material_label, frequency_coefficient)
    arrhenius_barrier_grid = lookup(material_label, arrhenius_barrier)
    layer_spacing = 1.0 / (kelvin_before_step.shape[1] * lax.axis_size("depth"))
    spokes = 2.0 * (
        lengthwise_coupling_table + circumferential_coupling_table + layerwise_coupling_table
    )
    kelvin_after_step = kelvin_before_step
    for iteration in range(NEWTON):
        charring_speed, speed_sensitivity = charring_production(
            kelvin_after_step,
            frequency_coefficient_grid,
            arrhenius_barrier_grid,
            unburnt_resin_share,
        )
        column_own = jnp.sum(charring_speed, axis=1)
        from_below = carried_in(column_own, "depth", combine_sum, jnp.zeros_like(column_own))
        outgassing_mass_stream = (
            from_below[:, None, :] + column_own[:, None, :] - jnp.cumsum(charring_speed, axis=1)
        ) * layer_spacing
        bordered_kelvin_values = extended(kelvin_after_step, (("axial", 0), ("depth", 1)), 1)
        lengthwise_couple, circumferential_couple, inward_layer_value, outward_layer_value = (
            coupling_components(bordered_kelvin_values)
        )
        iterative_mismatch = (
            storage_coefficient * (kelvin_after_step - kelvin_before_step)
            - transfer_coefficient
            * (
                lengthwise_coupling_table * (lengthwise_couple - 2.0 * kelvin_after_step)
                + circumferential_coupling_table
                * (circumferential_couple - 2.0 * kelvin_after_step)
                + layerwise_coupling_table
                * (inward_layer_value + outward_layer_value - 2.0 * kelvin_after_step)
            )
            + charring_enthalpy * charring_speed
            + outgassing_advection_enthalpy
            * outgassing_mass_stream
            * (kelvin_after_step - inward_layer_value)
            - deposited_energy_amount
        )
        diagonal = (
            storage_coefficient
            + transfer_coefficient * spokes
            + charring_enthalpy * speed_sensitivity
            + outgassing_advection_enthalpy * outgassing_mass_stream
        )
        gas_term = outgassing_advection_enthalpy * outgassing_mass_stream
        iterative_correction = -iterative_mismatch / diagonal
        for sweep_index in range(1, SWEEPS):
            widened = extended(iterative_correction, (("axial", 0), ("depth", 1)), 1)
            iterative_correction = sweep_value(
                iterative_mismatch, diagonal, transfer_coefficient, gas_term, widened
            )
        kelvin_after_step = kelvin_after_step + iterative_correction
    charring_speed, speed_sensitivity = charring_production(
        kelvin_after_step, frequency_coefficient_grid, arrhenius_barrier_grid, unburnt_resin_share
    )
    totals = lax.psum_scatter(
        jnp.sum(charring_speed, axis=1), "depth", scatter_dimension=1, tiled=True
    )
    blowing = totals * layer_spacing
    own_cap = 2 * stream_keeper.shape[0] * stream_keeper.shape[1]
    flat_keys = stream_keeper * own_cap + keeper_position
    senders = lax.axis_size("axial")
    slot_buffer = (
        jnp.zeros((senders * own_cap,), jnp.float32)
        .at[flat_keys.reshape(-1)]
        .set(blowing.reshape(-1))
    )
    delivered_blowing = lax.psum_scatter(slot_buffer, "axial", scatter_dimension=0, tiled=True)
    return (kelvin_after_step, delivered_blowing)


def solution(mesh):
    in_specs = (
        P("axial", "depth", None),
        P("axial", "depth", None),
        P("axial", "depth", None),
        P("axial", "depth", None),
        P(),
        P(),
        P(),
        P(),
        P("axial", "depth"),
        P("axial", "depth"),
    )
    out_specs = (P("axial", "depth", None), P(("axial", "depth")))
    return jax.shard_map(shards, mesh=mesh, in_specs=in_specs, out_specs=out_specs, check_vma=False)
```

profile of v0, /device:TPU:1, one launch (start us, length us, event | category | flops | bytes accessed | tf_op | source)
XLA Modules:
  0.0 650.6 jit_solution(3750951211041456868)
XLA Ops:
  10.5 16.9 %fusion.145 = (f32[16,2048]{1,0:T(8,128)}, f32[16,8,2048]{2,0,1:T(8,128)}, f32[16,8,2048]{2,0,1:T(8,128)S(1)}, f32[16,8,2048]{2,0,1:T(8,128)}, pred[16,8,2048]{2...) fusion(f32[16,8,2048]{2,1,0:T(8,128)} %param.16, ...), kind=kLoop, calls=%fused_computation.319 | loop fusion | flops 8093696 | bytes 8519744 | tf_op jit(solution)/shard_map/reduce_sum | solution.py:130
  28.1 5.1 collective-permute-start
  34.0 1.9 collective-permute-start.1
  42.1 3.0 collective-permute-start.3
  46.4 36.8 %all-gather.7.cloned.1.call-done = f32[256,2048]{1,0:T(8,128)} async-done(((f32[16,2048]{1,0:T(8,128)}), f32[256,2048]{1,0:T(8,128)}) %all-gather.7.cloned.1.call-update) | async-done | bytes 2097168 | tf_op jit(solution)/shard_map/all_gather | solution.py:21
  83.2 14.4 %while.36 = (s32[]{:T(128)}, f32[16,2048]{1,0:T(8,128)S(1)}, s32[]{:T(128)}, f32[16,16,2048]{2,1,0:T(8,128)}, s32[]{:T(128)}, /*index=5*/s32[]{:T(128)}, s32[]{:T(128)}, s32[]{:T(128)}) while((s32[]{:T(128)}, f32[16,2048]{1,0:T(8,128)S(1)}, s32[]{:T(128)}, f32[16,16,2048]{2,1,0:T(8,128)}, s32[]{:T(128)}, /*index=5*/s32[]{:T(128)}, s32[]{:T(128)}, ...), condition=%wide.region_2.3_spmd, body=%wide.region_1.2_spmd.sunk | while | flops 32774 | bytes 393359 | solution.py:28
  98.4 19.8 %fusion.143 = (f32[16,8,2048]{2,0,1:T(8,128)S(1)}, f32[16,8,2048]{2,0,1:T(8,128)S(1)}, f32[16,8,2048]{2,0,1:T(8,128)S(1)}, f32[16,8,2048]{2,0,1:T(8,128)S(1)}, f...) fusion(f32[16,8,2048]{2,1,0:T(8,128)} %param.18, f32[16,8,2048]{2,0,1:T(8,128)} %copy-done.4, ...), kind=kOutput, calls=%fused_computation.318 | output fusion | flops 17563648 | bytes 16285760 | tf_op jit(solution)/shard_map/jit(cumsum)/reduce_window_sum | solution.py:133
  118.3 3.4 collective-permute-start.4
  121.7 3.1 collective-permute-start.5
  126.1 1.8 collective-permute-start.7
  129.4 2.7 collective-permute-done.7
  132.1 4.1 collective-permute-done.6
  137.3 2.3 collective-permute-start.8
  139.6 3.7 collective-permute-start.9
  144.6 1.9 collective-permute-start.11
  149.4 4.1 collective-permute-done.10
  154.6 1.9 collective-permute-start.12
  156.6 5.6 collective-permute-start.13
  163.4 2.9 collective-permute-start.15
  168.9 3.8 collective-permute-done.14
  172.7 4.0 fusion.141
  176.9 1.9 collective-permute-start.16
  178.9 7.1 %collective-permute-start.17 = (f32[1,8,2048]{2,0,1:T(1,128)S(1)}, f32[1,8,2048]{2,0,1:T(1,128)S(1)}, u32[]{:S(2)}, u32[]{:S(2)}) collective-permute-start(f32[1,8,2048]{2,0,1:T(1,128)S(1)} %get-tuple-element.300), channel_id=1, source_target_pairs={{0,16},{16,32},{32,48},{48,64},{64,80},{80,96},{96,112},{112,128},... | collective-permute-start | bytes 196616 | tf_op jit(solution)/shard_map/ppermute | solution.py:39
  189.2 4.7 collective-permute-start.19
  195.2 36.6 %all-gather.9.cloned.1.call-done = f32[256,2048]{1,0:T(8,128)} async-done(((f32[16,2048]{1,0:T(8,128)}), f32[256,2048]{1,0:T(8,128)}) %all-gather.9.cloned.1.call-update) | async-done | bytes 2097168 | tf_op jit(solution)/shard_map/all_gather | solution.py:21
  231.8 14.4 %while.37 = (s32[]{:T(128)}, f32[16,2048]{1,0:T(8,128)S(1)}, s32[]{:T(128)}, f32[16,16,2048]{2,1,0:T(8,128)}, s32[]{:T(128)}, /*index=5*/s32[]{:T(128)}, s32[]{:T(128)}, s32[]{:T(128)}) while((s32[]{:T(128)}, f32[16,2048]{1,0:T(8,128)S(1)}, s32[]{:T(128)}, f32[16,16,2048]{2,1,0:T(8,128)}, s32[]{:T(128)}, /*index=5*/s32[]{:T(128)}, s32[]{:T(128)}, ...), condition=%wide.region_6.7_spmd, body=%wide.region_5.6_spmd.sunk | while | flops 32774 | bytes 393359 | solution.py:28
  246.3 6.0 fusion.139
  252.4 3.4 collective-permute-start.20
  255.8 3.1 collective-permute-start.21
  260.2 1.8 collective-permute-start.23
  263.5 2.7 collective-permute-done.23
  266.1 4.1 collective-permute-done.22
  271.3 2.3 collective-permute-start.24
  273.7 3.7 collective-permute-start.25
  278.7 1.9 collective-permute-start.27
  283.5 4.1 collective-permute-done.26
  288.7 1.9 collective-permute-start.28
  290.6 5.5 collective-permute-start.29
  297.5 2.9 collective-permute-start.31
  303.0 3.8 collective-permute-done.30
  306.8 3.4 fusion.137
  310.5 1.9 collective-permute-start.32
  312.4 7.1 %collective-permute-start.33 = (f32[1,8,2048]{2,0,1:T(1,128)S(1)}, f32[1,8,2048]{2,0,1:T(1,128)S(1)}, u32[]{:S(2)}, u32[]{:S(2)}) collective-permute-start(f32[1,8,2048]{2,0,1:T(1,128)S(1)} %get-tuple-element.276), channel_id=1, source_target_pairs={{0,16},{16,32},{32,48},{48,64},{64,80},{80,96},{96,112},{112,128},... | collective-permute-start | bytes 196616 | tf_op jit(solution)/shard_map/ppermute | solution.py:39
  322.7 4.9 collective-permute-start.35
  329.0 36.3 %all-gather.11.cloned.1.call-done = f32[256,2048]{1,0:T(8,128)} async-done(((f32[16,2048]{1,0:T(8,128)}), f32[256,2048]{1,0:T(8,128)}) %all-gather.11.cloned.1.call-update) | async-done | bytes 2097168 | tf_op jit(solution)/shard_map/all_gather | solution.py:21
  365.3 14.4 %while.38 = (s32[]{:T(128)}, f32[16,2048]{1,0:T(8,128)S(1)}, s32[]{:T(128)}, f32[16,16,2048]{2,1,0:T(8,128)}, s32[]{:T(128)}, /*index=5*/s32[]{:T(128)}, s32[]{:T(128)}, s32[]{:T(128)}) while((s32[]{:T(128)}, f32[16,2048]{1,0:T(8,128)S(1)}, s32[]{:T(128)}, f32[16,16,2048]{2,1,0:T(8,128)}, s32[]{:T(128)}, /*index=5*/s32[]{:T(128)}, ...), condition=%wide.region_10.11_spmd, body=%wide.region_9.10_spmd.sunk | while | flops 32774 | bytes 393359 | solution.py:28
  379.8 6.0 fusion.135
  385.9 3.4 collective-permute-start.36
  389.3 3.1 collective-permute-start.37
  397.0 2.7 collective-permute-done.39
  399.6 4.1 collective-permute-done.38
  404.8 2.3 collective-permute-start.40
  407.2 3.7 collective-permute-start.41
  412.2 1.9 collective-permute-start.43
  417.0 4.1 collective-permute-done.42
  422.2 1.9 collective-permute-start.44
  424.1 5.5 collective-permute-start.45
  431.0 2.9 collective-permute-start.47
  436.5 3.8 collective-permute-done.46
  440.3 3.5 multiply_reduce_fusion
  443.9 79.4 %reduce-scatter.2.cloned.1.call-done = f32[16,128]{1,0:T(8,128)} async-done(((f32[16,2048]{1,0:T(8,128)}), f32[16,128]{1,0:T(8,128)}) %reduce-scatter.2.cloned.1.call-update) | async-done | bytes 8208 | tf_op jit(solution)/shard_map/reduce_scatter | solution.py:172
  523.9 8.7 %scatter_custom_fusion = f32[65536]{0:T(1024)} fusion(s32[2048]{0:T(1024)S(1)} %bitcast.59, f32[2048]{0:T(1024)S(1)} %multiply_bitcast_fusion, f32[]{:T(128)} %constant.111.clone.1), kind=kCustom, calls=%fused_computation.309 | custom fusion | bytes 262148 | tf_op jit(solution)/shard_map/scatter | solution.py:182
  533.9 2.8 copy.42
  536.8 106.0 %all-reduce.3.cloned.1.call-done = f32[65536]{0:T(1024)} async-done(((f32[65536]{0:T(1024)}), f32[65536]{0:T(1024)}) %all-reduce.3.cloned.1.call-update) | async-done | bytes 262160
  (212 shorter events, 108.1 us)
Async XLA Ops:
  7.2 76.0 %all-gather.7.cloned.1.call-start = ((), (), s32[]{:S(2)}) async-start(), calls=%async_computation.2 | async-start | bytes 2228224 | tf_op jit(solution)/shard_map/all_gather | solution.py:21
  10.5 16.9 %copy-start.2 = (f32[16,8,2048]{2,1,0:T(8,128)S(1)}, f32[16,8,2048]{2,1,0:T(8,128)}, u32[]{:S(2)}) copy-start(f32[16,8,2048]{2,1,0:T(8,128)} %param.16) | copy-start | bytes 3145732
  27.4 204.4 %all-gather.9.cloned.1.call-start = ((), (), s32[]{:S(2)}) async-start(), calls=%async_computation.3 | async-start | bytes 2228224 | tf_op jit(solution)/shard_map/all_gather | solution.py:21
  28.1 12.3 %collective-permute-start = (f32[1,8,2048]{2,0,1:T(1,128)}, f32[1,8,2048]{2,0,1:T(1,128)}, u32[]{:S(2)}, u32[]{:S(2)}) collective-permute-start(f32[1,8,2048]{2,0,1:T(1,128)} %copy.22), channel_id=1, source_target_pairs={{16,0},{32,16},{48,32},{64,48},{80,64},{96,80},{112,96},{128,112},... | collective-permute-start | bytes 196616 | tf_op jit(solution)/shard_map/ppermute | solution.py:41
  34.0 6.5 %collective-permute-start.1 = (f32[1,8,2048]{2,0,1:T(1,128)}, f32[1,8,2048]{2,0,1:T(1,128)}, u32[]{:S(2)}, u32[]{:S(2)}) collective-permute-start(f32[1,8,2048]{2,0,1:T(1,128)} %copy.24), channel_id=1, source_target_pairs={{0,16},{16,32},{32,48},{48,64},{64,80},{80,96},{96,112},{112,128},... | collective-permute-start | bytes 196616 | tf_op jit(solution)/shard_map/ppermute | solution.py:39
  39.8 57.8 %copy-start.8 = (f32[16,2048]{1,0:T(8,128)S(1)}, f32[16,2048]{1,0:T(8,128)}, u32[]{:S(2)}) copy-start(f32[16,2048]{1,0:T(8,128)} %get-tuple-element.218) | copy-start | bytes 393220
  42.1 55.6 %collective-permute-start.3 = (f32[18,1,2048]{2,0,1:T(8,128)}, f32[18,1,2048]{2,0,1:T(8,128)S(1)}, u32[]{:S(2)}, u32[]{:S(2)}) collective-permute-start(f32[18,1,2048]{2,0,1:T(8,128)} %get-tuple-element.253), channel_id=1, source_target_pairs={{0,1},{1,2},{2,3},{3,4},{4,5},{5,6},{6,7},{7,8},{8,9},{9,10},{10,1... | collective-permute-start | bytes 442376 | tf_op jit(solution)/shard_map/ppermute | solution.py:39
  45.1 52.6 %collective-permute-start.2 = (f32[18,1,2048]{2,0,1:T(8,128)}, f32[18,1,2048]{2,0,1:T(8,128)S(1)}, u32[]{:S(2)}, u32[]{:S(2)}) collective-permute-start(f32[18,1,2048]{2,0,1:T(8,128)} %get-tuple-element.252), channel_id=1, source_target_pairs={{1,0},{2,1},{3,2},{4,3},{5,4},{6,5},{7,6},{8,7},{9,8},{10,9},{11,1... | collective-permute-start | bytes 442376 | tf_op jit(solution)/shard_map/ppermute | solution.py:41
  118.3 6.9 %collective-permute-start.4 = (f32[1,8,2048]{2,0,1:T(1,128)S(1)}, f32[1,8,2048]{2,0,1:T(1,128)S(1)}, u32[]{:S(2)}, u32[]{:S(2)}) collective-permute-start(f32[1,8,2048]{2,0,1:T(1,128)S(1)} %get-tuple-element.319), channel_id=1, source_target_pairs={{16,0},{32,16},{48,32},{64,48},{80,64},{96,80},{112,96},{128,112},... | collective-permute-start | bytes 196616 | tf_op jit(solution)/shard_map/ppermute | solution.py:41
  121.7 4.4 collective-permute-start.5
  126.1 5.9 collective-permute-start.7
  128.0 8.2 %collective-permute-start.6 = (f32[18,1,2048]{2,0,1:T(8,128)S(1)}, f32[18,1,2048]{2,0,1:T(8,128)S(1)}, u32[]{:S(2)}, u32[]{:S(2)}) collective-permute-start(f32[18,1,2048]{2,0,1:T(8,128)S(1)} %get-tuple-element.250), channel_id=1, source_target_pairs={{1,0},{2,1},{3,2},{4,3},{5,4},{6,5},{7,6},{8,7},{9,8},{10,9},{11,1... | collective-permute-start | bytes 442376 | tf_op jit(solution)/shard_map/ppermute | solution.py:41
  137.3 6.4 collective-permute-start.8
  139.6 5.0 collective-permute-start.9
  144.6 4.8 collective-permute-start.11
  146.6 7.0 %collective-permute-start.10 = (f32[18,1,2048]{2,0,1:T(8,128)S(1)}, f32[18,1,2048]{2,0,1:T(8,128)S(1)}, u32[]{:S(2)}, u32[]{:S(2)}) collective-permute-start(f32[18,1,2048]{2,0,1:T(8,128)S(1)} %get-tuple-element.248), channel_id=1, source_target_pairs={{1,0},{2,1},{3,2},{4,3},{5,4},{6,5},{7,6},{8,7},{9,8},{10,9},{11,1... | collective-permute-start | bytes 442376 | tf_op jit(solution)/shard_map/ppermute | solution.py:41
  154.6 8.0 %collective-permute-start.12 = (f32[1,8,2048]{2,0,1:T(1,128)S(1)}, f32[1,8,2048]{2,0,1:T(1,128)S(1)}, u32[]{:S(2)}, u32[]{:S(2)}) collective-permute-start(f32[1,8,2048]{2,0,1:T(1,128)S(1)} %get-tuple-element.307), channel_id=1, source_target_pairs={{16,0},{32,16},{48,32},{64,48},{80,64},{96,80},{112,96},{128,112},... | collective-permute-start | bytes 196616 | tf_op jit(solution)/shard_map/ppermute | solution.py:41
  156.5 16.2 %copy-start.3 = (f32[16,8,2048]{2,1,0:T(8,128)S(1)}, f32[16,8,2048]{2,1,0:T(8,128)}, u32[]{:S(2)}) copy-start(f32[16,8,2048]{2,1,0:T(8,128)} %param.16) | copy-start | bytes 3145732
  156.5 16.2 %copy-start.5 = (f32[16,8,2048]{2,0,1:T(8,128)S(1)}, f32[16,8,2048]{2,0,1:T(8,128)}, u32[]{:S(2)}) copy-start(f32[16,8,2048]{2,0,1:T(8,128)} %get-tuple-element.221) | copy-start | bytes 3145732
  156.6 6.8 %collective-permute-start.13 = (f32[1,8,2048]{2,0,1:T(1,128)S(1)}, f32[1,8,2048]{2,0,1:T(1,128)S(1)}, u32[]{:S(2)}, u32[]{:S(2)}) collective-permute-start(f32[1,8,2048]{2,0,1:T(1,128)S(1)} %get-tuple-element.306), channel_id=1, source_target_pairs={{0,16},{16,32},{32,48},{48,64},{64,80},{80,96},{96,112},{112,128},... | collective-permute-start | bytes 196616 | tf_op jit(solution)/shard_map/ppermute | solution.py:39
  163.4 5.5 collective-permute-start.15
  166.3 6.4 collective-permute-start.14
  176.8 69.5 %copy-start = (f32[16,8,2048]{2,0,1:T(8,128)}, f32[16,8,2048]{2,0,1:T(8,128)S(1)}, u32[]{:S(2)}) copy-start(f32[16,8,2048]{2,0,1:T(8,128)S(1)} %get-tuple-element.212) | copy-start | bytes 3145732
  176.8 188.5 %all-gather.11.cloned.1.call-start = ((), (), s32[]{:S(2)}) async-start(), calls=%async_computation.4 | async-start | bytes 2228224 | tf_op jit(solution)/shard_map/all_gather | solution.py:21
  176.9 11.5 %collective-permute-start.16 = (f32[1,8,2048]{2,0,1:T(1,128)S(1)}, f32[1,8,2048]{2,0,1:T(1,128)S(1)}, u32[]{:S(2)}, u32[]{:S(2)}) collective-permute-start(f32[1,8,2048]{2,0,1:T(1,128)S(1)} %get-tuple-element.301), channel_id=1, source_target_pairs={{16,0},{32,16},{48,32},{64,48},{80,64},{96,80},{112,96},{128,112},... | collective-permute-start | bytes 196616 | tf_op jit(solution)/shard_map/ppermute | solution.py:41
  178.9 9.5 %collective-permute-start.17 = (f32[1,8,2048]{2,0,1:T(1,128)S(1)}, f32[1,8,2048]{2,0,1:T(1,128)S(1)}, u32[]{:S(2)}, u32[]{:S(2)}) collective-permute-start(f32[1,8,2048]{2,0,1:T(1,128)S(1)} %get-tuple-element.300), channel_id=1, source_target_pairs={{0,16},{16,32},{32,48},{48,64},{64,80},{80,96},{96,112},{112,128},... | collective-permute-start | bytes 196616 | tf_op jit(solution)/shard_map/ppermute | solution.py:39
  187.7 58.5 %copy-start.10 = (f32[16,2048]{1,0:T(8,128)S(1)}, f32[16,2048]{1,0:T(8,128)}, u32[]{:S(2)}) copy-start(f32[16,2048]{1,0:T(8,128)} %get-tuple-element.210) | copy-start | bytes 393220
  189.2 57.0 %collective-permute-start.19 = (f32[18,1,2048]{2,0,1:T(8,128)}, f32[18,1,2048]{2,0,1:T(8,128)}, u32[]{:S(2)}, u32[]{:S(2)}) collective-permute-start(f32[18,1,2048]{2,0,1:T(8,128)} %get-tuple-element.245), channel_id=1, source_target_pairs={{0,1},{1,2},{2,3},{3,4},{4,5},{5,6},{6,7},{7,8},{8,9},{9,10},{10,1... | collective-permute-start | bytes 442376 | tf_op jit(solution)/shard_map/ppermute | solution.py:39
  193.9 52.3 %collective-permute-start.18 = (f32[18,1,2048]{2,0,1:T(8,128)}, f32[18,1,2048]{2,0,1:T(8,128)}, u32[]{:S(2)}, u32[]{:S(2)}) collective-permute-start(f32[18,1,2048]{2,0,1:T(8,128)} %get-tuple-element.244), channel_id=1, source_target_pairs={{1,0},{2,1},{3,2},{4,3},{5,4},{6,5},{7,6},{8,7},{9,8},{10,9},{11,1... | collective-permute-start | bytes 442376 | tf_op jit(solution)/shard_map/ppermute | solution.py:41
  252.4 6.9 %collective-permute-start.20 = (f32[1,8,2048]{2,0,1:T(1,128)S(1)}, f32[1,8,2048]{2,0,1:T(1,128)S(1)}, u32[]{:S(2)}, u32[]{:S(2)}) collective-permute-start(f32[1,8,2048]{2,0,1:T(1,128)S(1)} %get-tuple-element.295), channel_id=1, source_target_pairs={{16,0},{32,16},{48,32},{64,48},{80,64},{96,80},{112,96},{128,112},... | collective-permute-start | bytes 196616 | tf_op jit(solution)/shard_map/ppermute | solution.py:41
  255.8 4.4 collective-permute-start.21
  260.2 5.9 collective-permute-start.23
  262.1 8.2 %collective-permute-start.22 = (f32[18,1,2048]{2,0,1:T(8,128)S(1)}, f32[18,1,2048]{2,0,1:T(8,128)S(1)}, u32[]{:S(2)}, u32[]{:S(2)}) collective-permute-start(f32[18,1,2048]{2,0,1:T(8,128)S(1)} %get-tuple-element.242), channel_id=1, source_target_pairs={{1,0},{2,1},{3,2},{4,3},{5,4},{6,5},{7,6},{8,7},{9,8},{10,9},{11,1... | collective-permute-start | bytes 442376 | tf_op jit(solution)/shard_map/ppermute | solution.py:41
  271.3 6.4 collective-permute-start.24
  273.7 5.0 collective-permute-start.25
  278.7 4.8 collective-permute-start.27
  280.7 7.0 %collective-permute-start.26 = (f32[18,1,2048]{2,0,1:T(8,128)S(1)}, f32[18,1,2048]{2,0,1:T(8,128)S(1)}, u32[]{:S(2)}, u32[]{:S(2)}) collective-permute-start(f32[18,1,2048]{2,0,1:T(8,128)S(1)} %get-tuple-element.240), channel_id=1, source_target_pairs={{1,0},{2,1},{3,2},{4,3},{5,4},{6,5},{7,6},{8,7},{9,8},{10,9},{11,1... | collective-permute-start | bytes 442376 | tf_op jit(solution)/shard_map/ppermute | solution.py:41
  288.7 7.8 %collective-permute-start.28 = (f32[1,8,2048]{2,0,1:T(1,128)S(1)}, f32[1,8,2048]{2,0,1:T(1,128)S(1)}, u32[]{:S(2)}, u32[]{:S(2)}) collective-permute-start(f32[1,8,2048]{2,0,1:T(1,128)S(1)} %get-tuple-element.283), channel_id=1, source_target_pairs={{16,0},{32,16},{48,32},{64,48},{80,64},{96,80},{112,96},{128,112},... | collective-permute-start | bytes 196616 | tf_op jit(solution)/shard_map/ppermute | solution.py:41
  290.6 16.2 %copy-start.1 = (f32[16,8,2048]{2,0,1:T(8,128)S(1)}, f32[16,8,2048]{2,0,1:T(8,128)}, u32[]{:S(2)}) copy-start(f32[16,8,2048]{2,0,1:T(8,128)} %copy-done) | copy-start | bytes 3145732
  290.6 16.2 %copy-start.6 = (f32[16,8,2048]{2,0,1:T(8,128)S(1)}, f32[16,8,2048]{2,0,1:T(8,128)}, u32[]{:S(2)}) copy-start(f32[16,8,2048]{2,0,1:T(8,128)} %get-tuple-element.221) | copy-start | bytes 3145732
  290.6 6.8 %collective-permute-start.29 = (f32[1,8,2048]{2,0,1:T(1,128)S(1)}, f32[1,8,2048]{2,0,1:T(1,128)S(1)}, u32[]{:S(2)}, u32[]{:S(2)}) collective-permute-start(f32[1,8,2048]{2,0,1:T(1,128)S(1)} %get-tuple-element.282), channel_id=1, source_target_pairs={{0,16},{16,32},{32,48},{48,64},{64,80},{80,96},{96,112},{112,128},... | collective-permute-start | bytes 196616 | tf_op jit(solution)/shard_map/ppermute | solution.py:39
  297.5 5.5 collective-permute-start.31
  300.4 6.4 collective-permute-start.30
  310.3 213.0 %reduce-scatter.2.cloned.1.call-start = ((), (), s32[]{:S(2)}) async-start(), calls=%async_computation.1 | async-start | bytes 139264 | tf_op jit(solution)/shard_map/reduce_scatter | solution.py:172
  310.5 11.4 %collective-permute-start.32 = (f32[1,8,2048]{2,0,1:T(1,128)S(1)}, f32[1,8,2048]{2,0,1:T(1,128)S(1)}, u32[]{:S(2)}, u32[]{:S(2)}) collective-permute-start(f32[1,8,2048]{2,0,1:T(1,128)S(1)} %get-tuple-element.277), channel_id=1, source_target_pairs={{16,0},{32,16},{48,32},{64,48},{80,64},{96,80},{112,96},{128,112},... | collective-permute-start | bytes 196616 | tf_op jit(solution)/shard_map/ppermute | solution.py:41
  312.4 9.5 %collective-permute-start.33 = (f32[1,8,2048]{2,0,1:T(1,128)S(1)}, f32[1,8,2048]{2,0,1:T(1,128)S(1)}, u32[]{:S(2)}, u32[]{:S(2)}) collective-permute-start(f32[1,8,2048]{2,0,1:T(1,128)S(1)} %get-tuple-element.276), channel_id=1, source_target_pairs={{0,16},{16,32},{32,48},{48,64},{64,80},{80,96},{96,112},{112,128},... | collective-permute-start | bytes 196616 | tf_op jit(solution)/shard_map/ppermute | solution.py:39
  321.2 58.5 %copy-start.9 = (f32[16,2048]{1,0:T(8,128)S(1)}, f32[16,2048]{1,0:T(8,128)}, u32[]{:S(2)}) copy-start(f32[16,2048]{1,0:T(8,128)} %get-tuple-element.204) | copy-start | bytes 393220
  322.7 57.0 %collective-permute-start.35 = (f32[18,1,2048]{2,0,1:T(8,128)}, f32[18,1,2048]{2,0,1:T(8,128)}, u32[]{:S(2)}, u32[]{:S(2)}) collective-permute-start(f32[18,1,2048]{2,0,1:T(8,128)} %get-tuple-element.237), channel_id=1, source_target_pairs={{0,1},{1,2},{2,3},{3,4},{4,5},{5,6},{6,7},{7,8},{8,9},{9,10},{10,1... | collective-permute-start | bytes 442376 | tf_op jit(solution)/shard_map/ppermute | solution.py:39
  327.7 52.1 %collective-permute-start.34 = (f32[18,1,2048]{2,0,1:T(8,128)}, f32[18,1,2048]{2,0,1:T(8,128)}, u32[]{:S(2)}, u32[]{:S(2)}) collective-permute-start(f32[18,1,2048]{2,0,1:T(8,128)} %get-tuple-element.236), channel_id=1, source_target_pairs={{1,0},{2,1},{3,2},{4,3},{5,4},{6,5},{7,6},{8,7},{9,8},{10,9},{11,1... | collective-permute-start | bytes 442376 | tf_op jit(solution)/shard_map/ppermute | solution.py:41
  385.9 6.9 %collective-permute-start.36 = (f32[1,8,2048]{2,0,1:T(1,128)S(1)}, f32[1,8,2048]{2,0,1:T(1,128)S(1)}, u32[]{:S(2)}, u32[]{:S(2)}) collective-permute-start(f32[1,8,2048]{2,0,1:T(1,128)S(1)} %get-tuple-element.271), channel_id=1, source_target_pairs={{16,0},{32,16},{48,32},{64,48},{80,64},{96,80},{112,96},{128,112},... | collective-permute-start | bytes 196616 | tf_op jit(solution)/shard_map/ppermute | solution.py:41
  389.3 4.4 collective-permute-start.37
  393.7 5.9 collective-permute-start.39
  395.6 8.2 %collective-permute-start.38 = (f32[18,1,2048]{2,0,1:T(8,128)S(1)}, f32[18,1,2048]{2,0,1:T(8,128)S(1)}, u32[]{:S(2)}, u32[]{:S(2)}) collective-permute-start(f32[18,1,2048]{2,0,1:T(8,128)S(1)} %get-tuple-element.234), channel_id=1, source_target_pairs={{1,0},{2,1},{3,2},{4,3},{5,4},{6,5},{7,6},{8,7},{9,8},{10,9},{11,1... | collective-permute-start | bytes 442376 | tf_op jit(solution)/shard_map/ppermute | solution.py:41
  404.8 6.4 collective-permute-start.40
  407.2 5.0 collective-permute-start.41
  412.2 4.8 collective-permute-start.43
  414.2 7.0 %collective-permute-start.42 = (f32[18,1,2048]{2,0,1:T(8,128)S(1)}, f32[18,1,2048]{2,0,1:T(8,128)S(1)}, u32[]{:S(2)}, u32[]{:S(2)}) collective-permute-start(f32[18,1,2048]{2,0,1:T(8,128)S(1)} %get-tuple-element.232), channel_id=1, source_target_pairs={{1,0},{2,1},{3,2},{4,3},{5,4},{6,5},{7,6},{8,7},{9,8},{10,9},{11,1... | collective-permute-start | bytes 442376 | tf_op jit(solution)/shard_map/ppermute | solution.py:41
  422.2 7.8 %collective-permute-start.44 = (f32[1,8,2048]{2,0,1:T(1,128)S(1)}, f32[1,8,2048]{2,0,1:T(1,128)S(1)}, u32[]{:S(2)}, u32[]{:S(2)}) collective-permute-start(f32[1,8,2048]{2,0,1:T(1,128)S(1)} %get-tuple-element.259), channel_id=1, source_target_pairs={{16,0},{32,16},{48,32},{64,48},{80,64},{96,80},{112,96},{128,112},... | collective-permute-start | bytes 196616 | tf_op jit(solution)/shard_map/ppermute | solution.py:41
  424.1 16.2 %copy-start.7 = (f32[16,8,2048]{2,0,1:T(8,128)S(1)}, f32[16,8,2048]{2,0,1:T(8,128)}, u32[]{:S(2)}) copy-start(f32[16,8,2048]{2,0,1:T(8,128)} %get-tuple-element.221) | copy-start | bytes 3145732
  424.1 6.8 %collective-permute-start.45 = (f32[1,8,2048]{2,0,1:T(1,128)S(1)}, f32[1,8,2048]{2,0,1:T(1,128)S(1)}, u32[]{:S(2)}, u32[]{:S(2)}) collective-permute-start(f32[1,8,2048]{2,0,1:T(1,128)S(1)} %get-tuple-element.258), channel_id=1, source_target_pairs={{0,16},{16,32},{32,48},{48,64},{64,80},{80,96},{96,112},{112,128},... | collective-permute-start | bytes 196616 | tf_op jit(solution)/shard_map/ppermute | solution.py:39
  431.0 5.5 collective-permute-start.47
  433.9 6.4 collective-permute-start.46
  440.3 92.4 %copy-start.17 = (u32[256]{0:T(256)S(1)}, u32[256]{0:T(256)}, u32[]{:S(2)}) copy-start(u32[256]{0:T(256)} %constant.128) | copy-start | bytes 3076
  443.8 198.9 %all-reduce.3.cloned.1.call-start = ((), (), s32[]{:S(2)}) async-start(), calls=%async_computation.5 | async-start | bytes 524288
  (7 other events, 23.4 us)
Sparse Core Ops, SparseCore 0:
  27.5 55.6 all-gather.6
  176.9 54.8 all-gather.8
  310.4 54.8 all-gather.10
  443.9 79.2 reduce-scatter.1
  532.8 109.8 all-reduce.2
where the time goes:
time: 653 us; the launch traced here: 651 us
  waiting for transfers between devices  356 us (55%)
  starting transfers between devices  133 us (20%)
  other arithmetic  112 us (17%)
  local copies, waits for them, and re-layouts  33.3 us (5%)
  between operations  15.4 us (2%)
    all_gather x3, waiting for transfers between devices, carried_in(): gathered = lax.all_gather(part, axis)  110 us
    unnamed x6, waiting for transfers between devices  106 us
    ppermute x24, starting transfers between devices, extended(): lax.ppermute(tail, axis, [(i, (i + 1) % count) for i in range(ends)])  85.6 us
    reduce_scatter x1, waiting for transfers between devices, shards(): lax.psum_scatter(jnp.sum(charring_speed, axis=1), 'depth', scatter_dimens...  79.4 us
    ppermute x24, starting transfers between devices, extended(): lax.ppermute(head, axis, [((i + 1) % count, i) for i in range(ends)])  47.4 us
    add x45, other arithmetic, combine_sum(): return earlier + later  42.2 us
    ppermute x24, waiting for transfers between devices, extended(): lax.ppermute(head, axis, [((i + 1) % count, i) for i in range(ends)])  36.3 us
    another operation x3, other arithmetic, shards(): jnp.cumsum(charring_speed, axis=1)  31.8 us
  transfers between devices with their start and end apart: 53, of which 32 were waited for; matrix products, arithmetic and copies ran while one was open for 10% of the time, Pallas kernels for 0%

commit v1 on v0

v1 whole, which is shorter than its diff:
```python
import functools

import jax
import jax.numpy as jnp
from jax import lax
from jax.experimental import pallas as pl
from jax.experimental.pallas import tpu as pltpu
from jax.sharding import PartitionSpec as P

SWEEPS = 4
H = 4
W = 16
PAD = 8
LANES = 128
LO, HI = PAD, PAD + 2 * W + LANES
FULL = HI + PAD
CORE = slice(PAD + W, PAD + W + LANES)
VMEM_LIMIT = 56 * 1024 * 1024

VM = pl.BlockSpec(memory_space=pltpu.VMEM)
SM = pl.BlockSpec(memory_space=pltpu.SMEM)


def params():
    return pltpu.CompilerParams(vmem_limit_bytes=VMEM_LIMIT)


def f32(*shape):
    return jax.ShapeDtypeStruct(shape, jnp.float32)


def lane_iota(rows):
    return lax.broadcasted_iota(jnp.int32, (rows, LANES), 1)


def split3(x):
    a = x.astype(jnp.bfloat16)
    rest = x - a.astype(jnp.float32)
    b = rest.astype(jnp.bfloat16)
    c = (rest - b.astype(jnp.float32)).astype(jnp.bfloat16)
    return a, b, c


def edges_kernel(*refs):
    ins, out = refs[:-1], refs[-1]
    slices = out.shape[0]
    lane = lane_iota(8)

    def row(a, _):
        turned = [
            [
                pltpu.roll(
                    x[a, :, LANES * s : LANES * (s + 1)].astype(jnp.float32), (2 * W * i + W) % LANES, 1
                )
                for s in range(slices)
            ]
            for i, x in enumerate(ins)
        ]
        for s in range(slices):
            result = jnp.zeros((8, LANES), jnp.float32)
            for i in range(len(ins)):
                before, after = turned[i][s - 1], turned[i][(s + 1) % slices]
                result = jnp.where(lane >= 2 * W * i, before, result)
                result = jnp.where(lane >= 2 * W * i + W, after, result)
            out[s, a] = result
        return 0

    lax.fori_loop(0, out.shape[1], row, 0)


def suffix_matrix(m_ref):
    rows, cols = m_ref.shape
    source = lax.broadcasted_iota(jnp.int32, (rows, cols), 0) & (LANES - 1)
    target = lax.broadcasted_iota(jnp.int32, (rows, cols), 1)
    m_ref[...] = jnp.where(source > target, 4.0 / LANES, 0.0).astype(jnp.bfloat16)


def newton(first_row, total_rows, t, t0, conduct, capacity, act, pre, dep, m_ref, cs, cd, ua, ub, uc, finish):
    span = HI - LO
    lane = lane_iota(span)

    def setup(r, _):
        tc = t[r, LO:HI]
        a = act[r, LO:HI]
        q = 1.0 / (1.0 + jnp.abs(tc))
        aq = a * q
        p = pre[r, LO:HI] * jnp.exp(aq * tc)
        gas = jnp.dot(
            jnp.concatenate(split3(p), axis=1), m_ref[...], preferred_element_type=jnp.float32
        )
        c = conduct[r, LO:HI]
        cap = capacity[r, LO:HI]
        deeper = jnp.where(lane == LANES - 1, 0.0, pltpu.roll(tc, LANES - 1, 1))
        shallower = jnp.where(lane == 0, 0.0, pltpu.roll(tc, 1, 1))
        pairs = t[r - 1, LO:HI] + t[r + 1, LO:HI] + t[r, LO - 1 : HI - 1] + t[r, LO + 1 : HI + 1]
        spread = pairs + 2.0 * (deeper + shallower) - 8.0 * tc
        residual = (
            cap * (tc - t0[r, LO:HI])
            - c * spread
            + 0.5 * p
            + gas * (tc - deeper)
            - dep[r, LO:HI]
        )
        diagonal = cap + 8.0 * c + 0.5 * p * (aq * q) + gas
        row = first_row + r
        inside = jnp.where((row >= 0) & (row < total_rows), 1.0, 0.0)
        inverse = inside / diagonal
        ua[r, LO:HI] = -residual * inverse
        cs[r, LO:HI] = c * inverse
        cd[r, LO:HI] = jnp.where(lane == LANES - 1, 0.0, (2.0 * c + gas) * inverse)
        return 0

    rows = t.shape[0]
    lax.fori_loop(1, rows - 1, setup, 0)

    def swept(src, r):
        u = src[r, LO:HI]
        pairs = src[r - 1, LO:HI] + src[r + 1, LO:HI] + src[r, LO - 1 : HI - 1] + src[r, LO + 1 : HI + 1]
        shallower = jnp.where(lane == 0, 0.0, pltpu.roll(u, 1, 1))
        deeper = pltpu.roll(u, LANES - 1, 1)
        return ua[r, LO:HI] + cs[r, LO:HI] * (pairs + 2.0 * shallower) + cd[r, LO:HI] * deeper

    def to(dst, src):
        def one(r, _):
            dst[r, LO:HI] = swept(src, r)
            return 0

        return one

    lax.fori_loop(2, rows - 2, to(ub, ua), 0)
    lax.fori_loop(3, rows - 3, to(uc, ub), 0)

    def last(r, _):
        finish(r - H, t[r, LO:HI] + swept(uc, r))
        return 0

    lax.fori_loop(H, rows - H, last, 0)


def from_cells(ref, r):
    x = ref[:, r]
    return x.reshape(x.shape[0] * x.shape[1], LANES).T


def hand_on(out, up, down):
    own = out.shape[0]

    def finish(r, value):
        out[r] = value

        @pl.when(r >= own - H)
        def _():
            up[r - (own - H)] = value

        @pl.when(r < H)
        def _():
            down[r] = value

    return finish


def work_arrays(rows):
    return [pltpu.VMEM((rows, FULL, LANES), jnp.float32) for _ in range(5)] + [
        pltpu.VMEM((3 * LANES, LANES), jnp.bfloat16)
    ]


def first_kernel(total_rows, scalars, tables, *refs):
    inputs, refs = refs[:15], refs[15:]
    t0, conduct, capacity, act, pre, dep, out, up, down, cs, cd, ua, ub, uc, m_ref = refs
    suffix_matrix(m_ref)
    own = out.shape[0]
    span = HI - LO

    def unpack(which, offset):
        t_in, label_in, share_in, dep_in, edge_in = (inputs[3 * i + which] for i in range(5))

        def one(i, _):
            r = i + offset
            edges = from_cells(edge_in, i)

            def whole(ref, index):
                at = 2 * W * index
                return jnp.concatenate(
                    [edges[at : at + W], from_cells(ref, i), edges[at + W : at + 2 * W]], axis=0
                )

            t0[r, LO:HI] = whole(t_in, 0)
            dep[r, LO:HI] = whole(dep_in, 3)
            label = whole(label_in, 1)
            fields = [jnp.full((span, LANES), tables[f, 0], jnp.float32) for f in range(4)]
            for zone in range(1, tables.shape[1]):
                here = label == float(zone)
                fields = [jnp.where(here, tables[f, zone], x) for f, x in enumerate(fields)]
            conduct[r, LO:HI] = fields[0]
            capacity[r, LO:HI] = fields[1]
            pre[r, LO:HI] = fields[2] * whole(share_in, 2)
            act[r, LO:HI] = fields[3]
            return 0

        return one

    lax.fori_loop(0, own, unpack(0, H), 0)
    lax.fori_loop(0, H, unpack(1, 0), 0)
    lax.fori_loop(0, H, unpack(2, own + H), 0)
    newton(
        scalars[0] * own - H, total_rows, t0, t0, conduct, capacity, act, pre, dep, m_ref,
        cs, cd, ua, ub, uc, hand_on(out, up, down),
    )


def spread_rows(t, own_t, above, below):
    own = own_t.shape[0]
    t[0:H, LO:HI] = above[...]
    t[H : H + own, LO:HI] = own_t[...]
    t[H + own :, LO:HI] = below[...]


def second_kernel(total_rows, scalars, own_t, above, below, t0, conduct, capacity, act, pre, dep, *refs):
    out, up, down, cs, cd, ua, ub, uc, m_ref, t = refs
    suffix_matrix(m_ref)
    spread_rows(t, own_t, above, below)
    newton(
        scalars[0] * out.shape[0] - H, total_rows, t, t0, conduct, capacity, act, pre, dep, m_ref,
        cs, cd, ua, ub, uc, hand_on(out, up, down),
    )


def third_kernel(total_rows, scalars, own_t, above, below, t0, conduct, capacity, act, pre, dep, *refs):
    out, blowing, cs, cd, ua, ub, uc, m_ref, t = refs
    suffix_matrix(m_ref)
    spread_rows(t, own_t, above, below)

    def finish(r, value):
        value = value[W : W + LANES]
        out[:, r] = value.T.reshape(out.shape[0], 8, LANES)
        p = pre[r + H, CORE] * jnp.exp(act[r + H, CORE] * value / (1.0 + jnp.abs(value)))
        blowing[pl.ds(r, 1), :] = jnp.sum(p.T, axis=0, keepdims=True) * (1.0 / LANES)

    newton(
        scalars[0] * out.shape[1] - H, total_rows, t, t0, conduct, capacity, act, pre, dep, m_ref,
        cs, cd, ua, ub, uc, finish,
    )


def deliver_kernel(scalars, gathered, out, left, right):
    groups, rows3, _ = gathered.shape
    rows = rows3 // 3
    me = scalars[0]
    owners = gathered[:, 2 * rows :, :].astype(jnp.int32)
    shape = owners.shape
    number = lax.broadcasted_iota(jnp.int32, shape, 0) * rows + lax.broadcasted_iota(jnp.int32, shape, 1)
    first = jnp.min(jnp.where(owners == me, number, groups * rows))
    most = out.shape[0]
    first = jnp.minimum(first, groups * rows - most)
    high_of = lax.broadcasted_iota(jnp.int32, (most, LANES), 0)
    low_of = lax.broadcasted_iota(jnp.int32, (LANES, LANES), 0)
    for i in range(most):
        at = first + i
        group, r = at // rows, at % rows
        value = gathered[group, pl.ds(r, 1), :]
        slot = gathered[group, pl.ds(rows + r, 1), :].astype(jnp.int32)
        owner = gathered[group, pl.ds(2 * rows + r, 1), :].astype(jnp.int32)
        high = jnp.where(owner == me, slot >> 7, -1)
        low = slot & (LANES - 1)
        here = slice(LANES * i, LANES * (i + 1))
        hit = high_of == high
        for k, part in enumerate(split3(value)):
            left[most * k : most * (k + 1), here] = jnp.where(hit, part.astype(jnp.float32), 0.0).astype(
                jnp.bfloat16
            )
        right[:, here] = jnp.where(low_of == low, 1.0, 0.0).astype(jnp.bfloat16)
    parts = lax.dot_general(
        left[...], right[...], (((1,), (1,)), ((), ())), preferred_element_type=jnp.float32
    )
    out[...] = parts[:most] + parts[most : 2 * most] + parts[2 * most :]


def shards(
    kelvin_before_step,
    unburnt_resin_share,
    deposited_energy_amount,
    material_label,
    zonal_diffusivity,
    zonal_storage_coefficient,
    frequency_coefficient,
    arrhenius_barrier,
    stream_keeper,
    keeper_position,
):
    own, layers, columns = kelvin_before_step.shape
    n_axial, n_depth = lax.axis_size("axial"), lax.axis_size("depth")
    place = lax.axis_index("axial").astype(jnp.int32).reshape(1)
    total_rows = own * n_axial
    label = material_label.astype(jnp.float32)
    tables = jnp.stack(
        [zonal_diffusivity, zonal_storage_coefficient, frequency_coefficient, arrhenius_barrier]
    )

    edges = pl.pallas_call(
        edges_kernel,
        out_shape=f32(n_depth, own, layers, LANES),
        in_specs=[VM] * 4,
        out_specs=VM,
        compiler_params=params(),
        name="edges",
    )(kelvin_before_step, material_label, unburnt_resin_share, deposited_energy_amount)

    def packed(x):
        return jnp.transpose(x.reshape(own, layers, n_depth, LANES), (2, 0, 1, 3))

    def up(x):
        return lax.ppermute(x, "axial", [(i, i + 1) for i in range(n_axial - 1)])

    def down(x):
        return lax.ppermute(x, "axial", [(i + 1, i) for i in range(n_axial - 1)])

    operands = []
    for x in (packed(kelvin_before_step), packed(label), packed(unburnt_resin_share),
              packed(deposited_energy_amount), edges):
        y = lax.all_to_all(x, "depth", 0, 0)
        operands += [y, up(y[:, own - H :]), down(y[:, :H])]

    extended = f32(own + 2 * H, FULL, LANES)
    block = f32(own, HI - LO, LANES)
    rim = f32(H, HI - LO, LANES)
    *state, t, above, below = pl.pallas_call(
        functools.partial(first_kernel, total_rows),
        out_shape=[extended] * 6 + [block, rim, rim],
        in_specs=[SM, SM] + [VM] * 15,
        out_specs=[VM] * 9,
        scratch_shapes=work_arrays(own + 2 * H),
        compiler_params=params(),
        name="newton1",
    )(place, tables, *operands)
    t, above, below = pl.pallas_call(
        functools.partial(second_kernel, total_rows),
        out_shape=[block, rim, rim],
        in_specs=[SM] + [VM] * 9,
        out_specs=[VM] * 3,
        scratch_shapes=work_arrays(own + 2 * H) + [pltpu.VMEM((own + 2 * H, FULL, LANES), jnp.float32)],
        compiler_params=params(),
        name="newton2",
    )(place, t, up(above), down(below), *state)
    kelvin, blowing = pl.pallas_call(
        functools.partial(third_kernel, total_rows),
        out_shape=[f32(n_depth, own, layers, LANES), f32(own, LANES)],
        in_specs=[SM] + [VM] * 9,
        out_specs=[VM] * 2,
        scratch_shapes=work_arrays(own + 2 * H) + [pltpu.VMEM((own + 2 * H, FULL, LANES), jnp.float32)],
        compiler_params=params(),
        name="newton3",
    )(place, t, up(above), down(below), *state)

    kelvin = lax.all_to_all(kelvin, "depth", 0, 0)
    kelvin = jnp.transpose(kelvin, (1, 2, 0, 3)).reshape(own, layers, columns)

    faces = jnp.concatenate(
        [blowing, keeper_position.astype(jnp.float32), stream_keeper.astype(jnp.float32)], axis=0
    )
    gathered = lax.all_gather(faces, "axial")
    slots = 2 * own * LANES
    delivered = pl.pallas_call(
        deliver_kernel,
        out_shape=f32(slots // LANES, LANES),
        in_specs=[SM, VM],
        out_specs=VM,
        scratch_shapes=[
            pltpu.VMEM((3 * slots // LANES, slots), jnp.bfloat16),
            pltpu.VMEM((LANES, slots), jnp.bfloat16),
        ],
        compiler_params=params(),
        name="deliver",
    )(place, gathered)
    return (kelvin, delivered.reshape(slots))


def solution(mesh):
    cells = P("axial", "depth", None)
    faces = P("axial", "depth")
    return jax.shard_map(
        shards,
        mesh=mesh,
        in_specs=(cells, cells, cells, cells, P(), P(), P(), P(), faces, faces),
        out_specs=(cells, P(("axial", "depth"))),
        check_vma=False,
    )
```

time: 653 us -> 255 us (0.39)
  waiting for transfers between devices: 356 us -> 70.4 us
  other arithmetic: 112 us -> 2.38 us
  Pallas kernels: 0 us -> 69.3 us
  starting transfers between devices: 133 us -> 72.8 us
  blocking collectives: 0 us -> 22.6 us
  local copies, waits for them, and re-layouts: 33.3 us -> 15.1 us
  between operations: 15.4 us -> 1.08 us
    all_gather x3 -> x0, waiting for transfers between devices: 110 us -> none  [carried_in(): gathered = lax.all_gather(part, axis)]
    unnamed x6 -> x0, waiting for transfers between devices: 106 us -> none
    ppermute x48 -> x14, starting transfers between devices: 133 us -> 39.2 us  [the longest x7 24.7 us: up(): return lax.ppermute(x, 'axial', [(i, i + 1) for i in range(n_axial - 1)])]
    reduce_scatter x1 -> x0, waiting for transfers between devices: 79.4 us -> none  [shards(): lax.psum_scatter(jnp.sum(charring_speed, axis=1), 'depth', scatter_dimens...]
    pallas_call x0 -> x5, Pallas kernels: none -> 69.3 us  [the longest x1 24.1 us: shards(): pl.pallas_call(functools.partial(first_kernel, total_rows), out_shape=[ex...]
    all_to_all x0 -> x6, waiting for transfers between devices: none -> 49 us  [the longest x5 49 us: shards(): y = lax.all_to_all(x, 'depth', 0, 0)]
    add x49 -> x0, other arithmetic: 42.2 us -> none  [the longest x45 42.2 us: combine_sum(): return earlier + later]
    ppermute x48 -> x14, waiting for transfers between devices: 60.6 us -> 21.4 us  [the longest x7 16.7 us: down(): return lax.ppermute(x, 'axial', [(i + 1, i) for i in range(n_axial - 1)])]
  transfers between devices with their start and end apart: 53 -> 20, of which waited for: 32 -> 10; matrix products, arithmetic and copies ran while one was open for 10% -> 5% of each run, Pallas kernels for 0% -> 3%
where the time goes in v1:
time: 255 us; the launch traced here: 254 us
  starting transfers between devices  72.8 us (29%)
  waiting for transfers between devices  70.4 us (28%)
  Pallas kernels  69.3 us (27%)
  blocking collectives  22.6 us (9%)
  local copies, waits for them, and re-layouts  15.1 us (6%)
    all_to_all x5, waiting for transfers between devices, shards(): y = lax.all_to_all(x, 'depth', 0, 0)  49 us
    all_to_all x5, starting transfers between devices, shards(): y = lax.all_to_all(x, 'depth', 0, 0)  26.8 us
    ppermute x7, starting transfers between devices, up(): return lax.ppermute(x, 'axial', [(i, i + 1) for i in range(n_axial - 1)])  24.7 us
    pallas_call x1, Pallas kernels, shards(): pl.pallas_call(functools.partial(first_kernel, total_rows), out_shape=[ex...  24.1 us
    all_gather x1, blocking collectives, shards(): gathered = lax.all_gather(faces, 'axial')  22.6 us
    pallas_call x1, Pallas kernels, shards(): pl.pallas_call(functools.partial(third_kernel, total_rows), out_shape=[f3...  19 us
    pallas_call x1, Pallas kernels, shards(): pl.pallas_call(functools.partial(second_kernel, total_rows), out_shape=[b...  18.1 us
    ppermute x7, waiting for transfers between devices, down(): return lax.ppermute(x, 'axial', [(i + 1, i) for i in range(n_axial - 1)])  16.7 us
  transfers between devices with their start and end apart: 20, of which 10 were waited for; matrix products, arithmetic and copies ran while one was open for 5% of the time, Pallas kernels for 3%

profile of v1, /device:TPU:1, one launch (start us, length us, event | category | flops | bytes accessed | tf_op | source)
XLA Modules:
  0.0 253.7 jit_solution(4247265239101553615)
XLA Ops:
  0.6 0.0 copy-start.3
  0.6 2.4 bitcast_bitcast_fusion.3
  3.0 7.6 %all-to-all-start = ((f32[16,16,8,128]{3,2,1,0:T(8,128)}), f32[16,16,8,128]{3,2,1,0:T(8,128)S(1)}, u32[]{:S(2)}, u32[]{:S(2)}) async-start(f32[16,16,8,128]{3,2,1,0:T(8,128)} %bitcast_bitcast_fusion.3), calls=%async_computation | async-start | bytes 2097152 | tf_op jit(solution)/shard_map/all_to_all | solution.py:321
  10.6 0.0 copy-start.4
  10.6 1.1 bitcast_bitcast_fusion.2
  11.7 14.4 %all-to-all-done.refs_0_ = f32[16,16,8,128]{3,2,1,0:T(8,128)S(1)} async-done(((f32[16,16,8,128]{3,2,1,0:T(8,128)}), f32[16,16,8,128]{3,2,1,0:T(8,128)S(1)}, u32[]{:S(2)}, u32[]{:S(2)}) %all-to-all-start) | async-done | bytes 1048608 | tf_op jit(solution)/shard_map/all_to_all | solution.py:321
  26.1 4.0 %all-to-all-start.1 = ((f32[16,16,8,128]{3,2,1,0:T(8,128)}), f32[16,16,8,128]{3,2,1,0:T(8,128)S(1)}, u32[]{:S(2)}, u32[]{:S(2)}) async-start(f32[16,16,8,128]{3,2,1,0:T(8,128)} %bitcast_bitcast_fusion.2), calls=%async_computation.1 | async-start | bytes 2097152 | tf_op jit(solution)/shard_map/all_to_all | solution.py:321
  30.1 1.1 bitcast_bitcast_fusion.1
  31.3 13.2 %all-to-all-done.1.refs_3_ = f32[16,16,8,128]{3,2,1,0:T(8,128)S(1)} async-done(((f32[16,16,8,128]{3,2,1,0:T(8,128)}), f32[16,16,8,128]{3,2,1,0:T(8,128)S(1)}, u32[]{:S(2)}, u32[]{:S(2)}) %all-to-all-start.1) | async-done | bytes 1048608 | tf_op jit(solution)/shard_map/all_to_all | solution.py:321
  44.5 5.2 %all-to-all-start.2 = ((f32[16,16,8,128]{3,2,1,0:T(8,128)}), f32[16,16,8,128]{3,2,1,0:T(8,128)S(1)}, u32[]{:S(2)}, u32[]{:S(2)}) async-start(f32[16,16,8,128]{3,2,1,0:T(8,128)} %bitcast_bitcast_fusion.1), calls=%async_computation.2 | async-start | bytes 2097152 | tf_op jit(solution)/shard_map/all_to_all | solution.py:321
  49.7 2.3 bitcast_bitcast_fusion
  52.0 12.5 %all-to-all-done.2.refs_6_ = f32[16,16,8,128]{3,2,1,0:T(8,128)S(1)} async-done(((f32[16,16,8,128]{3,2,1,0:T(8,128)}), f32[16,16,8,128]{3,2,1,0:T(8,128)S(1)}, u32[]{:S(2)}, u32[]{:S(2)}) %all-to-all-start.2) | async-done | bytes 1048608 | tf_op jit(solution)/shard_map/all_to_all | solution.py:321
  64.4 4.7 %all-to-all-start.3 = ((f32[16,16,8,128]{3,2,1,0:T(8,128)}), f32[16,16,8,128]{3,2,1,0:T(8,128)}, u32[]{:S(2)}, u32[]{:S(2)}) async-start(f32[16,16,8,128]{3,2,1,0:T(8,128)} %bitcast_bitcast_fusion), calls=%async_computation.3 | async-start | bytes 2097152 | tf_op jit(solution)/shard_map/all_to_all | solution.py:321
  69.2 5.4 %edges.1 = f32[16,16,8,128]{3,2,1,0:T(8,128)} custom-call(f32[16,8,2048]{2,1,0:T(8,128)} %refs_0_.1, s32[16,8,2048]{2,1,0:T(8,128)} %refs_1_.1, f32[16,8,2048]{2,1,0:T(8,128)} %refs_2_.1, f32[16,8,2048]{2,1,0:T(8,128)} %refs_3_.1), custom_call_target="tpu_custom_call" | custom-call | tf_op jit(solution)/shard_map/edges/pallas_call | solution.py:300
  74.5 8.9 %all-to-all-done.3.refs_9_ = f32[16,16,8,128]{3,2,1,0:T(8,128)} async-done(((f32[16,16,8,128]{3,2,1,0:T(8,128)}), f32[16,16,8,128]{3,2,1,0:T(8,128)}, u32[]{:S(2)}, u32[]{:S(2)}) %all-to-all-start.3) | async-done | bytes 1048608 | tf_op jit(solution)/shard_map/all_to_all | solution.py:321
  83.4 5.4 %all-to-all-start.4 = ((f32[16,16,8,128]{3,2,1,0:T(8,128)}), f32[16,16,8,128]{3,2,1,0:T(8,128)}, u32[]{:S(2)}, u32[]{:S(2)}) async-start(f32[16,16,8,128]{3,2,1,0:T(8,128)} %edges.1), calls=%async_computation.4 | async-start | bytes 2097152 | tf_op jit(solution)/shard_map/all_to_all | solution.py:321
  88.8 0.8 fusion.4
  89.7 6.4 %collective-permute-start = (f32[16,4,8,128]{3,2,1,0:T(8,128)}, f32[16,4,8,128]{3,2,1,0:T(8,128)S(1)}, u32[]{:S(2)}, u32[]{:S(2)}) collective-permute-start(f32[16,4,8,128]{3,2,1,0:T(8,128)} %get-tuple-element.39), channel_id=1, source_target_pairs={{0,16},{16,32},{32,48},{48,64},{64,80},{80,96},{96,112},{112,128},... | collective-permute-start | bytes 786440 | tf_op jit(solution)/shard_map/ppermute | solution.py:313
  96.1 1.9 collective-permute-start.1
  98.0 0.8 fusion.3
  98.8 3.6 %collective-permute-start.2 = (f32[16,4,8,128]{3,2,1,0:T(8,128)}, f32[16,4,8,128]{3,2,1,0:T(8,128)S(1)}, u32[]{:S(2)}, u32[]{:S(2)}) collective-permute-start(f32[16,4,8,128]{3,2,1,0:T(8,128)} %get-tuple-element.37), channel_id=1, source_target_pairs={{0,16},{16,32},{32,48},{48,64},{64,80},{80,96},{96,112},{112,128},... | collective-permute-start | bytes 786440 | tf_op jit(solution)/shard_map/ppermute | solution.py:313
  102.5 1.9 collective-permute-start.3
  104.4 0.8 fusion.2
  105.2 3.6 %collective-permute-start.4 = (f32[16,4,8,128]{3,2,1,0:T(8,128)}, f32[16,4,8,128]{3,2,1,0:T(8,128)S(1)}, u32[]{:S(2)}, u32[]{:S(2)}) collective-permute-start(f32[16,4,8,128]{3,2,1,0:T(8,128)} %get-tuple-element.35), channel_id=1, source_target_pairs={{0,16},{16,32},{32,48},{48,64},{64,80},{80,96},{96,112},{112,128},... | collective-permute-start | bytes 786440 | tf_op jit(solution)/shard_map/ppermute | solution.py:313
  108.8 1.8 fusion.1
  110.6 0.0 all-to-all-done.4.refs_12_
  110.6 1.8 fusion
  112.4 0.0 collective-permute-done.refs_1_
  112.4 1.9 collective-permute-start.5
  114.3 0.0 collective-permute-done.1.refs_2_
  114.3 3.6 %collective-permute-start.6 = (f32[16,4,8,128]{3,2,1,0:T(8,128)}, f32[16,4,8,128]{3,2,1,0:T(8,128)S(1)}, u32[]{:S(2)}, u32[]{:S(2)}) collective-permute-start(f32[16,4,8,128]{3,2,1,0:T(8,128)} %get-tuple-element.33), channel_id=1, source_target_pairs={{0,16},{16,32},{32,48},{48,64},{64,80},{80,96},{96,112},{112,128},... | collective-permute-start | bytes 786440 | tf_op jit(solution)/shard_map/ppermute | solution.py:313
  118.0 0.0 collective-permute-done.2.refs_4_
  118.0 1.9 collective-permute-start.7
  119.9 0.0 collective-permute-done.3.refs_5_
  120.0 3.6 %collective-permute-start.8 = (f32[16,4,8,128]{3,2,1,0:T(8,128)}, f32[16,4,8,128]{3,2,1,0:T(8,128)S(1)}, u32[]{:S(2)}, u32[]{:S(2)}) collective-permute-start(f32[16,4,8,128]{3,2,1,0:T(8,128)} %get-tuple-element.31), channel_id=1, source_target_pairs={{0,16},{16,32},{32,48},{48,64},{64,80},{80,96},{96,112},{112,128},... | collective-permute-start | bytes 786440 | tf_op jit(solution)/shard_map/ppermute | solution.py:313
  123.6 0.0 collective-permute-done.4.refs_7_
  123.6 1.9 collective-permute-start.9
  125.6 0.6 pad_maximum_fusion.1.tables
  126.2 0.0 collective-permute-done.5.refs_8_
  126.2 0.0 collective-permute-done.6.refs_10_
  126.2 0.0 copy-start.15
  126.2 0.0 collective-permute-done.7.refs_11_
  126.2 1.0 collective-permute-done.8.refs_13_
  127.2 4.1 %collective-permute-done.9.refs_14_ = f32[16,4,8,128]{3,2,1,0:T(8,128)S(1)} collective-permute-done((f32[16,4,8,128]{3,2,1,0:T(8,128)S(1)}, f32[16,4,8,128]{3,2,1,0:T(8,128)S(1)}, u32[]{:S(2)}, u32[]{:S(2)}) %collective-permute-start.9) | collective-permute-done | bytes 262176 | tf_op jit(solution)/shard_map/ppermute | solution.py:316
  131.4 0.6 copy-done.18
  132.0 24.1 %newton1.1 = (f32[24,176,128]{2,1,0:T(8,128)}, f32[24,176,128]{2,1,0:T(8,128)}, f32[24,176,128]{2,1,0:T(8,128)}, f32[24,176,128]{2,1,0:T(8,128)}, f32[24,176,128...) custom-call(s32[1]{0:T(128)} %bitcast.scalars, ...), custom_call_target="tpu_custom_call" | custom-call | tf_op jit(solution)/shard_map/newton1/pallas_call | solution.py:327
  156.1 1.9 collective-permute-start.10
  158.0 2.4 collective-permute-start.11
  160.4 1.9 collective-permute-done.10.above
  162.3 4.6 %collective-permute-done.11.below = f32[4,160,128]{2,1,0:T(8,128)S(1)} collective-permute-done((f32[4,160,128]{2,1,0:T(8,128)}, f32[4,160,128]{2,1,0:T(8,128)S(1)}, u32[]{:S(2)}, u32[]{:S(2)}) %collective-permute-start.11) | collective-permute-done | bytes 327712 | tf_op jit(solution)/shard_map/ppermute | solution.py:316
  166.9 0.7 copy-done.8
  167.6 18.1 %newton2.1 = (f32[16,160,128]{2,1,0:T(8,128)}, f32[4,160,128]{2,1,0:T(8,128)}, f32[4,160,128]{2,1,0:T(8,128)}) custom-call(s32[1]{0:T(128)} %bitcast.scalars, f32[16,160,128]{2,1,0:T(8,128)} %get-tuple-element.16.own_t, f32[4,160,128]{2,1,0:T(8,128)} %copy-done.7, f32[4,160,128]{2,1,0:T(8,128)} %copy-done.8, f32[24,176,128]{2,1,0:T(8,128)} %get-tuple-element.19.t0, ...), custom_call_target="tpu_custom_call" | custom-call | tf_op jit(solution)/shard_map/newton2/pallas_call | solution.py:336
  185.7 1.9 collective-permute-start.12
  187.6 2.4 collective-permute-start.13
  190.1 1.9 collective-permute-done.12.above
  192.0 8.0 %collective-permute-done.13.below = f32[4,160,128]{2,1,0:T(8,128)S(1)} collective-permute-done((f32[4,160,128]{2,1,0:T(8,128)}, f32[4,160,128]{2,1,0:T(8,128)S(1)}, u32[]{:S(2)}, u32[]{:S(2)}) %collective-permute-start.13) | collective-permute-done | bytes 327712 | tf_op jit(solution)/shard_map/ppermute | solution.py:316
  199.9 0.7 copy-done.6
  200.7 19.0 %newton3.1 = (f32[16,16,8,128]{3,2,1,0:T(8,128)}, f32[16,128]{1,0:T(8,128)}) custom-call(s32[1]{0:T(128)} %bitcast.scalars, f32[16,160,128]{2,1,0:T(8,128)} %get-tuple-element.25.own_t, f32[4,160,128]{2,1,0:T(8,128)} %copy-done.5, f32[4,160,128]{2,1,0:T(8,128)} %copy-done.6, f32[24,176,128]{2,1,0:T(8,128)} %get-tuple-element.19.t0, ...), custom_call_target="tpu_custom_call" | custom-call | tf_op jit(solution)/shard_map/newton3/pallas_call | solution.py:345
  219.7 6.8 %all-to-all-start.5 = ((f32[16,16,8,128]{3,2,1,0:T(8,128)}), f32[16,16,8,128]{3,2,1,0:T(8,128)S(1)}, u32[]{:S(2)}, u32[]{:S(2)}) async-start(f32[16,16,8,128]{3,2,1,0:T(8,128)} %get-tuple-element.28), calls=%async_computation.5 | async-start | bytes 2097152 | tf_op jit(solution)/shard_map/all_to_all | solution.py:355
  226.6 0.7 pad_maximum_fusion
  227.3 22.6 %all-gather = f32[768,128]{1,0:T(8,128)} all-gather(f32[48,128]{1,0:T(8,128)S(1)} %pad_maximum_fusion), channel_id=2, replica_groups=mesh['axial'=16,'depth'=16] {'axial'}, dimensions={0}, use_global_device_ids=true | all-gather | bytes 417792 | tf_op jit(solution)/shard_map/all_gather | solution.py:361
  249.9 2.7 %deliver.1 = f32[32,128]{1,0:T(8,128)} custom-call(s32[1]{0:T(128)} %bitcast.scalars, f32[16,48,128]{2,1,0:T(8,128)} %bitcast.41), custom_call_target="tpu_custom_call" | custom-call | tf_op jit(solution)/shard_map/deliver/pallas_call | solution.py:363
  252.6 0.0 all-to-all-done.5
  252.6 1.1 copy_bitcast_fusion
  (46 shorter events, 0.1 us)
Async XLA Ops:
  0.6 10.0 %copy-start.3 = (s32[16,8,2048]{2,1,0:T(8,128)S(1)}, s32[16,8,2048]{2,1,0:T(8,128)}, u32[]{:S(2)}) copy-start(s32[16,8,2048]{2,1,0:T(8,128)} %refs_1_.1) | copy-start | bytes 3145732
  3.0 23.1 %all-to-all-start = ((f32[16,16,8,128]{3,2,1,0:T(8,128)}), f32[16,16,8,128]{3,2,1,0:T(8,128)S(1)}, u32[]{:S(2)}, u32[]{:S(2)}) async-start(f32[16,16,8,128]{3,2,1,0:T(8,128)} %bitcast_bitcast_fusion.3), calls=%async_computation | async-start | bytes 2097152 | tf_op jit(solution)/shard_map/all_to_all | solution.py:321
  10.6 19.5 %copy-start.4 = (f32[16,8,2048]{2,1,0:T(8,128)S(1)}, f32[16,8,2048]{2,1,0:T(8,128)}, u32[]{:S(2)}) copy-start(f32[16,8,2048]{2,1,0:T(8,128)} %refs_2_.1) | copy-start | bytes 3145732
  26.1 62.7 %copy-start = (f32[16,16,8,128]{3,2,1,0:T(8,128)}, f32[16,16,8,128]{3,2,1,0:T(8,128)S(1)}, u32[]{:S(2)}) copy-start(f32[16,16,8,128]{3,2,1,0:T(8,128)S(1)} %all-to-all-done.refs_0_) | copy-start | bytes 3145732
  26.1 18.3 %all-to-all-start.1 = ((f32[16,16,8,128]{3,2,1,0:T(8,128)}), f32[16,16,8,128]{3,2,1,0:T(8,128)S(1)}, u32[]{:S(2)}, u32[]{:S(2)}) async-start(f32[16,16,8,128]{3,2,1,0:T(8,128)} %bitcast_bitcast_fusion.2), calls=%async_computation.1 | async-start | bytes 2097152 | tf_op jit(solution)/shard_map/all_to_all | solution.py:321
  44.5 53.5 %copy-start.1 = (f32[16,16,8,128]{3,2,1,0:T(8,128)}, f32[16,16,8,128]{3,2,1,0:T(8,128)S(1)}, u32[]{:S(2)}) copy-start(f32[16,16,8,128]{3,2,1,0:T(8,128)S(1)} %all-to-all-done.1.refs_3_) | copy-start | bytes 3145732
  44.5 20.0 %all-to-all-start.2 = ((f32[16,16,8,128]{3,2,1,0:T(8,128)}), f32[16,16,8,128]{3,2,1,0:T(8,128)S(1)}, u32[]{:S(2)}, u32[]{:S(2)}) async-start(f32[16,16,8,128]{3,2,1,0:T(8,128)} %bitcast_bitcast_fusion.1), calls=%async_computation.2 | async-start | bytes 2097152 | tf_op jit(solution)/shard_map/all_to_all | solution.py:321
  64.4 40.0 %copy-start.2 = (f32[16,16,8,128]{3,2,1,0:T(8,128)}, f32[16,16,8,128]{3,2,1,0:T(8,128)S(1)}, u32[]{:S(2)}) copy-start(f32[16,16,8,128]{3,2,1,0:T(8,128)S(1)} %all-to-all-done.2.refs_6_) | copy-start | bytes 3145732
  64.4 19.0 %all-to-all-start.3 = ((f32[16,16,8,128]{3,2,1,0:T(8,128)}), f32[16,16,8,128]{3,2,1,0:T(8,128)}, u32[]{:S(2)}, u32[]{:S(2)}) async-start(f32[16,16,8,128]{3,2,1,0:T(8,128)} %bitcast_bitcast_fusion), calls=%async_computation.3 | async-start | bytes 2097152 | tf_op jit(solution)/shard_map/all_to_all | solution.py:321
  83.4 27.2 %all-to-all-start.4 = ((f32[16,16,8,128]{3,2,1,0:T(8,128)}), f32[16,16,8,128]{3,2,1,0:T(8,128)}, u32[]{:S(2)}, u32[]{:S(2)}) async-start(f32[16,16,8,128]{3,2,1,0:T(8,128)} %edges.1), calls=%async_computation.4 | async-start | bytes 2097152 | tf_op jit(solution)/shard_map/all_to_all | solution.py:321
  89.7 35.9 %copy-start.21 = (f32[8]{0:T(128)S(1)}, f32[8]{0:T(128)}, u32[]{:S(2)}) copy-start(f32[8]{0:T(128)} %param.17) | copy-start | bytes 100
  89.7 35.9 %copy-start.22 = (f32[8]{0:T(128)S(1)}, f32[8]{0:T(128)}, u32[]{:S(2)}) copy-start(f32[8]{0:T(128)} %param.16) | copy-start | bytes 100
  89.7 35.9 %copy-start.23 = (f32[8]{0:T(128)S(1)}, f32[8]{0:T(128)}, u32[]{:S(2)}) copy-start(f32[8]{0:T(128)} %param.15) | copy-start | bytes 100
  89.7 35.9 %copy-start.24 = (f32[8]{0:T(128)S(1)}, f32[8]{0:T(128)}, u32[]{:S(2)}) copy-start(f32[8]{0:T(128)} %param.14) | copy-start | bytes 100
  89.7 22.7 %collective-permute-start = (f32[16,4,8,128]{3,2,1,0:T(8,128)}, f32[16,4,8,128]{3,2,1,0:T(8,128)S(1)}, u32[]{:S(2)}, u32[]{:S(2)}) collective-permute-start(f32[16,4,8,128]{3,2,1,0:T(8,128)} %get-tuple-element.39), channel_id=1, source_target_pairs={{0,16},{16,32},{32,48},{48,64},{64,80},{80,96},{96,112},{112,128},... | collective-permute-start | bytes 786440 | tf_op jit(solution)/shard_map/ppermute | solution.py:313
  96.1 18.3 %collective-permute-start.1 = (f32[16,4,8,128]{3,2,1,0:T(8,128)}, f32[16,4,8,128]{3,2,1,0:T(8,128)S(1)}, u32[]{:S(2)}, u32[]{:S(2)}) collective-permute-start(f32[16,4,8,128]{3,2,1,0:T(8,128)} %get-tuple-element.38), channel_id=1, source_target_pairs={{16,0},{32,16},{48,32},{64,48},{80,64},{96,80},{112,96},{128,112},... | collective-permute-start | bytes 786440 | tf_op jit(solution)/shard_map/ppermute | solution.py:316
  98.8 19.2 %collective-permute-start.2 = (f32[16,4,8,128]{3,2,1,0:T(8,128)}, f32[16,4,8,128]{3,2,1,0:T(8,128)S(1)}, u32[]{:S(2)}, u32[]{:S(2)}) collective-permute-start(f32[16,4,8,128]{3,2,1,0:T(8,128)} %get-tuple-element.37), channel_id=1, source_target_pairs={{0,16},{16,32},{32,48},{48,64},{64,80},{80,96},{96,112},{112,128},... | collective-permute-start | bytes 786440 | tf_op jit(solution)/shard_map/ppermute | solution.py:313
  102.5 17.5 %collective-permute-start.3 = (f32[16,4,8,128]{3,2,1,0:T(8,128)}, f32[16,4,8,128]{3,2,1,0:T(8,128)S(1)}, u32[]{:S(2)}, u32[]{:S(2)}) collective-permute-start(f32[16,4,8,128]{3,2,1,0:T(8,128)} %get-tuple-element.36), channel_id=1, source_target_pairs={{16,0},{32,16},{48,32},{64,48},{80,64},{96,80},{112,96},{128,112},... | collective-permute-start | bytes 786440 | tf_op jit(solution)/shard_map/ppermute | solution.py:316
  105.2 18.4 %collective-permute-start.4 = (f32[16,4,8,128]{3,2,1,0:T(8,128)}, f32[16,4,8,128]{3,2,1,0:T(8,128)S(1)}, u32[]{:S(2)}, u32[]{:S(2)}) collective-permute-start(f32[16,4,8,128]{3,2,1,0:T(8,128)} %get-tuple-element.35), channel_id=1, source_target_pairs={{0,16},{16,32},{32,48},{48,64},{64,80},{80,96},{96,112},{112,128},... | collective-permute-start | bytes 786440 | tf_op jit(solution)/shard_map/ppermute | solution.py:313
  112.4 18.9 %copy-start.9 = (f32[16,4,8,128]{3,2,1,0:T(8,128)}, f32[16,4,8,128]{3,2,1,0:T(8,128)S(1)}, u32[]{:S(2)}) copy-start(f32[16,4,8,128]{3,2,1,0:T(8,128)S(1)} %collective-permute-done.refs_1_) | copy-start | bytes 786436
  112.4 13.8 %collective-permute-start.5 = (f32[16,4,8,128]{3,2,1,0:T(8,128)S(1)}, f32[16,4,8,128]{3,2,1,0:T(8,128)S(1)}, u32[]{:S(2)}, u32[]{:S(2)}) collective-permute-start(f32[16,4,8,128]{3,2,1,0:T(8,128)S(1)} %get-tuple-element.34), channel_id=1, source_target_pairs={{16,0},{32,16},{48,32},{64,48},{80,64},{96,80},{112,96},{128,112},... | collective-permute-start | bytes 786440 | tf_op jit(solution)/shard_map/ppermute | solution.py:316
  114.3 17.0 %copy-start.10 = (f32[16,4,8,128]{3,2,1,0:T(8,128)}, f32[16,4,8,128]{3,2,1,0:T(8,128)S(1)}, u32[]{:S(2)}) copy-start(f32[16,4,8,128]{3,2,1,0:T(8,128)S(1)} %collective-permute-done.1.refs_2_) | copy-start | bytes 786436
  114.3 11.9 %collective-permute-start.6 = (f32[16,4,8,128]{3,2,1,0:T(8,128)}, f32[16,4,8,128]{3,2,1,0:T(8,128)S(1)}, u32[]{:S(2)}, u32[]{:S(2)}) collective-permute-start(f32[16,4,8,128]{3,2,1,0:T(8,128)} %get-tuple-element.33), channel_id=1, source_target_pairs={{0,16},{16,32},{32,48},{48,64},{64,80},{80,96},{96,112},{112,128},... | collective-permute-start | bytes 786440 | tf_op jit(solution)/shard_map/ppermute | solution.py:313
  118.0 13.3 %copy-start.11 = (f32[16,4,8,128]{3,2,1,0:T(8,128)}, f32[16,4,8,128]{3,2,1,0:T(8,128)S(1)}, u32[]{:S(2)}) copy-start(f32[16,4,8,128]{3,2,1,0:T(8,128)S(1)} %collective-permute-done.2.refs_4_) | copy-start | bytes 786436
  118.0 8.2 %collective-permute-start.7 = (f32[16,4,8,128]{3,2,1,0:T(8,128)S(1)}, f32[16,4,8,128]{3,2,1,0:T(8,128)S(1)}, u32[]{:S(2)}, u32[]{:S(2)}) collective-permute-start(f32[16,4,8,128]{3,2,1,0:T(8,128)S(1)} %get-tuple-element.32), channel_id=1, source_target_pairs={{16,0},{32,16},{48,32},{64,48},{80,64},{96,80},{112,96},{128,112},... | collective-permute-start | bytes 786440 | tf_op jit(solution)/shard_map/ppermute | solution.py:316
  120.0 11.4 %copy-start.12 = (f32[16,4,8,128]{3,2,1,0:T(8,128)}, f32[16,4,8,128]{3,2,1,0:T(8,128)S(1)}, u32[]{:S(2)}) copy-start(f32[16,4,8,128]{3,2,1,0:T(8,128)S(1)} %collective-permute-done.3.refs_5_) | copy-start | bytes 786436
  120.0 7.3 %collective-permute-start.8 = (f32[16,4,8,128]{3,2,1,0:T(8,128)}, f32[16,4,8,128]{3,2,1,0:T(8,128)S(1)}, u32[]{:S(2)}, u32[]{:S(2)}) collective-permute-start(f32[16,4,8,128]{3,2,1,0:T(8,128)} %get-tuple-element.31), channel_id=1, source_target_pairs={{0,16},{16,32},{32,48},{48,64},{64,80},{80,96},{96,112},{112,128},... | collective-permute-start | bytes 786440 | tf_op jit(solution)/shard_map/ppermute | solution.py:313
  123.6 7.7 %copy-start.13 = (f32[16,4,8,128]{3,2,1,0:T(8,128)}, f32[16,4,8,128]{3,2,1,0:T(8,128)S(1)}, u32[]{:S(2)}) copy-start(f32[16,4,8,128]{3,2,1,0:T(8,128)S(1)} %collective-permute-done.4.refs_7_) | copy-start | bytes 786436
  123.6 7.7 %collective-permute-start.9 = (f32[16,4,8,128]{3,2,1,0:T(8,128)S(1)}, f32[16,4,8,128]{3,2,1,0:T(8,128)S(1)}, u32[]{:S(2)}, u32[]{:S(2)}) collective-permute-start(f32[16,4,8,128]{3,2,1,0:T(8,128)S(1)} %get-tuple-element.30), channel_id=1, source_target_pairs={{16,0},{32,16},{48,32},{64,48},{80,64},{96,80},{112,96},{128,112},... | collective-permute-start | bytes 786440 | tf_op jit(solution)/shard_map/ppermute | solution.py:316
  126.2 5.2 %copy-start.14 = (f32[16,4,8,128]{3,2,1,0:T(8,128)}, f32[16,4,8,128]{3,2,1,0:T(8,128)S(1)}, u32[]{:S(2)}) copy-start(f32[16,4,8,128]{3,2,1,0:T(8,128)S(1)} %collective-permute-done.5.refs_8_) | copy-start | bytes 786436
  126.2 5.2 %copy-start.15 = (f32[16,4,8,128]{3,2,1,0:T(8,128)}, f32[16,4,8,128]{3,2,1,0:T(8,128)S(1)}, u32[]{:S(2)}) copy-start(f32[16,4,8,128]{3,2,1,0:T(8,128)S(1)} %collective-permute-done.6.refs_10_) | copy-start | bytes 786436
  126.2 5.2 %copy-start.16 = (f32[16,4,8,128]{3,2,1,0:T(8,128)}, f32[16,4,8,128]{3,2,1,0:T(8,128)S(1)}, u32[]{:S(2)}) copy-start(f32[16,4,8,128]{3,2,1,0:T(8,128)S(1)} %collective-permute-done.7.refs_11_) | copy-start | bytes 786436
  127.2 4.2 %copy-start.17 = (f32[16,4,8,128]{3,2,1,0:T(8,128)}, f32[16,4,8,128]{3,2,1,0:T(8,128)S(1)}, u32[]{:S(2)}) copy-start(f32[16,4,8,128]{3,2,1,0:T(8,128)S(1)} %collective-permute-done.8.refs_13_) | copy-start | bytes 786436
  131.3 0.7 copy-start.18
  156.1 6.2 %collective-permute-start.10 = (f32[4,160,128]{2,1,0:T(8,128)}, f32[4,160,128]{2,1,0:T(8,128)S(1)}, u32[]{:S(2)}, u32[]{:S(2)}) collective-permute-start(f32[4,160,128]{2,1,0:T(8,128)} %get-tuple-element.17), channel_id=1, source_target_pairs={{0,16},{16,32},{32,48},{48,64},{64,80},{80,96},{96,112},{112,128},... | collective-permute-start | bytes 983048 | tf_op jit(solution)/shard_map/ppermute | solution.py:313
  158.0 8.9 %collective-permute-start.11 = (f32[4,160,128]{2,1,0:T(8,128)}, f32[4,160,128]{2,1,0:T(8,128)S(1)}, u32[]{:S(2)}, u32[]{:S(2)}) collective-permute-start(f32[4,160,128]{2,1,0:T(8,128)} %get-tuple-element.18), channel_id=1, source_target_pairs={{16,0},{32,16},{48,32},{64,48},{80,64},{96,80},{112,96},{128,112},... | collective-permute-start | bytes 983048 | tf_op jit(solution)/shard_map/ppermute | solution.py:316
  162.3 4.6 %copy-start.7 = (f32[4,160,128]{2,1,0:T(8,128)}, f32[4,160,128]{2,1,0:T(8,128)S(1)}, u32[]{:S(2)}) copy-start(f32[4,160,128]{2,1,0:T(8,128)S(1)} %collective-permute-done.10.above) | copy-start | bytes 983044
  166.9 0.7 copy-start.8
  185.7 6.2 %collective-permute-start.12 = (f32[4,160,128]{2,1,0:T(8,128)}, f32[4,160,128]{2,1,0:T(8,128)S(1)}, u32[]{:S(2)}, u32[]{:S(2)}) collective-permute-start(f32[4,160,128]{2,1,0:T(8,128)} %get-tuple-element.26), channel_id=1, source_target_pairs={{0,16},{16,32},{32,48},{48,64},{64,80},{80,96},{96,112},{112,128},... | collective-permute-start | bytes 983048 | tf_op jit(solution)/shard_map/ppermute | solution.py:313
  187.6 12.3 %collective-permute-start.13 = (f32[4,160,128]{2,1,0:T(8,128)}, f32[4,160,128]{2,1,0:T(8,128)S(1)}, u32[]{:S(2)}, u32[]{:S(2)}) collective-permute-start(f32[4,160,128]{2,1,0:T(8,128)} %get-tuple-element.27), channel_id=1, source_target_pairs={{16,0},{32,16},{48,32},{64,48},{80,64},{96,80},{112,96},{128,112},... | collective-permute-start | bytes 983048 | tf_op jit(solution)/shard_map/ppermute | solution.py:316
  192.0 8.0 %copy-start.5 = (f32[4,160,128]{2,1,0:T(8,128)}, f32[4,160,128]{2,1,0:T(8,128)S(1)}, u32[]{:S(2)}) copy-start(f32[4,160,128]{2,1,0:T(8,128)S(1)} %collective-permute-done.12.above) | copy-start | bytes 983044
  199.9 0.7 copy-start.6
  200.7 25.9 %copy-start.19 = (s32[16,128]{1,0:T(8,128)S(1)}, s32[16,128]{1,0:T(8,128)}, u32[]{:S(2)}) copy-start(s32[16,128]{1,0:T(8,128)} %param.19) | copy-start | bytes 24580
  200.7 25.9 %copy-start.20 = (s32[16,128]{1,0:T(8,128)S(1)}, s32[16,128]{1,0:T(8,128)}, u32[]{:S(2)}) copy-start(s32[16,128]{1,0:T(8,128)} %param.18) | copy-start | bytes 24580
  219.7 32.9 %all-to-all-start.5 = ((f32[16,16,8,128]{3,2,1,0:T(8,128)}), f32[16,16,8,128]{3,2,1,0:T(8,128)S(1)}, u32[]{:S(2)}, u32[]{:S(2)}) async-start(f32[16,16,8,128]{3,2,1,0:T(8,128)} %get-tuple-element.28), calls=%async_computation.5 | async-start | bytes 2097152 | tf_op jit(solution)/shard_map/all_to_all | solution.py:355

commit v2 on v1

v2 whole, which is shorter than its diff:
```python
import functools

import jax
import jax.numpy as jnp
from jax import lax
from jax.experimental import pallas as pl
from jax.experimental.pallas import tpu as pltpu
from jax.sharding import PartitionSpec as P

SWEEPS = 4
H = 4
W = 16
PAD = 8
LANES = 128
WIDE = (PAD, PAD + 2 * W + LANES)
NEAR = (PAD + W // 2, PAD + W + LANES + W // 2)
CORE = (PAD + W, PAD + W + LANES)
FULL = WIDE[1] + PAD
VMEM_LIMIT = 12 * 1024 * 1024

VM = pl.BlockSpec(memory_space=pltpu.VMEM)
SM = pl.BlockSpec(memory_space=pltpu.SMEM)


def f32(*shape):
    return jax.ShapeDtypeStruct(shape, jnp.float32)


def call(kernel, name, scalars, reads, updates, makes, scratch=(), kept=True, space=pltpu.VMEM):
    counts = [len(scalars), len(reads), len(updates), len(updates), len(makes), len(scratch)]

    def body(*refs):
        groups, at = [], 0
        for count in counts:
            groups.append(refs[at : at + count])
            at += count
        kernel(groups[0], groups[1], groups[3], groups[4], groups[5])

    first = len(scalars) + len(reads)
    results = pl.pallas_call(
        body,
        out_shape=[pltpu.VMEM(u.shape, jnp.float32) for u in updates]
        + [pltpu.VMEM(s, jnp.float32) if kept else f32(*s) for s in makes],
        in_specs=[SM] * len(scalars)
        + [pl.BlockSpec(memory_space=space)] * len(reads)
        + [VM] * len(updates),
        out_specs=[VM] * (len(updates) + len(makes)),
        input_output_aliases={first + i: i for i in range(len(updates))},
        scratch_shapes=list(scratch),
        compiler_params=pltpu.CompilerParams(vmem_limit_bytes=VMEM_LIMIT),
        name=name,
    )(*scalars, *reads, *updates)
    return list(results)


def lane_iota(rows):
    return lax.broadcasted_iota(jnp.int32, (rows, LANES), 1)


def split3(x):
    a = x.astype(jnp.bfloat16)
    rest = x - a.astype(jnp.float32)
    b = rest.astype(jnp.bfloat16)
    c = (rest - b.astype(jnp.float32)).astype(jnp.bfloat16)
    return a, b, c


def over(ranges, body):
    for low, high in ranges:
        for r in range(low, high):
            body(r)


def pack_kernel(scalars, ins, updates, makes, scratch):
    (out,), held, sems = makes, scratch[:-1], scratch[-1]
    slices = out.shape[0]
    own = ins[0].shape[0]
    lane = lane_iota(8)
    copies = [pltpu.make_async_copy(x, y, sems.at[i]) for i, (x, y) in enumerate(zip(ins, held))]
    for copy in copies:
        copy.start()

    def spread(i):
        def row(a, _):
            for s in range(slices):
                out[s, i * own + a] = held[i][a, :, LANES * s : LANES * (s + 1)].astype(jnp.float32)
            return 0

        return row

    for i, copy in enumerate(copies):
        copy.wait()
        lax.fori_loop(0, own, spread(i), 0, unroll=4)

    def rims(a, _):
        turned = [
            [
                pltpu.roll(
                    x[a, :, LANES * s : LANES * (s + 1)].astype(jnp.float32), (2 * W * i + W) % LANES, 1
                )
                for s in range(slices)
            ]
            for i, x in enumerate(held)
        ]
        for s in range(slices):
            result = turned[0][s - 1]
            for i in range(len(ins)):
                if i:
                    result = jnp.where(lane >= 2 * W * i, turned[i][s - 1], result)
                result = jnp.where(lane >= 2 * W * i + W, turned[i][(s + 1) % slices], result)
            out[s, len(ins) * own + a] = result
        return 0

    lax.fori_loop(0, own, rims, 0)


def rim_rows(kind):
    return H if kind in (0, 4) else H - 1


def rim_start(kind):
    return sum(rim_rows(k) for k in range(kind))


def rims_kernel(scalars, reads, updates, makes, scratch):
    (arrived,), (top, bottom) = reads, makes
    own = arrived.shape[1] // 5
    for kind in range(5):
        count, at = rim_rows(kind), rim_start(kind)
        bottom[:, at : at + count] = arrived[:, kind * own : kind * own + count]
        top[:, at : at + count] = arrived[:, (kind + 1) * own - count : (kind + 1) * own]


def suffix_matrix(m_ref):
    rows, cols = m_ref.shape
    source = lax.broadcasted_iota(jnp.int32, (rows, cols), 0) & (LANES - 1)
    target = lax.broadcasted_iota(jnp.int32, (rows, cols), 1)
    m_ref[...] = jnp.where(source > target, 4.0 / LANES, 0.0).astype(jnp.bfloat16)


def linearise(r, row, total_rows, span, t, t0, fields, m_ref):
    lo, hi = span
    conduct, capacity, act, pre = fields
    lane = lane_iota(hi - lo)
    tc = t[r, lo:hi]
    a = act[r, lo:hi]
    q = 1.0 / (1.0 + jnp.abs(tc))
    aq = a * q
    p = pre[r, lo:hi] * jnp.exp(aq * tc)
    gas = jnp.dot(jnp.concatenate(split3(p), axis=1), m_ref[...], preferred_element_type=jnp.float32)
    c = conduct[r, lo:hi]
    cap = capacity[r, lo:hi]
    deeper = jnp.where(lane == LANES - 1, 0.0, pltpu.roll(tc, LANES - 1, 1))
    shallower = jnp.where(lane == 0, 0.0, pltpu.roll(tc, 1, 1))
    pairs = t[r - 1, lo:hi] + t[r + 1, lo:hi] + t[r, lo - 1 : hi - 1] + t[r, lo + 1 : hi + 1]
    spread = pairs + 2.0 * (deeper + shallower) - 8.0 * tc
    source = c * spread - 0.5 * p - gas * (tc - deeper)
    if t0 is not None:
        source = source - cap * (tc - t0[r, lo:hi])
    diagonal = cap + 8.0 * c + 0.5 * p * (aq * q) + gas
    inside = jnp.where((row >= 0) & (row < total_rows), 1.0, 0.0)
    inverse = inside / diagonal
    return source, inverse, c * inverse, jnp.where(lane == LANES - 1, 0.0, (2.0 * c + gas) * inverse)


def sweeps(span, work, ranges, finish):
    lo, hi = span
    first, side, down, b, c = work
    lane = lane_iota(hi - lo)

    def swept(src, r):
        u = src[r, lo:hi]
        pairs = src[r - 1, lo:hi] + src[r + 1, lo:hi] + src[r, lo - 1 : hi - 1] + src[r, lo + 1 : hi + 1]
        shallower = jnp.where(lane == 0, 0.0, pltpu.roll(u, 1, 1))
        deeper = pltpu.roll(u, LANES - 1, 1)
        return first[r, lo:hi] + side[r, lo:hi] * (pairs + 2.0 * shallower) + down[r, lo:hi] * deeper

    def second(r):
        b[r, lo:hi] = swept(first, r)

    def third(r):
        c[r, lo:hi] = swept(b, r)

    over(ranges[0], second)
    over(ranges[1], third)
    over(ranges[2], lambda r: finish(r, swept(c, r)))


def inner_rows(rows, k):
    return [(H + k, rows - H - k)]


def outer_rows(rows, k):
    return [(k, H + k), (rows - H - k, rows - k)]


def from_cells(ref, r):
    x = ref[:, r]
    return x.reshape(x.shape[0] * x.shape[1], LANES).T


def unpack_row(tables, arrived, at, r, state):
    t0, conduct, capacity, act, pre, dep = state
    lo, hi = WIDE
    edges = from_cells(arrived, at[4])

    def whole(kind):
        e = 2 * W * kind
        return jnp.concatenate(
            [edges[e : e + W], from_cells(arrived, at[kind]), edges[e + W : e + 2 * W]], axis=0
        )

    t0[r, lo:hi] = whole(0)
    if at[1] is None:
        return
    label = whole(1)
    fields = [jnp.full(label.shape, tables[f, 0], jnp.float32) for f in range(4)]
    for zone in range(1, tables.shape[1]):
        here = label == float(zone)
        fields = [jnp.where(here, tables[f, zone], x) for f, x in enumerate(fields)]
    conduct[r, lo:hi] = fields[0]
    capacity[r, lo:hi] = fields[1]
    pre[r, lo:hi] = fields[2] * whole(2)
    act[r, lo:hi] = fields[3]
    dep[r, lo:hi] = whole(3)


def keeper(span, t, t_new, rims):
    lo, hi = span
    own = t.shape[0] - 2 * H

    def finish(r, update):
        value = (t[r, lo:hi] + update)[NEAR[0] - lo : NEAR[1] - lo]
        t_new[r, slice(*NEAR)] = value
        if rims is not None and r >= own:
            rims[0][r - own] = value
        if rims is not None and r < 2 * H:
            rims[1][r - H] = value

    return finish


def first_kernel(outer, total_rows, scalars, reads, updates, makes, scratch):
    place, tables = scalars
    arrays, rims = (updates, makes) if outer else (makes, None)
    state, (ua, cs, cd, ub, uc, t_new) = arrays[:6], arrays[6:]
    t0, conduct, capacity, act, pre, dep = state
    rows = t0.shape[0]
    own = rows - 2 * H
    suffix_matrix(scratch[0])
    if outer:
        for i in range(H):
            for ref, r, missing in ((reads[0], i, i == 0), (reads[1], i + H + own, i == H - 1)):
                skip = H if ref is reads[0] else 0
                at = [rim_start(k) + (i - (H - rim_rows(k)) if skip else i) for k in range(5)]
                if missing:
                    at[1:4] = [None] * 3
                unpack_row(tables, ref, at, r, state)
    else:
        for i in range(own):
            unpack_row(tables, reads[0], [k * own + i for k in range(5)], i + H, state)
    lo, hi = WIDE

    def one(r):
        source, inverse, side, down = linearise(
            r, place[0] * own + r - H, total_rows, WIDE, t0, None, (conduct, capacity, act, pre), scratch[0]
        )
        ua[r, lo:hi] = (source + dep[r, lo:hi]) * inverse
        cs[r, lo:hi] = side
        cd[r, lo:hi] = down

    ranges = outer_rows if outer else inner_rows
    over(ranges(rows, 1), one)
    sweeps(WIDE, (ua, cs, cd, ub, uc), [ranges(rows, k) for k in (2, 3, 4)], keeper(WIDE, t0, t_new, rims))


def later_kernel(outer, last, total_rows, scalars, reads, updates, makes, scratch):
    (place,) = scalars
    lo, hi = NEAR
    if outer:
        above, below, t0, conduct, capacity, act, pre, dep = reads[:8]
        t, ua, cs, cd, ub, uc = updates[:6]
        results, rims = (makes, None) if last else (updates[6:], makes)
    else:
        t, t0, conduct, capacity, act, pre, dep = reads
        ua, cs, cd, ub, uc = makes[:5]
        results, rims = makes[5:], None
    rows = t0.shape[0]
    own = rows - 2 * H
    suffix_matrix(scratch[0])
    if outer:
        t[0:H, lo:hi] = above[...]
        t[H + own :, lo:hi] = below[...]

    def one(r):
        source, inverse, side, down = linearise(
            r, place[0] * own + r - H, total_rows, NEAR, t, t0, (conduct, capacity, act, pre), scratch[0]
        )
        ua[r, lo:hi] = (source + dep[r, lo:hi]) * inverse
        cs[r, lo:hi] = side
        cd[r, lo:hi] = down

    if last:
        out, blowing = results
        if outer:
            out[...], blowing[...] = reads[8][...], reads[9][...]
        core = slice(*CORE)
        mid = slice(CORE[0] - lo, CORE[1] - lo)

        def finish(r, update):
            value = t[r, core] + update[mid]
            out[:, r - H] = value.T.reshape(out.shape[0], 8, LANES)
            p = pre[r, core] * jnp.exp(act[r, core] * value / (1.0 + jnp.abs(value)))
            blowing[r - H : r - H + 1, :] = jnp.sum(p.T, axis=0, keepdims=True) * (1.0 / LANES)

    else:
        finish = keeper(NEAR, t, results[0], rims)
    ranges = outer_rows if outer else inner_rows
    over(ranges(rows, 1), one)
    sweeps(NEAR, (ua, cs, cd, ub, uc), [ranges(rows, k) for k in (2, 3, 4)], finish)


def deliver_kernel(scalars, reads, updates, makes, scratch):
    (gathered,), (out,), (left, right) = reads, makes, scratch
    groups, rows3, _ = gathered.shape
    rows = rows3 // 3
    me = scalars[0][0]
    owners = gathered[:, 2 * rows :, :].astype(jnp.int32)
    shape = owners.shape
    number = lax.broadcasted_iota(jnp.int32, shape, 0) * rows + lax.broadcasted_iota(jnp.int32, shape, 1)
    first = jnp.min(jnp.where(owners == me, number, groups * rows))
    most = out.shape[0]
    first = jnp.minimum(first, groups * rows - most)
    high_of = lax.broadcasted_iota(jnp.int32, (most, LANES), 0)
    low_of = lax.broadcasted_iota(jnp.int32, (LANES, LANES), 0)
    for i in range(most):
        at = first + i
        group, r = at // rows, at % rows
        value = gathered[group, pl.ds(r, 1), :]
        slot = gathered[group, pl.ds(rows + r, 1), :].astype(jnp.int32)
        owner = gathered[group, pl.ds(2 * rows + r, 1), :].astype(jnp.int32)
        high = jnp.where(owner == me, slot >> 7, -1)
        low = slot & (LANES - 1)
        here = slice(LANES * i, LANES * (i + 1))
        hit = high_of == high
        for k, part in enumerate(split3(value)):
            left[most * k : most * (k + 1), here] = jnp.where(hit, part.astype(jnp.float32), 0.0).astype(
                jnp.bfloat16
            )
        right[:, here] = jnp.where(low_of == low, 1.0, 0.0).astype(jnp.bfloat16)
    parts = lax.dot_general(
        left[...], right[...], (((1,), (1,)), ((), ())), preferred_element_type=jnp.float32
    )
    out[...] = parts[:most] + parts[most : 2 * most] + parts[2 * most :]


def shards(
    kelvin_before_step,
    unburnt_resin_share,
    deposited_energy_amount,
    material_label,
    zonal_diffusivity,
    zonal_storage_coefficient,
    frequency_coefficient,
    arrhenius_barrier,
    stream_keeper,
    keeper_position,
):
    own, layers, columns = kelvin_before_step.shape
    n_axial, n_depth = lax.axis_size("axial"), lax.axis_size("depth")
    place = lax.axis_index("axial").astype(jnp.int32).reshape(1)
    total_rows = own * n_axial
    tables = jnp.stack(
        [zonal_diffusivity, zonal_storage_coefficient, frequency_coefficient, arrhenius_barrier]
    )
    rows = own + 2 * H
    extended = (rows, FULL, LANES)
    rim = (H, NEAR[1] - NEAR[0], LANES)
    matrix = [pltpu.VMEM((3 * LANES, LANES), jnp.bfloat16)]

    def up(x):
        return lax.ppermute(x, "axial", [(i, i + 1) for i in range(n_axial - 1)])

    def down(x):
        return lax.ppermute(x, "axial", [(i + 1, i) for i in range(n_axial - 1)])

    cells = [kelvin_before_step, material_label, unburnt_resin_share, deposited_energy_amount]
    (sent,) = call(
        pack_kernel, "pack", [], cells, [], [(n_depth, 5 * own, layers, LANES)],
        [pltpu.VMEM(x.shape, x.dtype) for x in cells] + [pltpu.SemaphoreType.DMA((4,))],
        kept=False, space=pltpu.HBM,
    )
    arrived = lax.all_to_all(sent, "depth", 0, 0)
    top, bottom = call(
        rims_kernel, "rims", [], [arrived], [], [(n_depth, rim_start(5), layers, LANES)] * 2
    )
    above, below = up(top), down(bottom)
    arrays = call(
        functools.partial(first_kernel, False, total_rows), "newton1_inner",
        [place, tables], [arrived], [], [extended] * 12, matrix,
    )
    *arrays, top, bottom = call(
        functools.partial(first_kernel, True, total_rows), "newton1_outer",
        [place, tables], [above, below], arrays, [rim] * 2, matrix,
    )
    t0, conduct, capacity, act, pre, dep = arrays[:6]
    t = arrays[-1]
    for last in (False, True):
        above, below = up(top), down(bottom)
        fixed = [t0, conduct, capacity, act, pre, dep]
        results = [(n_depth, own, layers, LANES), (own, LANES)] if last else [extended]
        work = call(
            functools.partial(later_kernel, False, last, total_rows), "newton3_inner" if last else "newton2_inner",
            [place], [t] + fixed, [], [extended] * 5 + results, matrix,
        )
        work, results = work[:5], work[5:]
        work = call(
            functools.partial(later_kernel, True, last, total_rows), "newton3_outer" if last else "newton2_outer",
            [place], [above, below] + fixed + (results if last else []), [t] + work + ([] if last else results),
            [(n_depth, own, layers, LANES), (own, LANES)] if last else [rim] * 2, matrix, kept=not last,
        )
        if not last:
            t, top, bottom = work[6:]
    kelvin, blowing = work[6:]

    kelvin = lax.all_to_all(kelvin, "depth", 0, 0)
    kelvin = jnp.transpose(kelvin, (1, 2, 0, 3)).reshape(own, layers, columns)

    faces = jnp.concatenate(
        [blowing, keeper_position.astype(jnp.float32), stream_keeper.astype(jnp.float32)], axis=0
    )
    gathered = lax.all_gather(faces, "axial")
    slots = 2 * own * LANES
    (delivered,) = call(
        deliver_kernel, "deliver", [place], [gathered], [], [(slots // LANES, LANES)],
        [
            pltpu.VMEM((3 * slots // LANES, slots), jnp.bfloat16),
            pltpu.VMEM((LANES, slots), jnp.bfloat16),
        ],
        kept=False,
    )
    return (kelvin, delivered.reshape(slots))


def solution(mesh):
    cells = P("axial", "depth", None)
    faces = P("axial", "depth")
    return jax.shard_map(
        shards,
        mesh=mesh,
        in_specs=(cells, cells, cells, cells, P(), P(), P(), P(), faces, faces),
        out_specs=(cells, P(("axial", "depth"))),
        check_vma=False,
    )
```

time: 255 us -> 159 us (0.62)
  blocking collectives: 22.6 us -> 87.6 us
  waiting for transfers between devices: 70.4 us -> 10.3 us
  starting transfers between devices: 72.8 us -> 20.6 us
  Pallas kernels: 69.3 us -> 29.1 us
  local copies, waits for them, and re-layouts: 15.1 us -> 9.99 us
    all_to_all x0 -> x1, blocking collectives: none -> 68 us  [shards(): arrived = lax.all_to_all(sent, 'depth', 0, 0)]
    all_to_all x5 -> x0, waiting for transfers between devices: 49 us -> none  [shards(): y = lax.all_to_all(x, 'depth', 0, 0)]
    pallas_call x5 -> x9, Pallas kernels: 69.3 us -> 29.1 us  [call(): pl.pallas_call(body, out_shape=[pltpu.VMEM(u.shape, jnp.float32) for u in...]
    all_to_all x5 -> x0, starting transfers between devices: 26.8 us -> none  [shards(): y = lax.all_to_all(x, 'depth', 0, 0)]
    ppermute x7 -> x3, starting transfers between devices: 24.7 us -> 9.77 us  [up(): return lax.ppermute(x, 'axial', [(i, i + 1) for i in range(n_axial - 1)])]
    ppermute x7 -> x3, waiting for transfers between devices: 16.7 us -> 8.1 us  [down(): return lax.ppermute(x, 'axial', [(i + 1, i) for i in range(n_axial - 1)])]
    ppermute x7 -> x3, starting transfers between devices: 14.4 us -> 6.94 us  [down(): return lax.ppermute(x, 'axial', [(i + 1, i) for i in range(n_axial - 1)])]
    unnamed x50 -> x24, local copies, waits for them, and re-layouts: 2.19 us -> 8.91 us
  transfers between devices with their start and end apart: 20 -> 7, of which waited for: 10 -> 4; matrix products, arithmetic and copies ran while one was open for 5% -> 0% of each run, Pallas kernels for 3% -> 10%
where the time goes in v2:
time: 159 us
  blocking collectives  87.6 us (55%)
  Pallas kernels  29.1 us (18%)
  starting transfers between devices  20.6 us (13%)
  waiting for transfers between devices  10.3 us (6%)
  local copies, waits for them, and re-layouts  9.99 us (6%)
    all_to_all x1, blocking collectives, shards(): arrived = lax.all_to_all(sent, 'depth', 0, 0)  68 us
    pallas_call x9, Pallas kernels, call(): pl.pallas_call(body, out_shape=[pltpu.VMEM(u.shape, jnp.float32) for u in...  29.1 us
    all_gather x1, blocking collectives, shards(): gathered = lax.all_gather(faces, 'axial')  19.6 us
    ppermute x3, starting transfers between devices, up(): return lax.ppermute(x, 'axial', [(i, i + 1) for i in range(n_axial - 1)])  9.77 us
    unnamed x24, local copies, waits for them, and re-layouts  8.91 us
    ppermute x3, waiting for transfers between devices, down(): return lax.ppermute(x, 'axial', [(i + 1, i) for i in range(n_axial - 1)])  8.1 us
    ppermute x3, starting transfers between devices, down(): return lax.ppermute(x, 'axial', [(i + 1, i) for i in range(n_axial - 1)])  6.94 us
    all_to_all x1, starting transfers between devices, shards(): kelvin = lax.all_to_all(kelvin, 'depth', 0, 0)  3.92 us
  transfers between devices with their start and end apart: 7, of which 4 were waited for; matrix products, arithmetic and copies ran while one was open for 0% of the time, Pallas kernels for 10%

profile of v2, /device:TPU:1, one launch (start us, length us, event | category | flops | bytes accessed | tf_op | source)
XLA Modules:
  0.0 158.5 jit_solution(13422171799552146252)
XLA Ops:
  0.6 0.0 copy-start.2
  0.6 1.2 copy-done.2
  1.9 0.0 copy-start.3
  1.9 1.2 copy-done.3
  3.1 0.0 copy-start.4
  3.1 1.2 copy-done.4
  4.3 0.0 copy-start.5
  4.3 1.2 copy-done.5
  5.5 2.9 %pack.1 = f32[16,80,8,128]{3,2,1,0:T(8,128)S(1)} custom-call(f32[16,8,2048]{2,1,0:T(8,128)S(1)} %copy-done.2, s32[16,8,2048]{2,1,0:T(8,128)S(1)} %copy-done.3, f32[16,8,2048]{2,1,0:T(8,128)S(1)} %copy-done.4, f32[16,8,2048]{2,1,0:T(8,128)S(1)} %copy-done.5), custom_call_target="tpu_custom_call" | custom-call | tf_op jit(solution)/shard_map/pack/pallas_call | solution.py:40
  8.5 68.0 %all_to_all.10.refs_0_.refs_2_ = f32[16,80,8,128]{3,2,1,0:T(8,128)S(1)} all-to-all(f32[16,80,8,128]{3,2,1,0:T(8,128)S(1)} %pack.1), channel_id=1, replica_groups=mesh['axial'=16,'depth'=16] {'depth'}, dimensions={0} | all-to-all | bytes 10485760 | tf_op jit(solution)/shard_map/all_to_all | solution.py:393
  76.4 0.0 copy-start
  76.4 0.0 copy-start.8
  76.4 0.0 copy-start.9
  76.4 0.0 copy-start.10
  76.4 0.0 copy-start.11
  76.5 1.1 rims.1
  77.6 1.5 copy-done
  79.1 5.9 %collective-permute-start = (f32[16,17,8,128]{3,2,1,0:T(8,128)}, f32[16,17,8,128]{3,2,1,0:T(8,128)S(1)}, u32[]{:S(2)}, u32[]{:S(2)}) collective-permute-start(f32[16,17,8,128]{3,2,1,0:T(8,128)} %get-tuple-element.43), channel_id=1, source_target_pairs={{0,16},{16,32},{32,48},{48,64},{64,80},{80,96},{96,112},{112,128},... | collective-permute-start | bytes 3342344 | tf_op jit(solution)/shard_map/ppermute | solution.py:382
  85.1 1.9 %collective-permute-start.1 = (f32[16,17,8,128]{3,2,1,0:T(8,128)S(1)}, f32[16,17,8,128]{3,2,1,0:T(8,128)S(1)}, u32[]{:S(2)}, u32[]{:S(2)}) collective-permute-start(f32[16,17,8,128]{3,2,1,0:T(8,128)S(1)} %get-tuple-element.44), channel_id=1, source_target_pairs={{16,0},{32,16},{48,32},{64,48},{80,64},{96,80},{112,96},{128,112},... | collective-permute-start | bytes 3342344 | tf_op jit(solution)/shard_map/ppermute | solution.py:385
  87.0 0.0 copy-done.8
  87.0 0.0 copy-done.9
  87.0 0.0 copy-done.10
  87.0 0.0 copy-done.11
  87.0 0.0 copy-start.1
  87.1 2.5 %copy-done.1 = f32[16,80,8,128]{3,2,1,0:T(8,128)S(1)} copy-done((f32[16,80,8,128]{3,2,1,0:T(8,128)S(1)}, f32[16,80,8,128]{3,2,1,0:T(8,128)}, u32[]{:S(2)}) %copy-start.1) | copy-done | bytes 5242904
  89.5 6.0 %newton1_inner.1 = (f32[24,176,128]{2,1,0:T(8,128)S(1)}, f32[24,176,128]{2,1,0:T(8,128)S(1)}, f32[24,176,128]{2,1,0:T(8,128)S(1)}, f32[24,176,128]{2,1,0:T(8,128...) custom-call(s32[1]{0:T(128)} %bitcast.refs_0_, ...), custom_call_target="tpu_custom_call" | custom-call | tf_op jit(solution)/shard_map/newton1_inner/pallas_call | solution.py:40
  95.6 2.2 %collective-permute-done.refs_2_ = f32[16,17,8,128]{3,2,1,0:T(8,128)S(1)} collective-permute-done((f32[16,17,8,128]{3,2,1,0:T(8,128)}, f32[16,17,8,128]{3,2,1,0:T(8,128)S(1)}, u32[]{:S(2)}, u32[]{:S(2)}) %collective-permute-start) | collective-permute-done | bytes 1114144 | tf_op jit(solution)/shard_map/ppermute | solution.py:382
  97.8 4.1 %collective-permute-done.1.refs_3_ = f32[16,17,8,128]{3,2,1,0:T(8,128)S(1)} collective-permute-done((f32[16,17,8,128]{3,2,1,0:T(8,128)S(1)}, f32[16,17,8,128]{3,2,1,0:T(8,128)S(1)}, u32[]{:S(2)}, u32[]{:S(2)}) %collective-permute-start.1) | collective-permute-done | bytes 1114144 | tf_op jit(solution)/shard_map/ppermute | solution.py:385
  101.9 3.7 %newton1_outer.1 = (f32[24,176,128]{2,1,0:T(8,128)S(1)}, f32[24,176,128]{2,1,0:T(8,128)S(1)}, f32[24,176,128]{2,1,0:T(8,128)S(1)}, f32[24,176,128]{2,1,0:T(8,128...) custom-call(s32[1]{0:T(128)} %bitcast.refs_0_, ...), custom_call_target="tpu_custom_call", output_to_operand_aliasing={{0}: (4, {}), {1}: (5, {}), {2}: (6, {}), {3}: (7, {}), {4}... | custom-call | tf_op jit(solution)/shard_map/newton1_outer/pallas_call | solution.py:40
  105.6 1.9 %collective-permute-start.2 = (f32[4,144,128]{2,1,0:T(8,128)S(1)}, f32[4,144,128]{2,1,0:T(8,128)S(1)}, u32[]{:S(2)}, u32[]{:S(2)}) collective-permute-start(f32[4,144,128]{2,1,0:T(8,128)S(1)} %get-tuple-element.57), channel_id=1, source_target_pairs={{0,16},{16,32},{32,48},{48,64},{64,80},{80,96},{96,112},{112,128},... | collective-permute-start | bytes 884744 | tf_op jit(solution)/shard_map/ppermute | solution.py:382
  107.5 2.6 %collective-permute-start.3 = (f32[4,144,128]{2,1,0:T(8,128)S(1)}, f32[4,144,128]{2,1,0:T(8,128)S(1)}, u32[]{:S(2)}, u32[]{:S(2)}) collective-permute-start(f32[4,144,128]{2,1,0:T(8,128)S(1)} %get-tuple-element.58), channel_id=1, source_target_pairs={{16,0},{32,16},{48,32},{64,48},{80,64},{96,80},{112,96},{128,112},... | collective-permute-start | bytes 884744 | tf_op jit(solution)/shard_map/ppermute | solution.py:385
  110.2 3.7 %newton2_inner.1 = (f32[24,176,128]{2,1,0:T(8,128)S(1)}, f32[24,176,128]{2,1,0:T(8,128)S(1)}, f32[24,176,128]{2,1,0:T(8,128)S(1)}, f32[24,176,128]{2,1,0:T(8,128...) custom-call(s32[1]{0:T(128)} %bitcast.refs_0_, f32[24,176,128]{2,1,0:T(8,128)S(1)} %get-tuple-element.65.refs_1_.refs_9_, ...), custom_call_target="tpu_custom_call" | custom-call | tf_op jit(solution)/shard_map/newton2_inner/pallas_call | solution.py:40
  113.8 0.0 collective-permute-done.2.refs_1_
  113.8 2.0 %collective-permute-done.3.refs_2_ = f32[4,144,128]{2,1,0:T(8,128)S(1)} collective-permute-done((f32[4,144,128]{2,1,0:T(8,128)S(1)}, f32[4,144,128]{2,1,0:T(8,128)S(1)}, u32[]{:S(2)}, u32[]{:S(2)}) %collective-permute-start.3) | collective-permute-done | bytes 294944 | tf_op jit(solution)/shard_map/ppermute | solution.py:385
  115.9 2.4 %newton2_outer.1 = (f32[24,176,128]{2,1,0:T(8,128)S(1)}, f32[24,176,128]{2,1,0:T(8,128)S(1)}, f32[24,176,128]{2,1,0:T(8,128)S(1)}, f32[24,176,128]{2,1,0:T(8,128...) custom-call(s32[1]{0:T(128)} %bitcast.refs_0_, ...), custom_call_target="tpu_custom_call", output_to_operand_aliasing={{0}: (9, {}), {1}: (10, {}), {2}: (11, {}), {3}: (12, {}), ... | custom-call | tf_op jit(solution)/shard_map/newton2_outer/pallas_call | solution.py:40
  118.3 1.9 %collective-permute-start.4 = (f32[4,144,128]{2,1,0:T(8,128)S(1)}, f32[4,144,128]{2,1,0:T(8,128)S(1)}, u32[]{:S(2)}, u32[]{:S(2)}) collective-permute-start(f32[4,144,128]{2,1,0:T(8,128)S(1)} %get-tuple-element.72), channel_id=1, source_target_pairs={{0,16},{16,32},{32,48},{48,64},{64,80},{80,96},{96,112},{112,128},... | collective-permute-start | bytes 884744 | tf_op jit(solution)/shard_map/ppermute | solution.py:382
  120.2 2.4 %collective-permute-start.5 = (f32[4,144,128]{2,1,0:T(8,128)S(1)}, f32[4,144,128]{2,1,0:T(8,128)S(1)}, u32[]{:S(2)}, u32[]{:S(2)}) collective-permute-start(f32[4,144,128]{2,1,0:T(8,128)S(1)} %get-tuple-element.73), channel_id=1, source_target_pairs={{16,0},{32,16},{48,32},{64,48},{80,64},{96,80},{112,96},{128,112},... | collective-permute-start | bytes 884744 | tf_op jit(solution)/shard_map/ppermute | solution.py:385
  122.6 3.9 %newton3_inner.1 = (f32[24,176,128]{2,1,0:T(8,128)S(1)}, f32[24,176,128]{2,1,0:T(8,128)S(1)}, f32[24,176,128]{2,1,0:T(8,128)S(1)}, f32[24,176,128]{2,1,0:T(8,128...) custom-call(s32[1]{0:T(128)} %bitcast.refs_0_, ...), custom_call_target="tpu_custom_call" | custom-call | tf_op jit(solution)/shard_map/newton3_inner/pallas_call | solution.py:40
  126.5 0.0 collective-permute-done.4.refs_1_
  126.5 2.0 %collective-permute-done.5.refs_2_ = f32[4,144,128]{2,1,0:T(8,128)S(1)} collective-permute-done((f32[4,144,128]{2,1,0:T(8,128)S(1)}, f32[4,144,128]{2,1,0:T(8,128)S(1)}, u32[]{:S(2)}, u32[]{:S(2)}) %collective-permute-start.5) | collective-permute-done | bytes 294944 | tf_op jit(solution)/shard_map/ppermute | solution.py:385
  128.5 0.0 copy-start.6
  128.5 0.0 copy-start.7
  128.5 3.6 %newton3_outer.1 = (f32[24,176,128]{2,1,0:T(8,128)S(1)}, f32[24,176,128]{2,1,0:T(8,128)S(1)}, f32[24,176,128]{2,1,0:T(8,128)S(1)}, f32[24,176,128]{2,1,0:T(8,128...) custom-call(s32[1]{0:T(128)} %bitcast.refs_0_, ...), custom_call_target="tpu_custom_call", output_to_operand_aliasing={{0}: (11, {}), {1}: (12, {}), {2}: (13, {}), {3}: (14, {}),... | custom-call | tf_op jit(solution)/shard_map/newton3_outer/pallas_call | solution.py:40
  132.1 3.9 %all-to-all-start.1 = ((f32[16,16,8,128]{3,2,1,0:T(8,128)}), f32[16,16,8,128]{3,2,1,0:T(8,128)S(1)}, u32[]{:S(2)}, u32[]{:S(2)}) async-start(f32[16,16,8,128]{3,2,1,0:T(8,128)} %get-tuple-element.82), calls=%async_computation.1 | async-start | bytes 2097152 | tf_op jit(solution)/shard_map/all_to_all | solution.py:426
  136.1 0.0 copy-done.6
  136.1 0.0 copy-done.7
  136.1 19.6 %all-gather = f32[768,128]{1,0:T(8,128)S(1)} all-gather(f32[48,128]{1,0:T(8,128)S(1)} %pad_maximum_fusion), channel_id=2, replica_groups=mesh['axial'=16,'depth'=16] {'axial'}, dimensions={0}, use_global_device_ids=true | all-gather | bytes 417792 | tf_op jit(solution)/shard_map/all_gather | solution.py:432
  155.7 1.7 %deliver.1 = f32[32,128]{1,0:T(8,128)} custom-call(s32[1]{0:T(128)} %bitcast.refs_0_, f32[16,48,128]{2,1,0:T(8,128)S(1)} %bitcast.13), custom_call_target="tpu_custom_call" | custom-call | tf_op jit(solution)/shard_map/deliver/pallas_call | solution.py:40
  157.4 0.0 all-to-all-done.1
  157.4 1.1 copy_bitcast_fusion
  (4 shorter events, 0.0 us)
Async XLA Ops:
  0.6 1.2 copy-start.2
  1.9 1.2 copy-start.3
  3.1 1.2 copy-start.4
  4.3 1.2 copy-start.5
  76.4 2.7 %copy-start = (f32[16,80,8,128]{3,2,1,0:T(8,128)}, f32[16,80,8,128]{3,2,1,0:T(8,128)S(1)}, u32[]{:S(2)}) copy-start(f32[16,80,8,128]{3,2,1,0:T(8,128)S(1)} %all_to_all.10.refs_0_.refs_2_) | copy-start | bytes 15728644
  76.4 10.6 %copy-start.8 = (f32[8]{0:T(128)S(1)}, f32[8]{0:T(128)}, u32[]{:S(2)}) copy-start(f32[8]{0:T(128)} %param.17) | copy-start | bytes 100
  76.4 10.6 %copy-start.9 = (f32[8]{0:T(128)S(1)}, f32[8]{0:T(128)}, u32[]{:S(2)}) copy-start(f32[8]{0:T(128)} %param.16) | copy-start | bytes 100
  76.4 10.6 %copy-start.10 = (f32[8]{0:T(128)S(1)}, f32[8]{0:T(128)}, u32[]{:S(2)}) copy-start(f32[8]{0:T(128)} %param.15) | copy-start | bytes 100
  76.4 10.6 %copy-start.11 = (f32[8]{0:T(128)S(1)}, f32[8]{0:T(128)}, u32[]{:S(2)}) copy-start(f32[8]{0:T(128)} %param.14) | copy-start | bytes 100
  79.1 18.7 %collective-permute-start = (f32[16,17,8,128]{3,2,1,0:T(8,128)}, f32[16,17,8,128]{3,2,1,0:T(8,128)S(1)}, u32[]{:S(2)}, u32[]{:S(2)}) collective-permute-start(f32[16,17,8,128]{3,2,1,0:T(8,128)} %get-tuple-element.43), channel_id=1, source_target_pairs={{0,16},{16,32},{32,48},{48,64},{64,80},{80,96},{96,112},{112,128},... | collective-permute-start | bytes 3342344 | tf_op jit(solution)/shard_map/ppermute | solution.py:382
  85.1 16.8 %collective-permute-start.1 = (f32[16,17,8,128]{3,2,1,0:T(8,128)S(1)}, f32[16,17,8,128]{3,2,1,0:T(8,128)S(1)}, u32[]{:S(2)}, u32[]{:S(2)}) collective-permute-start(f32[16,17,8,128]{3,2,1,0:T(8,128)S(1)} %get-tuple-element.44), channel_id=1, source_target_pairs={{16,0},{32,16},{48,32},{64,48},{80,64},{96,80},{112,96},{128,112},... | collective-permute-start | bytes 3342344 | tf_op jit(solution)/shard_map/ppermute | solution.py:385
  87.0 2.5 %copy-start.1 = (f32[16,80,8,128]{3,2,1,0:T(8,128)S(1)}, f32[16,80,8,128]{3,2,1,0:T(8,128)}, u32[]{:S(2)}) copy-start(f32[16,80,8,128]{3,2,1,0:T(8,128)} %copy-done) | copy-start | bytes 15728644
  105.6 8.2 %collective-permute-start.2 = (f32[4,144,128]{2,1,0:T(8,128)S(1)}, f32[4,144,128]{2,1,0:T(8,128)S(1)}, u32[]{:S(2)}, u32[]{:S(2)}) collective-permute-start(f32[4,144,128]{2,1,0:T(8,128)S(1)} %get-tuple-element.57), channel_id=1, source_target_pairs={{0,16},{16,32},{32,48},{48,64},{64,80},{80,96},{96,112},{112,128},... | collective-permute-start | bytes 884744 | tf_op jit(solution)/shard_map/ppermute | solution.py:382
  107.5 8.3 %collective-permute-start.3 = (f32[4,144,128]{2,1,0:T(8,128)S(1)}, f32[4,144,128]{2,1,0:T(8,128)S(1)}, u32[]{:S(2)}, u32[]{:S(2)}) collective-permute-start(f32[4,144,128]{2,1,0:T(8,128)S(1)} %get-tuple-element.58), channel_id=1, source_target_pairs={{16,0},{32,16},{48,32},{64,48},{80,64},{96,80},{112,96},{128,112},... | collective-permute-start | bytes 884744 | tf_op jit(solution)/shard_map/ppermute | solution.py:385
  118.3 8.3 %collective-permute-start.4 = (f32[4,144,128]{2,1,0:T(8,128)S(1)}, f32[4,144,128]{2,1,0:T(8,128)S(1)}, u32[]{:S(2)}, u32[]{:S(2)}) collective-permute-start(f32[4,144,128]{2,1,0:T(8,128)S(1)} %get-tuple-element.72), channel_id=1, source_target_pairs={{0,16},{16,32},{32,48},{48,64},{64,80},{80,96},{96,112},{112,128},... | collective-permute-start | bytes 884744 | tf_op jit(solution)/shard_map/ppermute | solution.py:382
  120.2 8.3 %collective-permute-start.5 = (f32[4,144,128]{2,1,0:T(8,128)S(1)}, f32[4,144,128]{2,1,0:T(8,128)S(1)}, u32[]{:S(2)}, u32[]{:S(2)}) collective-permute-start(f32[4,144,128]{2,1,0:T(8,128)S(1)} %get-tuple-element.73), channel_id=1, source_target_pairs={{16,0},{32,16},{48,32},{64,48},{80,64},{96,80},{112,96},{128,112},... | collective-permute-start | bytes 884744 | tf_op jit(solution)/shard_map/ppermute | solution.py:385
  128.5 7.5 %copy-start.6 = (s32[16,128]{1,0:T(8,128)S(1)}, s32[16,128]{1,0:T(8,128)}, u32[]{:S(2)}) copy-start(s32[16,128]{1,0:T(8,128)} %param.19) | copy-start | bytes 24580
  128.5 7.6 %copy-start.7 = (s32[16,128]{1,0:T(8,128)S(1)}, s32[16,128]{1,0:T(8,128)}, u32[]{:S(2)}) copy-start(s32[16,128]{1,0:T(8,128)} %param.18) | copy-start | bytes 24580
  132.1 25.3 %all-to-all-start.1 = ((f32[16,16,8,128]{3,2,1,0:T(8,128)}), f32[16,16,8,128]{3,2,1,0:T(8,128)S(1)}, u32[]{:S(2)}, u32[]{:S(2)}) async-start(f32[16,16,8,128]{3,2,1,0:T(8,128)} %get-tuple-element.82), calls=%async_computation.1 | async-start | bytes 2097152 | tf_op jit(solution)/shard_map/all_to_all | solution.py:426

commit v3 on v2

--- a/solution.py
+++ b/solution.py
@@ -10,13 +10,11 @@
 SWEEPS = 4
 H = 4
 W = 16
-PAD = 8
 LANES = 128
-WIDE = (PAD, PAD + 2 * W + LANES)
-NEAR = (PAD + W // 2, PAD + W + LANES + W // 2)
-CORE = (PAD + W, PAD + W + LANES)
-FULL = WIDE[1] + PAD
-VMEM_LIMIT = 12 * 1024 * 1024
+FULL = 2 * W + LANES
+WIDE = (0, FULL)
+NEAR = (W // 2, FULL - W // 2)
+CORE = (W, W + LANES)
 
 VM = pl.BlockSpec(memory_space=pltpu.VMEM)
 SM = pl.BlockSpec(memory_space=pltpu.SMEM)
@@ -26,7 +24,7 @@
     return jax.ShapeDtypeStruct(shape, jnp.float32)
 
 
-def call(kernel, name, scalars, reads, updates, makes, scratch=(), kept=True, space=pltpu.VMEM):
+def call(kernel, name, scalars, reads, updates, makes, scratch=(), kept=True, space=pltpu.VMEM, out_space=pltpu.VMEM, limit=8):
     counts = [len(scalars), len(reads), len(updates), len(updates), len(makes), len(scratch)]
 
     def body(*refs):
@@ -40,14 +38,14 @@
     results = pl.pallas_call(
         body,
         out_shape=[pltpu.VMEM(u.shape, jnp.float32) for u in updates]
-        + [pltpu.VMEM(s, jnp.float32) if kept else f32(*s) for s in makes],
+        + [out_space(s, jnp.float32) if kept else f32(*s) for s in makes],
         in_specs=[SM] * len(scalars)
         + [pl.BlockSpec(memory_space=space)] * len(reads)
         + [VM] * len(updates),
-        out_specs=[VM] * (len(updates) + len(makes)),
+        out_specs=[VM] * len(updates) + [pl.BlockSpec(memory_space=out_space)] * len(makes),
         input_output_aliases={first + i: i for i in range(len(updates))},
         scratch_shapes=list(scratch),
-        compiler_params=pltpu.CompilerParams(vmem_limit_bytes=VMEM_LIMIT),
+        compiler_params=pltpu.CompilerParams(vmem_limit_bytes=limit * 1024 * 1024),
         name=name,
     )(*scalars, *reads, *updates)
     return list(results)
@@ -71,64 +69,68 @@
             body(r)
 
 
-def pack_kernel(scalars, ins, updates, makes, scratch):
-    (out,), held, sems = makes, scratch[:-1], scratch[-1]
+def rim_rows(kind):
+    return H if kind in (0, 4) else H - 1
+
+
+def planes(first, own):
+    if first:
+        low = [(k, r) for k in range(5) for r in range(rim_rows(k))]
+        high = [(k, r) for k in range(5) for r in range(own - rim_rows(k), own)]
+        return low + high
+    return [(k, r) for k in range(5) for r in range(rim_rows(k), own - rim_rows(k))]
+
+
+def pack_kernel(first, scalars, ins, updates, makes, scratch):
+    (result,), held, out, sems, out_sems = makes, scratch[:4], scratch[4], scratch[5], scratch[6]
     slices = out.shape[0]
     own = ins[0].shape[0]
     lane = lane_iota(8)
-    copies = [pltpu.make_async_copy(x, y, sems.at[i]) for i, (x, y) in enumerate(zip(ins, held))]
+    bands = [slice(0, H), slice(own - H, own)] if first else [slice(H - 1, own - H + 1)]
+    copies = [
+        pltpu.make_async_copy(x.at[band], y.at[band], sems.at[i, j])
+        for i, (x, y) in enumerate(zip(ins, held))
+        for j, band in enumerate(bands)
+    ]
     for copy in copies:
         copy.start()
-
-    def spread(i):
-        def row(a, _):
+    for copy in copies:
+        copy.wait()
+
+    def tile(k, a, s):
+        return held[k][a, :, LANES * s : LANES * (s + 1)].astype(jnp.float32)
+
+    order = planes(first, own)
+    sent = []
+    for p, (kind, a) in enumerate(order):
+        if kind < 4:
             for s in range(slices):
-                out[s, i * own + a] = held[i][a, :, LANES * s : LANES * (s + 1)].astype(jnp.float32)
-            return 0
-
-        return row
-
-    for i, copy in enumerate(copies):
+                out[s, p] = tile(kind, a, s)
+        else:
+            turned = [
+                [pltpu.roll(tile(k, a, s), (2 * W * k + W) % LANES, 1) for s in range(slices)] for k in range(4)
+            ]
+            for s in range(slices):
+                value = turned[0][s - 1]
+                for k in range(4):
+                    if k:
+                        value = jnp.where(lane >= 2 * W * k, turned[k][s - 1], value)
+                    value = jnp.where(lane >= 2 * W * k + W, turned[k][(s + 1) % slices], value)
+                out[s, p] = value
+        if p + 1 == len(order) or order[p + 1][0] != kind:
+            begin = sent[-1][1] if sent else 0
+            band = slice(begin, p + 1)
+            sent.append((pltpu.make_async_copy(out.at[:, band], result.at[:, band], out_sems.at[len(sent)]), p + 1))
+            sent[-1][0].start()
+    for copy, _ in sent:
         copy.wait()
-        lax.fori_loop(0, own, spread(i), 0, unroll=4)
-
-    def rims(a, _):
-        turned = [
-            [
-                pltpu.roll(
-                    x[a, :, LANES * s : LANES * (s + 1)].astype(jnp.float32), (2 * W * i + W) % LANES, 1
-                )
-                for s in range(slices)
-            ]
-            for i, x in enumerate(held)
-        ]
-        for s in range(slices):
-            result = turned[0][s - 1]
-            for i in range(len(ins)):
-                if i:
-                    result = jnp.where(lane >= 2 * W * i, turned[i][s - 1], result)
-                result = jnp.where(lane >= 2 * W * i + W, turned[i][(s + 1) % slices], result)
-            out[s, len(ins) * own + a] = result
-        return 0
-
-    lax.fori_loop(0, own, rims, 0)
-
-
-def rim_rows(kind):
-    return H if kind in (0, 4) else H - 1
-
-
-def rim_start(kind):
-    return sum(rim_rows(k) for k in range(kind))
 
 
 def rims_kernel(scalars, reads, updates, makes, scratch):
     (arrived,), (top, bottom) = reads, makes
-    own = arrived.shape[1] // 5
-    for kind in range(5):
-        count, at = rim_rows(kind), rim_start(kind)
-        bottom[:, at : at + count] = arrived[:, kind * own : kind * own + count]
-        top[:, at : at + count] = arrived[:, (kind + 1) * own - count : (kind + 1) * own]
+    count = top.shape[1]
+    bottom[...] = arrived[:, :count]
+    top[...] = arrived[:, count:]
 
 
 def suffix_matrix(m_ref):
@@ -136,6 +138,14 @@
     source = lax.broadcasted_iota(jnp.int32, (rows, cols), 0) & (LANES - 1)
     target = lax.broadcasted_iota(jnp.int32, (rows, cols), 1)
     m_ref[...] = jnp.where(source > target, 4.0 / LANES, 0.0).astype(jnp.bfloat16)
+
+
+def azimuth_pair(ref, r, span):
+    lo, hi = span
+    if span == WIDE:
+        x = ref[r]
+        return pltpu.roll(x, 1, 0) + pltpu.roll(x, FULL - 1, 0)
+    return ref[r, lo - 1 : hi - 1] + ref[r, lo + 1 : hi + 1]
 
 
 def linearise(r, row, total_rows, span, t, t0, fields, m_ref):
@@ -152,7 +162,7 @@
     cap = capacity[r, lo:hi]
     deeper = jnp.where(lane == LANES - 1, 0.0, pltpu.roll(tc, LANES - 1, 1))
     shallower = jnp.where(lane == 0, 0.0, pltpu.roll(tc, 1, 1))
-    pairs = t[r - 1, lo:hi] + t[r + 1, lo:hi] + t[r, lo - 1 : hi - 1] + t[r, lo + 1 : hi + 1]
+    pairs = t[r - 1, lo:hi] + t[r + 1, lo:hi] + azimuth_pair(t, r, span)
     spread = pairs + 2.0 * (deeper + shallower) - 8.0 * tc
     source = c * spread - 0.5 * p - gas * (tc - deeper)
     if t0 is not None:
@@ -170,7 +180,7 @@
 
     def swept(src, r):
         u = src[r, lo:hi]
-        pairs = src[r - 1, lo:hi] + src[r + 1, lo:hi] + src[r, lo - 1 : hi - 1] + src[r, lo + 1 : hi + 1]
+        pairs = src[r - 1, lo:hi] + src[r + 1, lo:hi] + azimuth_pair(src, r, span)
         shallower = jnp.where(lane == 0, 0.0, pltpu.roll(u, 1, 1))
         deeper = pltpu.roll(u, LANES - 1, 1)
         return first[r, lo:hi] + side[r, lo:hi] * (pairs + 2.0 * shallower) + down[r, lo:hi] * deeper
@@ -199,19 +209,19 @@
     return x.reshape(x.shape[0] * x.shape[1], LANES).T
 
 
-def unpack_row(tables, arrived, at, r, state):
+def unpack_row(tables, source, r, state):
     t0, conduct, capacity, act, pre, dep = state
     lo, hi = WIDE
-    edges = from_cells(arrived, at[4])
+    edges = from_cells(*source(4))
 
     def whole(kind):
         e = 2 * W * kind
         return jnp.concatenate(
-            [edges[e : e + W], from_cells(arrived, at[kind]), edges[e + W : e + 2 * W]], axis=0
+            [edges[e : e + W], from_cells(*source(kind)), edges[e + W : e + 2 * W]], axis=0
         )
 
     t0[r, lo:hi] = whole(0)
-    if at[1] is None:
+    if source(1) is None:
         return
     label = whole(1)
     fields = [jnp.full(label.shape, tables[f, 0], jnp.float32) for f in range(4)]
@@ -240,38 +250,61 @@
     return finish
 
 
-def first_kernel(outer, total_rows, scalars, reads, updates, makes, scratch):
+def first_kernel(total_rows, scalars, reads, updates, makes, scratch):
     place, tables = scalars
-    arrays, rims = (updates, makes) if outer else (makes, None)
-    state, (ua, cs, cd, ub, uc, t_new) = arrays[:6], arrays[6:]
+    state, ub, rims = makes[:6], makes[6], makes[7:]
+    matrix, held, (ua, cs, cd, uc), sems = scratch[0], scratch[1:5], scratch[5:9], scratch[9]
     t0, conduct, capacity, act, pre, dep = state
+    work = ua, cs, cd, ub, uc
     rows = t0.shape[0]
     own = rows - 2 * H
-    suffix_matrix(scratch[0])
-    if outer:
-        for i in range(H):
-            for ref, r, missing in ((reads[0], i, i == 0), (reads[1], i + H + own, i == H - 1)):
-                skip = H if ref is reads[0] else 0
-                at = [rim_start(k) + (i - (H - rim_rows(k)) if skip else i) for k in range(5)]
-                if missing:
-                    at[1:4] = [None] * 3
-                unpack_row(tables, ref, at, r, state)
-    else:
-        for i in range(own):
-            unpack_row(tables, reads[0], [k * own + i for k in range(5)], i + H, state)
+    copies = [pltpu.make_async_copy(x, y, sems.at[i]) for i, (x, y) in enumerate(zip(reads, held))]
+    for copy in copies:
+        copy.start()
+    suffix_matrix(matrix)
+    tables_of = [{plane: i for i, plane in enumerate(planes(first, own))} for first in (True, False)]
+    rim_planes = len(tables_of[0]) // 2
+
+    def own_plane(r):
+        def source(kind):
+            for ref, table in zip(held, tables_of):
+                if (kind, r) in table:
+                    return ref, table[kind, r]
+
+        return source
+
+    def halo_plane(r):
+        low = tables_of[0]
+
+        def source(kind):
+            if r < 0:
+                at = low.get((kind, r + own))
+                return None if at is None else (held[2], at - rim_planes)
+            return (held[3], low[kind, r - own]) if (kind, r - own) in low else None
+
+        return source
+
+    copies[0].wait()
+    copies[1].wait()
+    for r in range(own):
+        unpack_row(tables, own_plane(r), r + H, state)
+    copies[2].wait()
+    copies[3].wait()
+    for r in range(H):
+        unpack_row(tables, halo_plane(r - H), r, state)
+        unpack_row(tables, halo_plane(own + r), own + r + H, state)
     lo, hi = WIDE
 
     def one(r):
         source, inverse, side, down = linearise(
-            r, place[0] * own + r - H, total_rows, WIDE, t0, None, (conduct, capacity, act, pre), scratch[0]
+            r, place[0] * own + r - H, total_rows, WIDE, t0, None, (conduct, capacity, act, pre), matrix
         )
         ua[r, lo:hi] = (source + dep[r, lo:hi]) * inverse
         cs[r, lo:hi] = side
         cd[r, lo:hi] = down
 
-    ranges = outer_rows if outer else inner_rows
-    over(ranges(rows, 1), one)
-    sweeps(WIDE, (ua, cs, cd, ub, uc), [ranges(rows, k) for k in (2, 3, 4)], keeper(WIDE, t0, t_new, rims))
+    over([(1, rows - 1)], one)
+    sweeps(WIDE, work, [[(k, rows - k)] for k in (2, 3, 4)], keeper(WIDE, t0, ub, rims))
 
 
 def later_kernel(outer, last, total_rows, scalars, reads, updates, makes, scratch):
@@ -279,12 +312,12 @@
     lo, hi = NEAR
     if outer:
         above, below, t0, conduct, capacity, act, pre, dep = reads[:8]
-        t, ua, cs, cd, ub, uc = updates[:6]
-        results, rims = (makes, None) if last else (updates[6:], makes)
+        t, ua, cs, cd, ub, uc = updates
+        rims = None if last else makes
     else:
         t, t0, conduct, capacity, act, pre, dep = reads
         ua, cs, cd, ub, uc = makes[:5]
-        results, rims = makes[5:], None
+        rims = None
     rows = t0.shape[0]
     own = rows - 2 * H
     suffix_matrix(scratch[0])
@@ -301,7 +334,7 @@
         cd[r, lo:hi] = down
 
     if last:
-        out, blowing = results
+        out, blowing = makes[-2:]
         if outer:
             out[...], blowing[...] = reads[8][...], reads[9][...]
         core = slice(*CORE)
@@ -314,7 +347,7 @@
             blowing[r - H : r - H + 1, :] = jnp.sum(p.T, axis=0, keepdims=True) * (1.0 / LANES)
 
     else:
-        finish = keeper(NEAR, t, results[0], rims)
+        finish = keeper(NEAR, t, ub, rims)
     ranges = outer_rows if outer else inner_rows
     over(ranges(rows, 1), one)
     sweeps(NEAR, (ua, cs, cd, ub, uc), [ranges(rows, k) for k in (2, 3, 4)], finish)
@@ -385,42 +418,50 @@
         return lax.ppermute(x, "axial", [(i + 1, i) for i in range(n_axial - 1)])
 
     cells = [kelvin_before_step, material_label, unburnt_resin_share, deposited_energy_amount]
-    (sent,) = call(
-        pack_kernel, "pack", [], cells, [], [(n_depth, 5 * own, layers, LANES)],
-        [pltpu.VMEM(x.shape, x.dtype) for x in cells] + [pltpu.SemaphoreType.DMA((4,))],
-        kept=False, space=pltpu.HBM,
-    )
-    arrived = lax.all_to_all(sent, "depth", 0, 0)
-    top, bottom = call(
-        rims_kernel, "rims", [], [arrived], [], [(n_depth, rim_start(5), layers, LANES)] * 2
-    )
-    above, below = up(top), down(bottom)
-    arrays = call(
-        functools.partial(first_kernel, False, total_rows), "newton1_inner",
-        [place, tables], [arrived], [], [extended] * 12, matrix,
-    )
+    cells = [kelvin_before_step, material_label, unburnt_resin_share, deposited_energy_amount]
+    cells = [pltpu.with_memory_space_constraint(x, pltpu.HBM) for x in cells]
+
+    def sent(first):
+        return call(
+            functools.partial(pack_kernel, first), "pack1" if first else "pack2", [], cells, [],
+            [(n_depth, len(planes(first, own)), layers, LANES)],
+            [pltpu.VMEM(x.shape, x.dtype) for x in cells]
+            + [pltpu.VMEM((n_depth, len(planes(first, own)), layers, LANES), jnp.float32)]
+            + [pltpu.SemaphoreType.DMA((4, 2)), pltpu.SemaphoreType.DMA((10,))],
+            space=pltpu.HBM, out_space=pltpu.HBM,
+        )[0]
+
+    arrived = [lax.all_to_all(sent(first), "depth", 0, 0) for first in (True, False)]
+    rims = (n_depth, len(planes(True, own)) // 2, layers, LANES)
+    top, bottom = call(rims_kernel, "rims", [], arrived[:1], [], [rims] * 2, kept=False)
+    came = [*arrived, up(top), down(bottom)]
     *arrays, top, bottom = call(
-        functools.partial(first_kernel, True, total_rows), "newton1_outer",
-        [place, tables], [above, below], arrays, [rim] * 2, matrix,
+        functools.partial(first_kernel, total_rows), "newton1",
+        [place, tables], [pltpu.with_memory_space_constraint(x, pltpu.HBM) for x in came], [],
+        [extended] * 7 + [rim] * 2,
+        matrix
+        + [pltpu.VMEM(x.shape, jnp.float32) for x in came]
+        + [pltpu.VMEM(extended, jnp.float32)] * 4
+        + [pltpu.SemaphoreType.DMA((4,))],
+        space=pltpu.HBM, limit=20,
     )
     t0, conduct, capacity, act, pre, dep = arrays[:6]
-    t = arrays[-1]
+    t = arrays[6]
     for last in (False, True):
         above, below = up(top), down(bottom)
         fixed = [t0, conduct, capacity, act, pre, dep]
-        results = [(n_depth, own, layers, LANES), (own, LANES)] if last else [extended]
+        results = [(n_depth, own, layers, LANES), (own, LANES)] if last else []
         work = call(
             functools.partial(later_kernel, False, last, total_rows), "newton3_inner" if last else "newton2_inner",
             [place], [t] + fixed, [], [extended] * 5 + results, matrix,
         )
-        work, results = work[:5], work[5:]
         work = call(
             functools.partial(later_kernel, True, last, total_rows), "newton3_outer" if last else "newton2_outer",
-            [place], [above, below] + fixed + (results if last else []), [t] + work + ([] if last else results),
-            [(n_depth, own, layers, LANES), (own, LANES)] if last else [rim] * 2, matrix, kept=not last,
+            [place], [above, below] + fixed + work[5:], [t] + work[:5], results if last else [rim] * 2, matrix,
+            kept=not last,
         )
         if not last:
-            t, top, bottom = work[6:]
+            t, top, bottom = work[4], *work[6:]
     kelvin, blowing = work[6:]
 
     kelvin = lax.all_to_all(kelvin, "depth", 0, 0)

time: 159 us -> 154 us (0.969)
  blocking collectives: 87.6 us -> 19.4 us
  waiting for transfers between devices: 10.3 us -> 55.7 us
  starting transfers between devices: 20.6 us -> 42.9 us
  local copies, waits for them, and re-layouts: 9.99 us -> 2.54 us
  Pallas kernels: 29.1 us -> 32.4 us
    all_to_all x1 -> x0, blocking collectives: 68 us -> none  [shards(): arrived = lax.all_to_all(sent, 'depth', 0, 0)]
    all_to_all x0 -> x2, waiting for transfers between devices: none -> 50.3 us  [shards(): lax.all_to_all(sent(first), 'depth', 0, 0)]
    all_to_all x0 -> x2, starting transfers between devices: none -> 12.1 us  [shards(): lax.all_to_all(sent(first), 'depth', 0, 0)]
    ppermute x3, starting transfers between devices: 9.77 us -> 18.8 us  [up(): return lax.ppermute(x, 'axial', [(i, i + 1) for i in range(n_axial - 1)])]
    unnamed x24 -> x18, local copies, waits for them, and re-layouts: 8.91 us -> 1.46 us
    pallas_call x9, Pallas kernels: 29.1 us -> 32.4 us  [call(): pl.pallas_call(body, out_shape=[pltpu.VMEM(u.shape, jnp.float32) for u in...]
    ppermute x3, waiting for transfers between devices: 8.1 us -> 5.42 us  [down(): return lax.ppermute(x, 'axial', [(i + 1, i) for i in range(n_axial - 1)])]
    ppermute x3, waiting for transfers between devices: 2.24 us -> 0.01 us  [up(): return lax.ppermute(x, 'axial', [(i, i + 1) for i in range(n_axial - 1)])]
  transfers between devices with their start and end apart: 7 -> 9, of which waited for: 4 -> 4; matrix products, arithmetic and copies ran while one was open for 0% -> 0% of each run, Pallas kernels for 10% -> 8%
where the time goes in v3:
time: 154 us
  waiting for transfers between devices  55.7 us (36%)
  starting transfers between devices  42.9 us (28%)
  Pallas kernels  32.4 us (21%)
  blocking collectives  19.4 us (13%)
  local copies, waits for them, and re-layouts  2.54 us (2%)
    all_to_all x2, waiting for transfers between devices, shards(): lax.all_to_all(sent(first), 'depth', 0, 0)  50.3 us
    pallas_call x9, Pallas kernels, call(): pl.pallas_call(body, out_shape=[pltpu.VMEM(u.shape, jnp.float32) for u in...  32.4 us
    all_gather x1, blocking collectives, shards(): gathered = lax.all_gather(faces, 'axial')  19.4 us
    ppermute x3, starting transfers between devices, up(): return lax.ppermute(x, 'axial', [(i, i + 1) for i in range(n_axial - 1)])  18.8 us
    all_to_all x2, starting transfers between devices, shards(): lax.all_to_all(sent(first), 'depth', 0, 0)  12.1 us
    ppermute x3, starting transfers between devices, down(): return lax.ppermute(x, 'axial', [(i + 1, i) for i in range(n_axial - 1)])  6.44 us
    all_to_all x1, starting transfers between devices, shards(): kelvin = lax.all_to_all(kelvin, 'depth', 0, 0)  5.52 us
    ppermute x3, waiting for transfers between devices, down(): return lax.ppermute(x, 'axial', [(i + 1, i) for i in range(n_axial - 1)])  5.42 us
  transfers between devices with their start and end apart: 9, of which 4 were waited for; matrix products, arithmetic and copies ran while one was open for 0% of the time, Pallas kernels for 8%

profile of v3, /device:TPU:1, one launch (start us, length us, event | category | flops | bytes accessed | tf_op | source)
XLA Modules:
  0.0 153.8 jit_solution(12169942094803078203)
XLA Ops:
  0.6 3.1 %pack1.1 = f32[16,34,8,128]{3,2,1,0:T(8,128)} custom-call(f32[16,8,2048]{2,1,0:T(8,128)} %refs_0_.3, s32[16,8,2048]{2,1,0:T(8,128)} %refs_1_.3, f32[16,8,2048]{2,1,0:T(8,128)} %refs_2_.3, f32[16,8,2048]{2,1,0:T(8,128)} %refs_3_.3), custom_call_target="tpu_custom_call" | custom-call | tf_op jit(solution)/shard_map/pack1/pallas_call | solution.py:38
  3.8 7.6 %all-to-all-start = ((f32[16,34,8,128]{3,2,1,0:T(8,128)}), f32[16,34,8,128]{3,2,1,0:T(8,128)S(1)}, u32[]{:S(2)}, u32[]{:S(2)}) async-start(f32[16,34,8,128]{3,2,1,0:T(8,128)} %pack1.1), calls=%async_computation | async-start | bytes 4456448 | tf_op jit(solution)/shard_map/all_to_all | solution.py:434
  11.4 3.5 %pack2.1 = f32[16,46,8,128]{3,2,1,0:T(8,128)} custom-call(f32[16,8,2048]{2,1,0:T(8,128)} %refs_0_.3, s32[16,8,2048]{2,1,0:T(8,128)} %refs_1_.3, f32[16,8,2048]{2,1,0:T(8,128)} %refs_2_.3, f32[16,8,2048]{2,1,0:T(8,128)} %refs_3_.3), custom_call_target="tpu_custom_call" | custom-call | tf_op jit(solution)/shard_map/pack2/pallas_call | solution.py:38
  14.9 26.1 %all-to-all-done.refs_0_.refs_2_ = f32[16,34,8,128]{3,2,1,0:T(8,128)S(1)} async-done(((f32[16,34,8,128]{3,2,1,0:T(8,128)}), f32[16,34,8,128]{3,2,1,0:T(8,128)S(1)}, u32[]{:S(2)}, u32[]{:S(2)}) %all-to-all-start) | async-done | bytes 2228256 | tf_op jit(solution)/shard_map/all_to_all | solution.py:434
  41.0 0.0 copy-start
  41.0 4.5 %all-to-all-start.1 = ((f32[16,46,8,128]{3,2,1,0:T(8,128)}), f32[16,46,8,128]{3,2,1,0:T(8,128)}, u32[]{:S(2)}, u32[]{:S(2)}) async-start(f32[16,46,8,128]{3,2,1,0:T(8,128)} %pack2.1), calls=%async_computation.1 | async-start | bytes 6029312 | tf_op jit(solution)/shard_map/all_to_all | solution.py:434
  45.5 0.0 copy-done
  45.5 0.0 copy-start.5
  45.5 0.0 copy-start.6
  45.5 0.0 copy-start.7
  45.5 0.0 copy-start.8
  45.5 1.2 rims.1
  46.8 6.8 %collective-permute-start = (f32[16,17,8,128]{3,2,1,0:T(8,128)}, f32[16,17,8,128]{3,2,1,0:T(8,128)S(1)}, u32[]{:S(2)}, u32[]{:S(2)}) collective-permute-start(f32[16,17,8,128]{3,2,1,0:T(8,128)} %get-tuple-element.30), channel_id=1, source_target_pairs={{0,16},{16,32},{32,48},{48,64},{64,80},{80,96},{96,112},{112,128},... | collective-permute-start | bytes 3342344 | tf_op jit(solution)/shard_map/ppermute | solution.py:415
  53.5 1.9 %collective-permute-start.1 = (f32[16,17,8,128]{3,2,1,0:T(8,128)S(1)}, f32[16,17,8,128]{3,2,1,0:T(8,128)S(1)}, u32[]{:S(2)}, u32[]{:S(2)}) collective-permute-start(f32[16,17,8,128]{3,2,1,0:T(8,128)S(1)} %get-tuple-element.31), channel_id=1, source_target_pairs={{16,0},{32,16},{48,32},{64,48},{80,64},{96,80},{112,96},{128,112},... | collective-permute-start | bytes 3342344 | tf_op jit(solution)/shard_map/ppermute | solution.py:418
  55.5 0.0 copy-done.5
  55.5 0.0 copy-done.6
  55.5 0.0 copy-done.7
  55.5 0.0 copy-done.8
  55.5 24.2 %all-to-all-done.1.refs_3_ = f32[16,46,8,128]{3,2,1,0:T(8,128)} async-done(((f32[16,46,8,128]{3,2,1,0:T(8,128)}), f32[16,46,8,128]{3,2,1,0:T(8,128)}, u32[]{:S(2)}, u32[]{:S(2)}) %all-to-all-start.1) | async-done | bytes 3014688 | tf_op jit(solution)/shard_map/all_to_all | solution.py:434
  79.8 0.0 collective-permute-done.refs_4_
  79.8 0.0 copy-start.1
  79.8 0.0 collective-permute-done.1.refs_5_
  79.8 0.0 copy-start.2
  79.8 1.0 copy-done.1
  80.8 0.4 copy-done.2
  81.2 11.2 %newton1.1 = (f32[24,160,128]{2,1,0:T(8,128)S(1)}, f32[24,160,128]{2,1,0:T(8,128)S(1)}, f32[24,160,128]{2,1,0:T(8,128)S(1)}, f32[24,160,128]{2,1,0:T(8,128)S(1)}...) custom-call(s32[1]{0:T(128)} %bitcast.refs_0_, ...), custom_call_target="tpu_custom_call" | custom-call | tf_op jit(solution)/shard_map/newton1/pallas_call | solution.py:38
  92.4 10.1 %collective-permute-start.2 = (f32[4,144,128]{2,1,0:T(8,128)S(1)}, f32[4,144,128]{2,1,0:T(8,128)S(1)}, u32[]{:S(2)}, u32[]{:S(2)}) collective-permute-start(f32[4,144,128]{2,1,0:T(8,128)S(1)} %get-tuple-element.32), channel_id=1, source_target_pairs={{0,16},{16,32},{32,48},{48,64},{64,80},{80,96},{96,112},{112,128},... | collective-permute-start | bytes 884744 | tf_op jit(solution)/shard_map/ppermute | solution.py:415
  102.5 2.1 %collective-permute-start.3 = (f32[4,144,128]{2,1,0:T(8,128)S(1)}, f32[4,144,128]{2,1,0:T(8,128)S(1)}, u32[]{:S(2)}, u32[]{:S(2)}) collective-permute-start(f32[4,144,128]{2,1,0:T(8,128)S(1)} %get-tuple-element.33), channel_id=1, source_target_pairs={{16,0},{32,16},{48,32},{64,48},{80,64},{96,80},{112,96},{128,112},... | collective-permute-start | bytes 884744 | tf_op jit(solution)/shard_map/ppermute | solution.py:418
  104.6 3.1 %newton2_inner.1 = (f32[24,160,128]{2,1,0:T(8,128)S(1)}, f32[24,160,128]{2,1,0:T(8,128)S(1)}, f32[24,160,128]{2,1,0:T(8,128)S(1)}, f32[24,160,128]{2,1,0:T(8,128)S(1)}, f32[24,160,128]{2,1,0:T(8,128)S(1)}) custom-call(s32[1]{0:T(128)} %bitcast.refs_0_, f32[24,160,128]{2,1,0:T(8,128)S(1)} %get-tuple-element.40.refs_1_.refs_9_, ...), custom_call_target="tpu_custom_call" | custom-call | tf_op jit(solution)/shard_map/newton2_inner/pallas_call | solution.py:38
  107.7 0.0 collective-permute-done.2.refs_1_
  107.7 2.8 %collective-permute-done.3.refs_2_ = f32[4,144,128]{2,1,0:T(8,128)S(1)} collective-permute-done((f32[4,144,128]{2,1,0:T(8,128)S(1)}, f32[4,144,128]{2,1,0:T(8,128)S(1)}, u32[]{:S(2)}, u32[]{:S(2)}) %collective-permute-start.3) | collective-permute-done | bytes 294944 | tf_op jit(solution)/shard_map/ppermute | solution.py:418
  110.6 2.0 %newton2_outer.1 = (f32[24,160,128]{2,1,0:T(8,128)S(1)}, f32[24,160,128]{2,1,0:T(8,128)S(1)}, f32[24,160,128]{2,1,0:T(8,128)S(1)}, f32[24,160,128]{2,1,0:T(8,128...) custom-call(s32[1]{0:T(128)} %bitcast.refs_0_, ...), custom_call_target="tpu_custom_call", output_to_operand_aliasing={{0}: (9, {}), {1}: (10, {}), {2}: (11, {}), {3}: (12, {}), ... | custom-call | tf_op jit(solution)/shard_map/newton2_outer/pallas_call | solution.py:38
  112.6 1.9 %collective-permute-start.4 = (f32[4,144,128]{2,1,0:T(8,128)S(1)}, f32[4,144,128]{2,1,0:T(8,128)S(1)}, u32[]{:S(2)}, u32[]{:S(2)}) collective-permute-start(f32[4,144,128]{2,1,0:T(8,128)S(1)} %get-tuple-element.46), channel_id=1, source_target_pairs={{0,16},{16,32},{32,48},{48,64},{64,80},{80,96},{96,112},{112,128},... | collective-permute-start | bytes 884744 | tf_op jit(solution)/shard_map/ppermute | solution.py:415
  114.5 2.4 %collective-permute-start.5 = (f32[4,144,128]{2,1,0:T(8,128)S(1)}, f32[4,144,128]{2,1,0:T(8,128)S(1)}, u32[]{:S(2)}, u32[]{:S(2)}) collective-permute-start(f32[4,144,128]{2,1,0:T(8,128)S(1)} %get-tuple-element.47), channel_id=1, source_target_pairs={{16,0},{32,16},{48,32},{64,48},{80,64},{96,80},{112,96},{128,112},... | collective-permute-start | bytes 884744 | tf_op jit(solution)/shard_map/ppermute | solution.py:418
  116.9 3.3 %newton3_inner.1 = (f32[24,160,128]{2,1,0:T(8,128)S(1)}, f32[24,160,128]{2,1,0:T(8,128)S(1)}, f32[24,160,128]{2,1,0:T(8,128)S(1)}, f32[24,160,128]{2,1,0:T(8,128...) custom-call(s32[1]{0:T(128)} %bitcast.refs_0_, ...), custom_call_target="tpu_custom_call" | custom-call | tf_op jit(solution)/shard_map/newton3_inner/pallas_call | solution.py:38
  120.2 0.0 collective-permute-done.4.refs_1_
  120.3 2.6 %collective-permute-done.5.refs_2_ = f32[4,144,128]{2,1,0:T(8,128)S(1)} collective-permute-done((f32[4,144,128]{2,1,0:T(8,128)S(1)}, f32[4,144,128]{2,1,0:T(8,128)S(1)}, u32[]{:S(2)}, u32[]{:S(2)}) %collective-permute-start.5) | collective-permute-done | bytes 294944 | tf_op jit(solution)/shard_map/ppermute | solution.py:418
  122.8 3.2 %newton3_outer.1 = (f32[24,160,128]{2,1,0:T(8,128)S(1)}, f32[24,160,128]{2,1,0:T(8,128)S(1)}, f32[24,160,128]{2,1,0:T(8,128)S(1)}, f32[24,160,128]{2,1,0:T(8,128...) custom-call(s32[1]{0:T(128)} %bitcast.refs_0_, ...), custom_call_target="tpu_custom_call", output_to_operand_aliasing={{0}: (11, {}), {1}: (12, {}), {2}: (13, {}), {3}: (14, {}),... | custom-call | tf_op jit(solution)/shard_map/newton3_outer/pallas_call | solution.py:38
  126.0 0.0 copy-start.3
  126.1 0.0 copy-start.4
  126.1 5.5 %all-to-all-start.2 = ((f32[16,16,8,128]{3,2,1,0:T(8,128)}), f32[16,16,8,128]{3,2,1,0:T(8,128)S(1)}, u32[]{:S(2)}, u32[]{:S(2)}) async-start(f32[16,16,8,128]{3,2,1,0:T(8,128)} %get-tuple-element.56), calls=%async_computation.2 | async-start | bytes 2097152 | tf_op jit(solution)/shard_map/all_to_all | solution.py:467
  131.6 0.0 copy-done.3
  131.6 0.0 copy-done.4
  131.6 19.4 %all-gather = f32[768,128]{1,0:T(8,128)S(1)} all-gather(f32[48,128]{1,0:T(8,128)S(1)} %pad_maximum_fusion), channel_id=2, replica_groups=mesh['axial'=16,'depth'=16] {'axial'}, dimensions={0}, use_global_device_ids=true | all-gather | bytes 417792 | tf_op jit(solution)/shard_map/all_gather | solution.py:473
  151.0 1.7 %deliver.1 = f32[32,128]{1,0:T(8,128)} custom-call(s32[1]{0:T(128)} %bitcast.refs_0_, f32[16,48,128]{2,1,0:T(8,128)S(1)} %bitcast.13), custom_call_target="tpu_custom_call" | custom-call | tf_op jit(solution)/shard_map/deliver/pallas_call | solution.py:38
  152.7 0.0 all-to-all-done.2
  152.7 1.1 copy_bitcast_fusion
  (4 shorter events, 0.0 us)
Async XLA Ops:
  3.8 37.2 %all-to-all-start = ((f32[16,34,8,128]{3,2,1,0:T(8,128)}), f32[16,34,8,128]{3,2,1,0:T(8,128)S(1)}, u32[]{:S(2)}, u32[]{:S(2)}) async-start(f32[16,34,8,128]{3,2,1,0:T(8,128)} %pack1.1), calls=%async_computation | async-start | bytes 4456448 | tf_op jit(solution)/shard_map/all_to_all | solution.py:434
  41.0 4.5 %copy-start = (f32[16,34,8,128]{3,2,1,0:T(8,128)}, f32[16,34,8,128]{3,2,1,0:T(8,128)S(1)}, u32[]{:S(2)}) copy-start(f32[16,34,8,128]{3,2,1,0:T(8,128)S(1)} %all-to-all-done.refs_0_.refs_2_) | copy-start | bytes 6684676
  41.0 38.8 %all-to-all-start.1 = ((f32[16,46,8,128]{3,2,1,0:T(8,128)}), f32[16,46,8,128]{3,2,1,0:T(8,128)}, u32[]{:S(2)}, u32[]{:S(2)}) async-start(f32[16,46,8,128]{3,2,1,0:T(8,128)} %pack2.1), calls=%async_computation.1 | async-start | bytes 6029312 | tf_op jit(solution)/shard_map/all_to_all | solution.py:434
  45.5 10.0 %copy-start.5 = (f32[8]{0:T(128)S(1)}, f32[8]{0:T(128)}, u32[]{:S(2)}) copy-start(f32[8]{0:T(128)} %param.17) | copy-start | bytes 100
  45.5 10.0 %copy-start.6 = (f32[8]{0:T(128)S(1)}, f32[8]{0:T(128)}, u32[]{:S(2)}) copy-start(f32[8]{0:T(128)} %param.16) | copy-start | bytes 100
  45.5 10.0 %copy-start.7 = (f32[8]{0:T(128)S(1)}, f32[8]{0:T(128)}, u32[]{:S(2)}) copy-start(f32[8]{0:T(128)} %param.15) | copy-start | bytes 100
  45.5 10.0 %copy-start.8 = (f32[8]{0:T(128)S(1)}, f32[8]{0:T(128)}, u32[]{:S(2)}) copy-start(f32[8]{0:T(128)} %param.14) | copy-start | bytes 100
  46.8 33.0 %collective-permute-start = (f32[16,17,8,128]{3,2,1,0:T(8,128)}, f32[16,17,8,128]{3,2,1,0:T(8,128)S(1)}, u32[]{:S(2)}, u32[]{:S(2)}) collective-permute-start(f32[16,17,8,128]{3,2,1,0:T(8,128)} %get-tuple-element.30), channel_id=1, source_target_pairs={{0,16},{16,32},{32,48},{48,64},{64,80},{80,96},{96,112},{112,128},... | collective-permute-start | bytes 3342344 | tf_op jit(solution)/shard_map/ppermute | solution.py:415
  53.5 26.2 %collective-permute-start.1 = (f32[16,17,8,128]{3,2,1,0:T(8,128)S(1)}, f32[16,17,8,128]{3,2,1,0:T(8,128)S(1)}, u32[]{:S(2)}, u32[]{:S(2)}) collective-permute-start(f32[16,17,8,128]{3,2,1,0:T(8,128)S(1)} %get-tuple-element.31), channel_id=1, source_target_pairs={{16,0},{32,16},{48,32},{64,48},{80,64},{96,80},{112,96},{128,112},... | collective-permute-start | bytes 3342344 | tf_op jit(solution)/shard_map/ppermute | solution.py:418
  79.8 1.0 copy-start.1
  79.8 1.4 copy-start.2
  92.4 15.3 %collective-permute-start.2 = (f32[4,144,128]{2,1,0:T(8,128)S(1)}, f32[4,144,128]{2,1,0:T(8,128)S(1)}, u32[]{:S(2)}, u32[]{:S(2)}) collective-permute-start(f32[4,144,128]{2,1,0:T(8,128)S(1)} %get-tuple-element.32), channel_id=1, source_target_pairs={{0,16},{16,32},{32,48},{48,64},{64,80},{80,96},{96,112},{112,128},... | collective-permute-start | bytes 884744 | tf_op jit(solution)/shard_map/ppermute | solution.py:415
  102.5 8.0 %collective-permute-start.3 = (f32[4,144,128]{2,1,0:T(8,128)S(1)}, f32[4,144,128]{2,1,0:T(8,128)S(1)}, u32[]{:S(2)}, u32[]{:S(2)}) collective-permute-start(f32[4,144,128]{2,1,0:T(8,128)S(1)} %get-tuple-element.33), channel_id=1, source_target_pairs={{16,0},{32,16},{48,32},{64,48},{80,64},{96,80},{112,96},{128,112},... | collective-permute-start | bytes 884744 | tf_op jit(solution)/shard_map/ppermute | solution.py:418
  112.6 7.7 %collective-permute-start.4 = (f32[4,144,128]{2,1,0:T(8,128)S(1)}, f32[4,144,128]{2,1,0:T(8,128)S(1)}, u32[]{:S(2)}, u32[]{:S(2)}) collective-permute-start(f32[4,144,128]{2,1,0:T(8,128)S(1)} %get-tuple-element.46), channel_id=1, source_target_pairs={{0,16},{16,32},{32,48},{48,64},{64,80},{80,96},{96,112},{112,128},... | collective-permute-start | bytes 884744 | tf_op jit(solution)/shard_map/ppermute | solution.py:415
  114.5 8.3 %collective-permute-start.5 = (f32[4,144,128]{2,1,0:T(8,128)S(1)}, f32[4,144,128]{2,1,0:T(8,128)S(1)}, u32[]{:S(2)}, u32[]{:S(2)}) collective-permute-start(f32[4,144,128]{2,1,0:T(8,128)S(1)} %get-tuple-element.47), channel_id=1, source_target_pairs={{16,0},{32,16},{48,32},{64,48},{80,64},{96,80},{112,96},{128,112},... | collective-permute-start | bytes 884744 | tf_op jit(solution)/shard_map/ppermute | solution.py:418
  126.0 5.5 %copy-start.3 = (s32[16,128]{1,0:T(8,128)S(1)}, s32[16,128]{1,0:T(8,128)}, u32[]{:S(2)}) copy-start(s32[16,128]{1,0:T(8,128)} %param.19) | copy-start | bytes 24580
  126.1 5.6 %copy-start.4 = (s32[16,128]{1,0:T(8,128)S(1)}, s32[16,128]{1,0:T(8,128)}, u32[]{:S(2)}) copy-start(s32[16,128]{1,0:T(8,128)} %param.18) | copy-start | bytes 24580
  126.1 26.7 %all-to-all-start.2 = ((f32[16,16,8,128]{3,2,1,0:T(8,128)}), f32[16,16,8,128]{3,2,1,0:T(8,128)S(1)}, u32[]{:S(2)}, u32[]{:S(2)}) async-start(f32[16,16,8,128]{3,2,1,0:T(8,128)} %get-tuple-element.56), calls=%async_computation.2 | async-start | bytes 2097152 | tf_op jit(solution)/shard_map/all_to_all | solution.py:467

commit v4 on v3

--- a/solution.py
+++ b/solution.py
@@ -9,12 +9,16 @@
 
 SWEEPS = 4
 H = 4
-W = 16
+W = 12
+EDGE = 16
 LANES = 128
-FULL = 2 * W + LANES
-WIDE = (0, FULL)
-NEAR = (W // 2, FULL - W // 2)
-CORE = (W, W + LANES)
+PAD = 8
+SPAN = 2 * EDGE + LANES
+FULL = SPAN + 2 * PAD
+WIDE = (PAD, PAD + SPAN)
+NEAR = (PAD + EDGE // 2, PAD + SPAN - EDGE // 2)
+CORE = (PAD + EDGE, PAD + EDGE + LANES)
+PACKED = 4 * H * 2 * W // LANES
 
 VM = pl.BlockSpec(memory_space=pltpu.VMEM)
 SM = pl.BlockSpec(memory_space=pltpu.SMEM)
@@ -69,16 +73,24 @@
             body(r)
 
 
-def rim_rows(kind):
-    return H if kind in (0, 4) else H - 1
+def groups(first, own):
+    return [0, own - H] if first else list(range(H, own - H, H))
 
 
 def planes(first, own):
-    if first:
-        low = [(k, r) for k in range(5) for r in range(rim_rows(k))]
-        high = [(k, r) for k in range(5) for r in range(own - rim_rows(k), own)]
-        return low + high
-    return [(k, r) for k in range(5) for r in range(rim_rows(k), own - rim_rows(k))]
+    result = []
+    for g in groups(first, own):
+        result += [(k, g + i) for k in range(4) for i in range(H)]
+        result += [(4, (g, j)) for j in range(PACKED)]
+    return result
+
+
+GROUP = 4 * H + PACKED
+
+
+def rim_planes(side):
+    fixed = range(1, H) if side else range(H - 1)
+    return list(range(H)) + [k * H + i for k in range(1, 4) for i in fixed] + list(range(4 * H, GROUP))
 
 
 def pack_kernel(first, scalars, ins, updates, makes, scratch):
@@ -86,7 +98,7 @@
     slices = out.shape[0]
     own = ins[0].shape[0]
     lane = lane_iota(8)
-    bands = [slice(0, H), slice(own - H, own)] if first else [slice(H - 1, own - H + 1)]
+    bands = [slice(0, H), slice(own - H, own)] if first else [slice(H, own - H)]
     copies = [
         pltpu.make_async_copy(x.at[band], y.at[band], sems.at[i, j])
         for i, (x, y) in enumerate(zip(ins, held))
@@ -100,37 +112,42 @@
     def tile(k, a, s):
         return held[k][a, :, LANES * s : LANES * (s + 1)].astype(jnp.float32)
 
+    sent = []
     order = planes(first, own)
-    sent = []
     for p, (kind, a) in enumerate(order):
         if kind < 4:
             for s in range(slices):
                 out[s, p] = tile(kind, a, s)
         else:
-            turned = [
-                [pltpu.roll(tile(k, a, s), (2 * W * k + W) % LANES, 1) for s in range(slices)] for k in range(4)
-            ]
+            (g, part), place = a, a[1] * LANES
+            pieces = range(place // (2 * W), (place + LANES - 1) // (2 * W) + 1)
+            turned = {
+                m: [pltpu.roll(tile(m % 4, g + m // 4, s), (2 * W * m + W) % LANES, 1) for s in range(slices)]
+                for m in pieces
+            }
             for s in range(slices):
-                value = turned[0][s - 1]
-                for k in range(4):
-                    if k:
-                        value = jnp.where(lane >= 2 * W * k, turned[k][s - 1], value)
-                    value = jnp.where(lane >= 2 * W * k + W, turned[k][(s + 1) % slices], value)
+                value = None
+                for m in pieces:
+                    for start, piece in (
+                        (2 * W * m, turned[m][s - 1]),
+                        (2 * W * m + W, turned[m][(s + 1) % slices]),
+                    ):
+                        value = piece if start <= place else jnp.where(lane >= start - place, piece, value)
                 out[s, p] = value
-        if p + 1 == len(order) or order[p + 1][0] != kind:
-            begin = sent[-1][1] if sent else 0
-            band = slice(begin, p + 1)
-            sent.append((pltpu.make_async_copy(out.at[:, band], result.at[:, band], out_sems.at[len(sent)]), p + 1))
-            sent[-1][0].start()
+        if (p + 1) % GROUP in (0, 2 * H):
+            band = slice(sent[-1][1] if sent else 0, p + 1)
+            copy = pltpu.make_async_copy(out.at[:, band], result.at[:, band], out_sems.at[len(sent)])
+            copy.start()
+            sent.append((copy, p + 1))
     for copy, _ in sent:
         copy.wait()
 
 
 def rims_kernel(scalars, reads, updates, makes, scratch):
     (arrived,), (top, bottom) = reads, makes
-    count = top.shape[1]
-    bottom[...] = arrived[:, :count]
-    top[...] = arrived[:, count:]
+    for side, ref in enumerate((bottom, top)):
+        for p, plane in enumerate(rim_planes(side)):
+            ref[:, p] = arrived[:, side * GROUP + plane]
 
 
 def suffix_matrix(m_ref):
@@ -138,14 +155,6 @@
     source = lax.broadcasted_iota(jnp.int32, (rows, cols), 0) & (LANES - 1)
     target = lax.broadcasted_iota(jnp.int32, (rows, cols), 1)
     m_ref[...] = jnp.where(source > target, 4.0 / LANES, 0.0).astype(jnp.bfloat16)
-
-
-def azimuth_pair(ref, r, span):
-    lo, hi = span
-    if span == WIDE:
-        x = ref[r]
-        return pltpu.roll(x, 1, 0) + pltpu.roll(x, FULL - 1, 0)
-    return ref[r, lo - 1 : hi - 1] + ref[r, lo + 1 : hi + 1]
 
 
 def linearise(r, row, total_rows, span, t, t0, fields, m_ref):
@@ -162,7 +171,7 @@
     cap = capacity[r, lo:hi]
     deeper = jnp.where(lane == LANES - 1, 0.0, pltpu.roll(tc, LANES - 1, 1))
     shallower = jnp.where(lane == 0, 0.0, pltpu.roll(tc, 1, 1))
-    pairs = t[r - 1, lo:hi] + t[r + 1, lo:hi] + azimuth_pair(t, r, span)
+    pairs = t[r - 1, lo:hi] + t[r + 1, lo:hi] + t[r, lo - 1 : hi - 1] + t[r, lo + 1 : hi + 1]
     spread = pairs + 2.0 * (deeper + shallower) - 8.0 * tc
     source = c * spread - 0.5 * p - gas * (tc - deeper)
     if t0 is not None:
@@ -173,27 +182,39 @@
     return source, inverse, c * inverse, jnp.where(lane == LANES - 1, 0.0, (2.0 * c + gas) * inverse)
 
 
+CHUNK = 80
+
+
+def chunks(span):
+    lo, hi = span
+    return [(c, min(c + CHUNK, hi)) for c in range(lo, hi, CHUNK)]
+
+
 def sweeps(span, work, ranges, finish):
-    lo, hi = span
     first, side, down, b, c = work
-    lane = lane_iota(hi - lo)
-
-    def swept(src, r):
+
+    def swept(src, r, lo, hi):
+        lane = lane_iota(hi - lo)
         u = src[r, lo:hi]
-        pairs = src[r - 1, lo:hi] + src[r + 1, lo:hi] + azimuth_pair(src, r, span)
+        pairs = src[r - 1, lo:hi] + src[r + 1, lo:hi] + src[r, lo - 1 : hi - 1] + src[r, lo + 1 : hi + 1]
         shallower = jnp.where(lane == 0, 0.0, pltpu.roll(u, 1, 1))
         deeper = pltpu.roll(u, LANES - 1, 1)
         return first[r, lo:hi] + side[r, lo:hi] * (pairs + 2.0 * shallower) + down[r, lo:hi] * deeper
 
     def second(r):
-        b[r, lo:hi] = swept(first, r)
+        for lo, hi in chunks(span):
+            b[r, lo:hi] = swept(first, r, lo, hi)
 
     def third(r):
-        c[r, lo:hi] = swept(b, r)
+        for lo, hi in chunks(span):
+            c[r, lo:hi] = swept(b, r, lo, hi)
+
+    def last(r):
+        finish(r, lambda lo, hi: swept(c, r, lo, hi))
 
     over(ranges[0], second)
     over(ranges[1], third)
-    over(ranges[2], lambda r: finish(r, swept(c, r)))
+    over(ranges[2], last)
 
 
 def inner_rows(rows, k):
@@ -209,102 +230,126 @@
     return x.reshape(x.shape[0] * x.shape[1], LANES).T
 
 
-def unpack_row(tables, source, r, state):
-    t0, conduct, capacity, act, pre, dep = state
-    lo, hi = WIDE
-    edges = from_cells(*source(4))
-
-    def whole(kind):
-        e = 2 * W * kind
-        return jnp.concatenate(
-            [edges[e : e + W], from_cells(*source(kind)), edges[e + W : e + 2 * W]], axis=0
-        )
-
-    t0[r, lo:hi] = whole(0)
-    if source(1) is None:
-        return
-    label = whole(1)
+def unpack_rows(ref, plane_of, first, lo, arrays):
+    edges = jnp.concatenate([from_cells(ref, plane_of(4 * H + j)) for j in range(PACKED)], axis=0)
+    pad = EDGE - W
+    for i in range(H):
+        for kind, array in enumerate(arrays):
+            plane = plane_of(kind * H + i)
+            if plane is None:
+                continue
+            at = 2 * W * (4 * i + kind)
+            array[first + i, lo : lo + EDGE] = pltpu.roll(edges[at : at + EDGE], pad, 0)
+            array[first + i, lo + EDGE : lo + EDGE + LANES] = from_cells(ref, plane)
+            array[first + i, lo + EDGE + LANES : lo + SPAN] = pltpu.roll(edges[at + 2 * W - EDGE : at + 2 * W], EDGE - pad, 0)
+
+
+def look_up(tables, r, state):
+    _, conduct, capacity, act, pre, _ = state
+    wide = slice(*WIDE)
+    label = conduct[r, wide]
     fields = [jnp.full(label.shape, tables[f, 0], jnp.float32) for f in range(4)]
     for zone in range(1, tables.shape[1]):
         here = label == float(zone)
         fields = [jnp.where(here, tables[f, zone], x) for f, x in enumerate(fields)]
-    conduct[r, lo:hi] = fields[0]
-    capacity[r, lo:hi] = fields[1]
-    pre[r, lo:hi] = fields[2] * whole(2)
-    act[r, lo:hi] = fields[3]
-    dep[r, lo:hi] = whole(3)
-
-
-def keeper(span, t, t_new, rims):
-    lo, hi = span
-    own = t.shape[0] - 2 * H
-
+    conduct[r, wide] = fields[0]
+    capacity[r, wide] = fields[1]
+    pre[r, wide] = fields[2] * pre[r, wide]
+    act[r, wide] = fields[3]
+
+
+def keeper(t, t_new):
     def finish(r, update):
-        value = (t[r, lo:hi] + update)[NEAR[0] - lo : NEAR[1] - lo]
-        t_new[r, slice(*NEAR)] = value
-        if rims is not None and r >= own:
-            rims[0][r - own] = value
-        if rims is not None and r < 2 * H:
-            rims[1][r - H] = value
+        for lo, hi in chunks(NEAR):
+            t_new[r, lo:hi] = t[r, lo:hi] + update(lo, hi)
 
     return finish
+
+
+def hand_on(t_new, rims):
+    own = t_new.shape[0] - 2 * H
+    rims[0][...] = t_new[own : own + H, slice(*NEAR)]
+    rims[1][...] = t_new[H : 2 * H, slice(*NEAR)]
+
+
+def rims_in_kernel(scalars, reads, updates, makes, scratch):
+    arrived, above, below = reads
+    arrays, sems = scratch[:4], scratch[4]
+    copies = []
+
+    def rim(side):
+        table = {plane: p for p, plane in enumerate(rim_planes(side))}
+        return table.get
+
+    def send(half):
+        rows = slice(half * 2 * H, (half + 1) * 2 * H)
+        for i, (x, y) in enumerate(zip(arrays, makes)):
+            copies.append(pltpu.make_async_copy(x.at[rows], y.at[rows], sems.at[i, half]))
+            copies[-1].start()
+
+    unpack_rows(above, rim(1), 0, 0, arrays)
+    unpack_rows(arrived, lambda plane: plane, H, 0, arrays)
+    send(0)
+    unpack_rows(arrived, lambda plane: GROUP + plane, 2 * H, 0, arrays)
+    unpack_rows(below, rim(0), 3 * H, 0, arrays)
+    send(1)
+    for copy in copies:
+        copy.wait()
 
 
 def first_kernel(total_rows, scalars, reads, updates, makes, scratch):
     place, tables = scalars
-    state, ub, rims = makes[:6], makes[6], makes[7:]
-    matrix, held, (ua, cs, cd, uc), sems = scratch[0], scratch[1:5], scratch[5:9], scratch[9]
+    arrived, rims_in = reads[0], reads[1:]
+    state, (ub, *rims) = makes[:6], makes[6:]
+    matrix, held, (ua, cs, cd, uc), sem, sems = scratch[0], scratch[1], scratch[2:6], scratch[6], scratch[7]
     t0, conduct, capacity, act, pre, dep = state
+    raw = t0, conduct, pre, dep
     work = ua, cs, cd, ub, uc
     rows = t0.shape[0]
     own = rows - 2 * H
-    copies = [pltpu.make_async_copy(x, y, sems.at[i]) for i, (x, y) in enumerate(zip(reads, held))]
-    for copy in copies:
+    lo, hi = WIDE
+    firsts = groups(False, own)
+    mine = []
+    for i in range(len(firsts)):
+        band = slice(i * GROUP, (i + 1) * GROUP)
+        mine.append(pltpu.make_async_copy(arrived.at[:, band], held.at[:, band], sem.at[i]))
+    others = [
+        pltpu.make_async_copy(
+            x.at[half * 2 * H : (half + 1) * 2 * H], y.at[first : first + 2 * H, lo:hi], sems.at[i, half]
+        )
+        for half, first in enumerate((0, own))
+        for i, (x, y) in enumerate(zip(rims_in, raw))
+    ]
+    for copy in mine:
         copy.start()
     suffix_matrix(matrix)
-    tables_of = [{plane: i for i, plane in enumerate(planes(first, own))} for first in (True, False)]
-    rim_planes = len(tables_of[0]) // 2
-
-    def own_plane(r):
-        def source(kind):
-            for ref, table in zip(held, tables_of):
-                if (kind, r) in table:
-                    return ref, table[kind, r]
-
-        return source
-
-    def halo_plane(r):
-        low = tables_of[0]
-
-        def source(kind):
-            if r < 0:
-                at = low.get((kind, r + own))
-                return None if at is None else (held[2], at - rim_planes)
-            return (held[3], low[kind, r - own]) if (kind, r - own) in low else None
-
-        return source
-
-    copies[0].wait()
-    copies[1].wait()
-    for r in range(own):
-        unpack_row(tables, own_plane(r), r + H, state)
-    copies[2].wait()
-    copies[3].wait()
-    for r in range(H):
-        unpack_row(tables, halo_plane(r - H), r, state)
-        unpack_row(tables, halo_plane(own + r), own + r + H, state)
-    lo, hi = WIDE
 
     def one(r):
-        source, inverse, side, down = linearise(
-            r, place[0] * own + r - H, total_rows, WIDE, t0, None, (conduct, capacity, act, pre), matrix
-        )
-        ua[r, lo:hi] = (source + dep[r, lo:hi]) * inverse
-        cs[r, lo:hi] = side
-        cd[r, lo:hi] = down
-
-    over([(1, rows - 1)], one)
-    sweeps(WIDE, work, [[(k, rows - k)] for k in (2, 3, 4)], keeper(WIDE, t0, ub, rims))
+        for lo, hi in chunks(WIDE):
+            source, inverse, side, down = linearise(
+                r, place[0] * own + r - H, total_rows, (lo, hi), t0, None, (conduct, capacity, act, pre), matrix
+            )
+            ua[r, lo:hi] = (source + dep[r, lo:hi]) * inverse
+            cs[r, lo:hi] = side
+            cd[r, lo:hi] = down
+
+    for i, g in enumerate(firsts):
+        mine[i].wait()
+        if i == 0:
+            for copy in others:
+                copy.start()
+        unpack_rows(held, lambda plane: i * GROUP + plane, g + H, WIDE[0], raw)
+        for r in range(g + H, g + 2 * H):
+            look_up(tables, r, state)
+    inner = 2 * H + 1, own - 1
+    over([inner], one)
+    for copy in others:
+        copy.wait()
+    for r in [*range(1, 2 * H), *range(own, rows - 1)]:
+        look_up(tables, r, state)
+    over([(1, inner[0]), (inner[1], rows - 1)], one)
+    sweeps(WIDE, work, [[(k, rows - k)] for k in (2, 3, 4)], keeper(t0, ub))
+    hand_on(ub, rims)
 
 
 def later_kernel(outer, last, total_rows, scalars, reads, updates, makes, scratch):
@@ -326,35 +371,44 @@
         t[H + own :, lo:hi] = below[...]
 
     def one(r):
-        source, inverse, side, down = linearise(
-            r, place[0] * own + r - H, total_rows, NEAR, t, t0, (conduct, capacity, act, pre), scratch[0]
-        )
-        ua[r, lo:hi] = (source + dep[r, lo:hi]) * inverse
-        cs[r, lo:hi] = side
-        cd[r, lo:hi] = down
+        for lo, hi in chunks(NEAR):
+            source, inverse, side, down = linearise(
+                r, place[0] * own + r - H, total_rows, (lo, hi), t, t0, (conduct, capacity, act, pre), scratch[0]
+            )
+            ua[r, lo:hi] = (source + dep[r, lo:hi]) * inverse
+            cs[r, lo:hi] = side
+            cd[r, lo:hi] = down
 
     if last:
         out, blowing = makes[-2:]
         if outer:
             out[...], blowing[...] = reads[8][...], reads[9][...]
         core = slice(*CORE)
-        mid = slice(CORE[0] - lo, CORE[1] - lo)
 
         def finish(r, update):
-            value = t[r, core] + update[mid]
+            value = t[r, core] + update(*CORE)
             out[:, r - H] = value.T.reshape(out.shape[0], 8, LANES)
             p = pre[r, core] * jnp.exp(act[r, core] * value / (1.0 + jnp.abs(value)))
-            blowing[r - H : r - H + 1, :] = jnp.sum(p.T, axis=0, keepdims=True) * (1.0 / LANES)
+            blowing[pl.ds(r - H, 1), :] = jnp.sum(p.T, axis=0, keepdims=True) * (1.0 / LANES)
 
     else:
-        finish = keeper(NEAR, t, ub, rims)
+        finish = keeper(t, ub)
     ranges = outer_rows if outer else inner_rows
     over(ranges(rows, 1), one)
     sweeps(NEAR, (ua, cs, cd, ub, uc), [ranges(rows, k) for k in (2, 3, 4)], finish)
+    if outer and not last:
+        hand_on(ub, rims)
 
 
 def deliver_kernel(scalars, reads, updates, makes, scratch):
-    (gathered,), (out,), (left, right) = reads, makes, scratch
+    gathered, arrived = reads
+    (out, kelvin), (left, right, sems) = makes, scratch
+    copies = [
+        pltpu.make_async_copy(arrived.at[s], kelvin.at[:, :, LANES * s : LANES * (s + 1)], sems.at[s])
+        for s in range(arrived.shape[0])
+    ]
+    for copy in copies:
+        copy.start()
     groups, rows3, _ = gathered.shape
     rows = rows3 // 3
     me = scalars[0][0]
@@ -385,6 +439,8 @@
         left[...], right[...], (((1,), (1,)), ((), ())), preferred_element_type=jnp.float32
     )
     out[...] = parts[:most] + parts[most : 2 * most] + parts[2 * most :]
+    for copy in copies:
+        copy.wait()
 
 
 def shards(
@@ -432,18 +488,23 @@
         )[0]
 
     arrived = [lax.all_to_all(sent(first), "depth", 0, 0) for first in (True, False)]
-    rims = (n_depth, len(planes(True, own)) // 2, layers, LANES)
-    top, bottom = call(rims_kernel, "rims", [], arrived[:1], [], [rims] * 2, kept=False)
-    came = [*arrived, up(top), down(bottom)]
+    rims = [(n_depth, len(rim_planes(side)), layers, LANES) for side in (1, 0)]
+    top, bottom = call(rims_kernel, "rims", [], arrived[:1], [], rims, kept=False)
+    outer = (4 * H, SPAN, LANES)
+    came = call(
+        rims_in_kernel, "rims_in", [], [arrived[0], up(top), down(bottom)], [], [outer] * 4,
+        [pltpu.VMEM(outer, jnp.float32)] * 4 + [pltpu.SemaphoreType.DMA((4, 2))],
+        out_space=pltpu.HBM, limit=16,
+    )
+    came = [pltpu.with_memory_space_constraint(x, pltpu.HBM) for x in [arrived[1], *came]]
     *arrays, top, bottom = call(
         functools.partial(first_kernel, total_rows), "newton1",
-        [place, tables], [pltpu.with_memory_space_constraint(x, pltpu.HBM) for x in came], [],
-        [extended] * 7 + [rim] * 2,
+        [place, tables], came, [], [extended] * 7 + [rim] * 2,
         matrix
-        + [pltpu.VMEM(x.shape, jnp.float32) for x in came]
+        + [pltpu.VMEM(came[0].shape, jnp.float32)]
         + [pltpu.VMEM(extended, jnp.float32)] * 4
-        + [pltpu.SemaphoreType.DMA((4,))],
-        space=pltpu.HBM, limit=20,
+        + [pltpu.SemaphoreType.DMA((2,)), pltpu.SemaphoreType.DMA((4, 2))],
+        space=pltpu.HBM, limit=14,
     )
     t0, conduct, capacity, act, pre, dep = arrays[:6]
     t = arrays[6]
@@ -465,21 +526,26 @@
     kelvin, blowing = work[6:]
 
     kelvin = lax.all_to_all(kelvin, "depth", 0, 0)
-    kelvin = jnp.transpose(kelvin, (1, 2, 0, 3)).reshape(own, layers, columns)
 
     faces = jnp.concatenate(
         [blowing, keeper_position.astype(jnp.float32), stream_keeper.astype(jnp.float32)], axis=0
     )
     gathered = lax.all_gather(faces, "axial")
     slots = 2 * own * LANES
-    (delivered,) = call(
-        deliver_kernel, "deliver", [place], [gathered], [], [(slots // LANES, LANES)],
-        [
+    any_space = pl.BlockSpec(memory_space=pl.ANY)
+    delivered, kelvin = pl.pallas_call(
+        lambda place, *refs: deliver_kernel([place], refs[:2], [], refs[2:4], refs[4:]),
+        out_shape=[f32(slots // LANES, LANES), f32(own, layers, columns)],
+        in_specs=[SM, VM, any_space],
+        out_specs=[VM, any_space],
+        scratch_shapes=[
             pltpu.VMEM((3 * slots // LANES, slots), jnp.bfloat16),
             pltpu.VMEM((LANES, slots), jnp.bfloat16),
+            pltpu.SemaphoreType.DMA((n_depth,)),
         ],
-        kept=False,
-    )
+        compiler_params=pltpu.CompilerParams(vmem_limit_bytes=8 * 1024 * 1024),
+        name="deliver",
+    )(place, gathered, kelvin)
     return (kelvin, delivered.reshape(slots))
 
 

time: 154 us -> 149 us (0.968)
  waiting for transfers between devices: 55.7 us -> 49.5 us
  Pallas kernels: 32.4 us -> 37.4 us
  starting transfers between devices: 42.9 us -> 40.3 us
  local copies, waits for them, and re-layouts: 2.54 us -> 0.03 us
    all_to_all x2, waiting for transfers between devices: 50.3 us -> 30 us  [shards(): lax.all_to_all(sent(first), 'depth', 0, 0)]
    ppermute x3, waiting for transfers between devices: 0.01 us -> 9.41 us  [up(): return lax.ppermute(x, 'axial', [(i, i + 1) for i in range(n_axial - 1)])]
    ppermute x3, waiting for transfers between devices: 5.42 us -> 10.1 us  [down(): return lax.ppermute(x, 'axial', [(i + 1, i) for i in range(n_axial - 1)])]
    pallas_call x0 -> x1, Pallas kernels: none -> 2.54 us  [shards(): pl.pallas_call(lambda place, *refs: deliver_kernel([place], refs[:2], [],...]
    pallas_call x9, Pallas kernels: 32.4 us -> 34.8 us  [call(): pl.pallas_call(body, out_shape=[pltpu.VMEM(u.shape, jnp.float32) for u in...]
  transfers between devices with their start and end apart: 9 -> 9, of which waited for: 4 -> 6; matrix products, arithmetic and copies ran while one was open for 0% -> 0% of each run, Pallas kernels for 8% -> 10%
where the time goes in v4:
time: 149 us; the launch traced here: 148 us
  waiting for transfers between devices  49.5 us (33%)
  starting transfers between devices  40.3 us (27%)
  Pallas kernels  37.4 us (25%)
  blocking collectives  19.4 us (13%)
    pallas_call x9, Pallas kernels, call(): pl.pallas_call(body, out_shape=[pltpu.VMEM(u.shape, jnp.float32) for u in...  34.8 us
    all_to_all x2, waiting for transfers between devices, shards(): lax.all_to_all(sent(first), 'depth', 0, 0)  30 us
    all_gather x1, blocking collectives, shards(): gathered = lax.all_gather(faces, 'axial')  19.4 us
    ppermute x3, starting transfers between devices, up(): return lax.ppermute(x, 'axial', [(i, i + 1) for i in range(n_axial - 1)])  17.8 us
    all_to_all x2, starting transfers between devices, shards(): lax.all_to_all(sent(first), 'depth', 0, 0)  12 us
    ppermute x3, waiting for transfers between devices, down(): return lax.ppermute(x, 'axial', [(i + 1, i) for i in range(n_axial - 1)])  10.1 us
    ppermute x3, waiting for transfers between devices, up(): return lax.ppermute(x, 'axial', [(i, i + 1) for i in range(n_axial - 1)])  9.41 us
    ppermute x3, starting transfers between devices, down(): return lax.ppermute(x, 'axial', [(i + 1, i) for i in range(n_axial - 1)])  6.44 us
  transfers between devices with their start and end apart: 9, of which 6 were waited for; matrix products, arithmetic and copies ran while one was open for 0% of the time, Pallas kernels for 10%

profile of v4, /device:TPU:1, one launch (start us, length us, event | category | flops | bytes accessed | tf_op | source)
XLA Modules:
  0.0 148.3 jit_solution(8206762214871210568)
XLA Ops:
  0.6 3.4 %pack1.1 = f32[16,38,8,128]{3,2,1,0:T(8,128)} custom-call(f32[16,8,2048]{2,1,0:T(8,128)} %refs_0_.3, s32[16,8,2048]{2,1,0:T(8,128)} %refs_1_.3, f32[16,8,2048]{2,1,0:T(8,128)} %refs_2_.3, f32[16,8,2048]{2,1,0:T(8,128)} %refs_3_.3), custom_call_target="tpu_custom_call" | custom-call | tf_op jit(solution)/shard_map/pack1/pallas_call | solution.py:42
  4.0 7.6 %all-to-all-start.1 = ((f32[16,38,8,128]{3,2,1,0:T(8,128)}), f32[16,38,8,128]{3,2,1,0:T(8,128)S(1)}, u32[]{:S(2)}, u32[]{:S(2)}) async-start(f32[16,38,8,128]{3,2,1,0:T(8,128)} %pack1.1), calls=%async_computation.1 | async-start | bytes 4980736 | tf_op jit(solution)/shard_map/all_to_all | solution.py:490
  11.6 3.4 %pack2.1 = f32[16,38,8,128]{3,2,1,0:T(8,128)} custom-call(f32[16,8,2048]{2,1,0:T(8,128)} %refs_0_.3, s32[16,8,2048]{2,1,0:T(8,128)} %refs_1_.3, f32[16,8,2048]{2,1,0:T(8,128)} %refs_2_.3, f32[16,8,2048]{2,1,0:T(8,128)} %refs_3_.3), custom_call_target="tpu_custom_call" | custom-call | tf_op jit(solution)/shard_map/pack2/pallas_call | solution.py:42
  15.0 29.9 %all-to-all-done.1.refs_0_ = f32[16,38,8,128]{3,2,1,0:T(8,128)S(1)} async-done(((f32[16,38,8,128]{3,2,1,0:T(8,128)}), f32[16,38,8,128]{3,2,1,0:T(8,128)S(1)}, u32[]{:S(2)}, u32[]{:S(2)}) %all-to-all-start.1) | async-done | bytes 2490400 | tf_op jit(solution)/shard_map/all_to_all | solution.py:490
  44.9 4.4 %all-to-all-start = ((f32[16,38,8,128]{3,2,1,0:T(8,128)}), f32[16,38,8,128]{3,2,1,0:T(8,128)}, u32[]{:S(2)}, u32[]{:S(2)}) async-start(f32[16,38,8,128]{3,2,1,0:T(8,128)} %pack2.1), calls=%async_computation | async-start | bytes 4980736 | tf_op jit(solution)/shard_map/all_to_all | solution.py:490
  49.3 0.0 copy-start.2
  49.4 0.0 copy-start.3
  49.4 0.0 copy-start.4
  49.4 1.5 %rims.1 = (f32[16,16,8,128]{3,2,1,0:T(8,128)}, f32[16,16,8,128]{3,2,1,0:T(8,128)}) custom-call(f32[16,38,8,128]{3,2,1,0:T(8,128)S(1)} %all-to-all-done.1.refs_0_), custom_call_target="tpu_custom_call" | custom-call | tf_op jit(solution)/shard_map/rims/pallas_call | solution.py:42
  50.9 6.5 %collective-permute-start = (f32[16,16,8,128]{3,2,1,0:T(8,128)}, f32[16,16,8,128]{3,2,1,0:T(8,128)S(1)}, u32[]{:S(2)}, u32[]{:S(2)}) collective-permute-start(f32[16,16,8,128]{3,2,1,0:T(8,128)} %get-tuple-element.36), channel_id=1, source_target_pairs={{0,16},{16,32},{32,48},{48,64},{64,80},{80,96},{96,112},{112,128},... | collective-permute-start | bytes 3145736 | tf_op jit(solution)/shard_map/ppermute | solution.py:471
  57.4 1.9 %collective-permute-start.1 = (f32[16,16,8,128]{3,2,1,0:T(8,128)}, f32[16,16,8,128]{3,2,1,0:T(8,128)}, u32[]{:S(2)}, u32[]{:S(2)}) collective-permute-start(f32[16,16,8,128]{3,2,1,0:T(8,128)} %get-tuple-element.37), channel_id=1, source_target_pairs={{16,0},{32,16},{48,32},{64,48},{80,64},{96,80},{112,96},{128,112},... | collective-permute-start | bytes 3145736 | tf_op jit(solution)/shard_map/ppermute | solution.py:474
  59.3 0.0 copy-done.2
  59.4 0.0 copy-done.3
  59.4 0.0 copy-done.4
  59.4 0.7 pad_maximum_fusion.1.refs_1_
  60.0 9.4 %collective-permute-done.refs_1_ = f32[16,16,8,128]{3,2,1,0:T(8,128)S(1)} collective-permute-done((f32[16,16,8,128]{3,2,1,0:T(8,128)}, f32[16,16,8,128]{3,2,1,0:T(8,128)S(1)}, u32[]{:S(2)}, u32[]{:S(2)}) %collective-permute-start) | collective-permute-done | bytes 1048608 | tf_op jit(solution)/shard_map/ppermute | solution.py:471
  69.4 4.7 %collective-permute-done.1.refs_2_ = f32[16,16,8,128]{3,2,1,0:T(8,128)} collective-permute-done((f32[16,16,8,128]{3,2,1,0:T(8,128)}, f32[16,16,8,128]{3,2,1,0:T(8,128)}, u32[]{:S(2)}, u32[]{:S(2)}) %collective-permute-start.1) | collective-permute-done | bytes 1048608 | tf_op jit(solution)/shard_map/ppermute | solution.py:474
  74.1 4.2 %rims_in.1 = (f32[16,160,128]{2,1,0:T(8,128)}, f32[16,160,128]{2,1,0:T(8,128)}, f32[16,160,128]{2,1,0:T(8,128)}, f32[16,160,128]{2,1,0:T(8,128)}) custom-call(f32[16,38,8,128]{3,2,1,0:T(8,128)S(1)} %all-to-all-done.1.refs_0_, f32[16,16,8,128]{3,2,1,0:T(8,128)S(1)} %collective-permute-done.refs_1_, f32[16,16,8,128]{3,2,1,0:T(8,128)} %collective-permute-done.1.refs_2_), custom_call_target="tpu_custom_call" | custom-call | tf_op jit(solution)/shard_map/rims_in/pallas_call | solution.py:42
  78.3 0.1 all-to-all-done.refs_2_
  78.4 10.7 %newton1.1 = (f32[24,176,128]{2,1,0:T(8,128)S(1)}, f32[24,176,128]{2,1,0:T(8,128)S(1)}, f32[24,176,128]{2,1,0:T(8,128)S(1)}, f32[24,176,128]{2,1,0:T(8,128)S(1)}...) custom-call(s32[1]{0:T(128)} %bitcast.refs_0_.place, ...), custom_call_target="tpu_custom_call" | custom-call | tf_op jit(solution)/shard_map/newton1/pallas_call | solution.py:42
  89.2 9.4 %collective-permute-start.2 = (f32[4,144,128]{2,1,0:T(8,128)S(1)}, f32[4,144,128]{2,1,0:T(8,128)S(1)}, u32[]{:S(2)}, u32[]{:S(2)}) collective-permute-start(f32[4,144,128]{2,1,0:T(8,128)S(1)} %get-tuple-element.42), channel_id=1, source_target_pairs={{0,16},{16,32},{32,48},{48,64},{64,80},{80,96},{96,112},{112,128},... | collective-permute-start | bytes 884744 | tf_op jit(solution)/shard_map/ppermute | solution.py:471
  98.6 2.1 %collective-permute-start.3 = (f32[4,144,128]{2,1,0:T(8,128)S(1)}, f32[4,144,128]{2,1,0:T(8,128)S(1)}, u32[]{:S(2)}, u32[]{:S(2)}) collective-permute-start(f32[4,144,128]{2,1,0:T(8,128)S(1)} %get-tuple-element.43), channel_id=1, source_target_pairs={{16,0},{32,16},{48,32},{64,48},{80,64},{96,80},{112,96},{128,112},... | collective-permute-start | bytes 884744 | tf_op jit(solution)/shard_map/ppermute | solution.py:474
  100.7 3.0 %newton2_inner.1 = (f32[24,176,128]{2,1,0:T(8,128)S(1)}, f32[24,176,128]{2,1,0:T(8,128)S(1)}, f32[24,176,128]{2,1,0:T(8,128)S(1)}, f32[24,176,128]{2,1,0:T(8,128)S(1)}, f32[24,176,128]{2,1,0:T(8,128)S(1)}) custom-call(s32[1]{0:T(128)} %bitcast.refs_0_.place, f32[24,176,128]{2,1,0:T(8,128)S(1)} %get-tuple-element.50.refs_1_.refs_9_, ...), custom_call_target="tpu_custom_call" | custom-call | tf_op jit(solution)/shard_map/newton2_inner/pallas_call | solution.py:42
  103.8 0.0 collective-permute-done.2.refs_1_
  103.8 2.9 %collective-permute-done.3.refs_2_ = f32[4,144,128]{2,1,0:T(8,128)S(1)} collective-permute-done((f32[4,144,128]{2,1,0:T(8,128)S(1)}, f32[4,144,128]{2,1,0:T(8,128)S(1)}, u32[]{:S(2)}, u32[]{:S(2)}) %collective-permute-start.3) | collective-permute-done | bytes 294944 | tf_op jit(solution)/shard_map/ppermute | solution.py:474
  106.7 2.0 %newton2_outer.1 = (f32[24,176,128]{2,1,0:T(8,128)S(1)}, f32[24,176,128]{2,1,0:T(8,128)S(1)}, f32[24,176,128]{2,1,0:T(8,128)S(1)}, f32[24,176,128]{2,1,0:T(8,128...) custom-call(s32[1]{0:T(128)} %bitcast.refs_0_.place, ...), custom_call_target="tpu_custom_call", output_to_operand_aliasing={{0}: (9, {}), {1}: (10, {}), {2}: (11, {}), {3}: (12, {}), ... | custom-call | tf_op jit(solution)/shard_map/newton2_outer/pallas_call | solution.py:42
  108.7 1.9 %collective-permute-start.4 = (f32[4,144,128]{2,1,0:T(8,128)S(1)}, f32[4,144,128]{2,1,0:T(8,128)S(1)}, u32[]{:S(2)}, u32[]{:S(2)}) collective-permute-start(f32[4,144,128]{2,1,0:T(8,128)S(1)} %get-tuple-element.56), channel_id=1, source_target_pairs={{0,16},{16,32},{32,48},{48,64},{64,80},{80,96},{96,112},{112,128},... | collective-permute-start | bytes 884744 | tf_op jit(solution)/shard_map/ppermute | solution.py:471
  110.6 2.4 %collective-permute-start.5 = (f32[4,144,128]{2,1,0:T(8,128)S(1)}, f32[4,144,128]{2,1,0:T(8,128)S(1)}, u32[]{:S(2)}, u32[]{:S(2)}) collective-permute-start(f32[4,144,128]{2,1,0:T(8,128)S(1)} %get-tuple-element.57), channel_id=1, source_target_pairs={{16,0},{32,16},{48,32},{64,48},{80,64},{96,80},{112,96},{128,112},... | collective-permute-start | bytes 884744 | tf_op jit(solution)/shard_map/ppermute | solution.py:474
  113.0 3.3 %newton3_inner.1 = (f32[24,176,128]{2,1,0:T(8,128)S(1)}, f32[24,176,128]{2,1,0:T(8,128)S(1)}, f32[24,176,128]{2,1,0:T(8,128)S(1)}, f32[24,176,128]{2,1,0:T(8,128...) custom-call(s32[1]{0:T(128)} %bitcast.refs_0_.place, ...), custom_call_target="tpu_custom_call" | custom-call | tf_op jit(solution)/shard_map/newton3_inner/pallas_call | solution.py:42
  116.4 0.0 collective-permute-done.4.refs_1_
  116.4 2.5 %collective-permute-done.5.refs_2_ = f32[4,144,128]{2,1,0:T(8,128)S(1)} collective-permute-done((f32[4,144,128]{2,1,0:T(8,128)S(1)}, f32[4,144,128]{2,1,0:T(8,128)S(1)}, u32[]{:S(2)}, u32[]{:S(2)}) %collective-permute-start.5) | collective-permute-done | bytes 294944 | tf_op jit(solution)/shard_map/ppermute | solution.py:474
  118.9 0.0 copy-start
  118.9 0.0 copy-start.1
  118.9 3.2 %newton3_outer.1 = (f32[24,176,128]{2,1,0:T(8,128)S(1)}, f32[24,176,128]{2,1,0:T(8,128)S(1)}, f32[24,176,128]{2,1,0:T(8,128)S(1)}, f32[24,176,128]{2,1,0:T(8,128...) custom-call(s32[1]{0:T(128)} %bitcast.refs_0_.place, ...), custom_call_target="tpu_custom_call", output_to_operand_aliasing={{0}: (11, {}), {1}: (12, {}), {2}: (13, {}), {3}: (14, {}),... | custom-call | tf_op jit(solution)/shard_map/newton3_outer/pallas_call | solution.py:42
  122.2 4.0 %all-to-all-start.2 = ((f32[16,16,8,128]{3,2,1,0:T(8,128)}), f32[16,16,8,128]{3,2,1,0:T(8,128)S(1)}, u32[]{:S(2)}, u32[]{:S(2)}) async-start(f32[16,16,8,128]{3,2,1,0:T(8,128)} %get-tuple-element.67), calls=%async_computation.2 | async-start | bytes 2097152 | tf_op jit(solution)/shard_map/all_to_all | solution.py:528
  126.2 0.0 copy-done
  126.2 0.0 copy-done.1
  126.2 19.4 %all-gather = f32[768,128]{1,0:T(8,128)S(1)} all-gather(f32[48,128]{1,0:T(8,128)S(1)} %pad_maximum_fusion), channel_id=2, replica_groups=mesh['axial'=16,'depth'=16] {'axial'}, dimensions={0}, use_global_device_ids=true | all-gather | bytes 417792 | tf_op jit(solution)/shard_map/all_gather | solution.py:533
  145.6 0.0 all-to-all-done.2.refs_1_
  145.6 2.5 %deliver.1 = (f32[32,128]{1,0:T(8,128)}, f32[16,8,2048]{2,1,0:T(8,128)}) custom-call(s32[1]{0:T(128)} %bitcast.refs_0_.place, f32[16,48,128]{2,1,0:T(8,128)S(1)} %bitcast.7, f32[16,16,8,128]{3,2,1,0:T(8,128)S(1)} %all-to-all-done.2.refs_1_), custom_call_target="tpu_custom_call" | custom-call | tf_op jit(solution)/shard_map/deliver/pallas_call | solution.py:536
  (3 shorter events, 0.0 us)
Async XLA Ops:
  4.0 40.9 %all-to-all-start.1 = ((f32[16,38,8,128]{3,2,1,0:T(8,128)}), f32[16,38,8,128]{3,2,1,0:T(8,128)S(1)}, u32[]{:S(2)}, u32[]{:S(2)}) async-start(f32[16,38,8,128]{3,2,1,0:T(8,128)} %pack1.1), calls=%async_computation.1 | async-start | bytes 4980736 | tf_op jit(solution)/shard_map/all_to_all | solution.py:490
  44.9 33.6 %all-to-all-start = ((f32[16,38,8,128]{3,2,1,0:T(8,128)}), f32[16,38,8,128]{3,2,1,0:T(8,128)}, u32[]{:S(2)}, u32[]{:S(2)}) async-start(f32[16,38,8,128]{3,2,1,0:T(8,128)} %pack2.1), calls=%async_computation | async-start | bytes 4980736 | tf_op jit(solution)/shard_map/all_to_all | solution.py:490
  49.3 10.0 %copy-start.2 = (f32[8]{0:T(128)S(1)}, f32[8]{0:T(128)}, u32[]{:S(2)}) copy-start(f32[8]{0:T(128)} %param.17) | copy-start | bytes 100
  49.4 10.0 %copy-start.3 = (f32[8]{0:T(128)S(1)}, f32[8]{0:T(128)}, u32[]{:S(2)}) copy-start(f32[8]{0:T(128)} %param.16) | copy-start | bytes 100
  49.4 10.0 %copy-start.4 = (f32[8]{0:T(128)S(1)}, f32[8]{0:T(128)}, u32[]{:S(2)}) copy-start(f32[8]{0:T(128)} %param.15) | copy-start | bytes 100
  50.9 18.5 %collective-permute-start = (f32[16,16,8,128]{3,2,1,0:T(8,128)}, f32[16,16,8,128]{3,2,1,0:T(8,128)S(1)}, u32[]{:S(2)}, u32[]{:S(2)}) collective-permute-start(f32[16,16,8,128]{3,2,1,0:T(8,128)} %get-tuple-element.36), channel_id=1, source_target_pairs={{0,16},{16,32},{32,48},{48,64},{64,80},{80,96},{96,112},{112,128},... | collective-permute-start | bytes 3145736 | tf_op jit(solution)/shard_map/ppermute | solution.py:471
  57.4 16.7 %collective-permute-start.1 = (f32[16,16,8,128]{3,2,1,0:T(8,128)}, f32[16,16,8,128]{3,2,1,0:T(8,128)}, u32[]{:S(2)}, u32[]{:S(2)}) collective-permute-start(f32[16,16,8,128]{3,2,1,0:T(8,128)} %get-tuple-element.37), channel_id=1, source_target_pairs={{16,0},{32,16},{48,32},{64,48},{80,64},{96,80},{112,96},{128,112},... | collective-permute-start | bytes 3145736 | tf_op jit(solution)/shard_map/ppermute | solution.py:474
  89.2 14.6 %collective-permute-start.2 = (f32[4,144,128]{2,1,0:T(8,128)S(1)}, f32[4,144,128]{2,1,0:T(8,128)S(1)}, u32[]{:S(2)}, u32[]{:S(2)}) collective-permute-start(f32[4,144,128]{2,1,0:T(8,128)S(1)} %get-tuple-element.42), channel_id=1, source_target_pairs={{0,16},{16,32},{32,48},{48,64},{64,80},{80,96},{96,112},{112,128},... | collective-permute-start | bytes 884744 | tf_op jit(solution)/shard_map/ppermute | solution.py:471
  98.6 8.0 %collective-permute-start.3 = (f32[4,144,128]{2,1,0:T(8,128)S(1)}, f32[4,144,128]{2,1,0:T(8,128)S(1)}, u32[]{:S(2)}, u32[]{:S(2)}) collective-permute-start(f32[4,144,128]{2,1,0:T(8,128)S(1)} %get-tuple-element.43), channel_id=1, source_target_pairs={{16,0},{32,16},{48,32},{64,48},{80,64},{96,80},{112,96},{128,112},... | collective-permute-start | bytes 884744 | tf_op jit(solution)/shard_map/ppermute | solution.py:474
  108.7 7.7 %collective-permute-start.4 = (f32[4,144,128]{2,1,0:T(8,128)S(1)}, f32[4,144,128]{2,1,0:T(8,128)S(1)}, u32[]{:S(2)}, u32[]{:S(2)}) collective-permute-start(f32[4,144,128]{2,1,0:T(8,128)S(1)} %get-tuple-element.56), channel_id=1, source_target_pairs={{0,16},{16,32},{32,48},{48,64},{64,80},{80,96},{96,112},{112,128},... | collective-permute-start | bytes 884744 | tf_op jit(solution)/shard_map/ppermute | solution.py:471
  110.6 8.3 %collective-permute-start.5 = (f32[4,144,128]{2,1,0:T(8,128)S(1)}, f32[4,144,128]{2,1,0:T(8,128)S(1)}, u32[]{:S(2)}, u32[]{:S(2)}) collective-permute-start(f32[4,144,128]{2,1,0:T(8,128)S(1)} %get-tuple-element.57), channel_id=1, source_target_pairs={{16,0},{32,16},{48,32},{64,48},{80,64},{96,80},{112,96},{128,112},... | collective-permute-start | bytes 884744 | tf_op jit(solution)/shard_map/ppermute | solution.py:474
  118.9 7.2 %copy-start = (s32[16,128]{1,0:T(8,128)S(1)}, s32[16,128]{1,0:T(8,128)}, u32[]{:S(2)}) copy-start(s32[16,128]{1,0:T(8,128)} %param.19) | copy-start | bytes 24580
  118.9 7.2 %copy-start.1 = (s32[16,128]{1,0:T(8,128)S(1)}, s32[16,128]{1,0:T(8,128)}, u32[]{:S(2)}) copy-start(s32[16,128]{1,0:T(8,128)} %param.18) | copy-start | bytes 24580
  122.2 23.4 %all-to-all-start.2 = ((f32[16,16,8,128]{3,2,1,0:T(8,128)}), f32[16,16,8,128]{3,2,1,0:T(8,128)S(1)}, u32[]{:S(2)}, u32[]{:S(2)}) async-start(f32[16,16,8,128]{3,2,1,0:T(8,128)} %get-tuple-element.67), calls=%async_computation.2 | async-start | bytes 2097152 | tf_op jit(solution)/shard_map/all_to_all | solution.py:528

commit v5 on v4

--- a/solution.py
+++ b/solution.py
@@ -99,15 +99,13 @@
     own = ins[0].shape[0]
     lane = lane_iota(8)
     bands = [slice(0, H), slice(own - H, own)] if first else [slice(H, own - H)]
-    copies = [
-        pltpu.make_async_copy(x.at[band], y.at[band], sems.at[i, j])
+    copies = {
+        (i, j): pltpu.make_async_copy(x.at[band], y.at[band], sems.at[i, j])
+        for j, band in enumerate(bands)
         for i, (x, y) in enumerate(zip(ins, held))
-        for j, band in enumerate(bands)
-    ]
-    for copy in copies:
+    }
+    for copy in copies.values():
         copy.start()
-    for copy in copies:
-        copy.wait()
 
     def tile(k, a, s):
         return held[k][a, :, LANES * s : LANES * (s + 1)].astype(jnp.float32)
@@ -116,6 +114,9 @@
     order = planes(first, own)
     for p, (kind, a) in enumerate(order):
         if kind < 4:
+            band = min(p // GROUP, len(bands) - 1)
+            if (kind, band) in copies:
+                copies.pop((kind, band)).wait()
             for s in range(slices):
                 out[s, p] = tile(kind, a, s)
         else:
@@ -244,9 +245,8 @@
             array[first + i, lo + EDGE + LANES : lo + SPAN] = pltpu.roll(edges[at + 2 * W - EDGE : at + 2 * W], EDGE - pad, 0)
 
 
-def look_up(tables, r, state):
+def look_up(tables, r, wide, state):
     _, conduct, capacity, act, pre, _ = state
-    wide = slice(*WIDE)
     label = conduct[r, wide]
     fields = [jnp.full(label.shape, tables[f, 0], jnp.float32) for f in range(4)]
     for zone in range(1, tables.shape[1]):
@@ -272,39 +272,56 @@
     rims[1][...] = t_new[H : 2 * H, slice(*NEAR)]
 
 
-def rims_in_kernel(scalars, reads, updates, makes, scratch):
-    arrived, above, below = reads
-    arrays, sems = scratch[:4], scratch[4]
+def unpack_own_kernel(scalars, reads, updates, makes, scratch):
+    t0, conduct, capacity, act, pre, dep = makes
+    for half in range(2):
+        unpack_rows(reads[0], lambda plane: half * GROUP + plane, half * H, 0, (t0, conduct, pre, dep))
+    for r in range(2 * H):
+        look_up(scalars[0], r, slice(0, SPAN), makes)
+
+
+def outer_kernel(total_rows, own, scalars, reads, updates, makes, scratch):
+    place, tables = scalars
+    above, below, own_rims = reads[0], reads[1], reads[2:]
+    arrays, matrix, sems = scratch[:9], scratch[9], scratch[10]
+    state, work = arrays[:6], arrays[6:]
+    t0, conduct, capacity, act, pre, dep = state
+    lo, hi = WIDE
     copies = []
+
+    def send(which):
+        for i in which:
+            copies.append(pltpu.make_async_copy(arrays[i].at[:, lo:hi], makes[i], sems.at[i]))
+            copies[-1].start()
 
     def rim(side):
         table = {plane: p for p, plane in enumerate(rim_planes(side))}
         return table.get
 
-    def send(half):
-        rows = slice(half * 2 * H, (half + 1) * 2 * H)
-        for i, (x, y) in enumerate(zip(arrays, makes)):
-            copies.append(pltpu.make_async_copy(x.at[rows], y.at[rows], sems.at[i, half]))
-            copies[-1].start()
-
-    unpack_rows(above, rim(1), 0, 0, arrays)
-    unpack_rows(arrived, lambda plane: plane, H, 0, arrays)
-    send(0)
-    unpack_rows(arrived, lambda plane: GROUP + plane, 2 * H, 0, arrays)
-    unpack_rows(below, rim(0), 3 * H, 0, arrays)
-    send(1)
+    suffix_matrix(matrix)
+    for x, y in zip(own_rims, state):
+        y[H : 3 * H, lo:hi] = x[...]
+    unpack_rows(above, rim(1), 0, lo, (t0, conduct, pre, dep))
+    unpack_rows(below, rim(0), 3 * H, lo, (t0, conduct, pre, dep))
+    send([0, 5])
+    for r in [*range(1, H), *range(3 * H, 4 * H - 1)]:
+        look_up(tables, r, slice(lo, hi), state)
+    send([1, 2, 3, 4])
+    for first, shift in ((1, -H), (2 * H + 1, own - 3 * H)):
+        one = first_row(total_rows, place, own, shift, state, work, matrix)
+        over([(first, first + 2 * H - 2)], one)
+    send([6, 7, 8])
     for copy in copies:
         copy.wait()
 
 
 def first_kernel(total_rows, scalars, reads, updates, makes, scratch):
     place, tables = scalars
-    arrived, rims_in = reads[0], reads[1:]
-    state, (ub, *rims) = makes[:6], makes[6:]
-    matrix, held, (ua, cs, cd, uc), sem, sems = scratch[0], scratch[1], scratch[2:6], scratch[6], scratch[7]
+    arrived, came = reads[0], reads[1:]
+    state, work, rims = makes[:6], makes[6:11], makes[11:]
+    matrix, held, sem, sems = scratch
     t0, conduct, capacity, act, pre, dep = state
-    raw = t0, conduct, pre, dep
-    work = ua, cs, cd, ub, uc
+    ua, cs, cd, ub, uc = work
     rows = t0.shape[0]
     own = rows - 2 * H
     lo, hi = WIDE
@@ -313,43 +330,68 @@
     for i in range(len(firsts)):
         band = slice(i * GROUP, (i + 1) * GROUP)
         mine.append(pltpu.make_async_copy(arrived.at[:, band], held.at[:, band], sem.at[i]))
-    others = [
-        pltpu.make_async_copy(
-            x.at[half * 2 * H : (half + 1) * 2 * H], y.at[first : first + 2 * H, lo:hi], sems.at[i, half]
-        )
-        for half, first in enumerate((0, own))
-        for i, (x, y) in enumerate(zip(rims_in, raw))
-    ]
+    others = []
+    for i, (x, y) in enumerate(zip(came, (*state, ua, cs, cd))):
+        edge = 0 if i < 6 else 1
+        for half, shift in enumerate((0, own - 2 * H)):
+            low, high = half * 2 * H + edge, (half + 1) * 2 * H - edge
+            others.append(
+                pltpu.make_async_copy(x.at[low:high], y.at[low + shift : high + shift, lo:hi], sems.at[i, half])
+            )
     for copy in mine:
         copy.start()
     suffix_matrix(matrix)
-
-    def one(r):
-        for lo, hi in chunks(WIDE):
-            source, inverse, side, down = linearise(
-                r, place[0] * own + r - H, total_rows, (lo, hi), t0, None, (conduct, capacity, act, pre), matrix
-            )
-            ua[r, lo:hi] = (source + dep[r, lo:hi]) * inverse
-            cs[r, lo:hi] = side
-            cd[r, lo:hi] = down
 
     for i, g in enumerate(firsts):
         mine[i].wait()
         if i == 0:
             for copy in others:
                 copy.start()
-        unpack_rows(held, lambda plane: i * GROUP + plane, g + H, WIDE[0], raw)
+        unpack_rows(held, lambda plane: i * GROUP + plane, g + H, lo, (t0, conduct, pre, dep))
         for r in range(g + H, g + 2 * H):
-            look_up(tables, r, state)
-    inner = 2 * H + 1, own - 1
-    over([inner], one)
-    for copy in others:
+            look_up(tables, r, slice(lo, hi), state)
+    one = first_row(total_rows, place, own, -H, state, work, matrix)
+    middle = rows // 2 - 1, rows // 2 + 1
+    over([(2 * H + 1, middle[0]), (middle[1], own - 1)], one)
+    for copy in others[:12]:
         copy.wait()
-    for r in [*range(1, 2 * H), *range(own, rows - 1)]:
-        look_up(tables, r, state)
-    over([(1, inner[0]), (inner[1], rows - 1)], one)
-    sweeps(WIDE, work, [[(k, rows - k)] for k in (2, 3, 4)], keeper(t0, ub))
+    over([(2 * H - 1, 2 * H + 1), (own - 1, own + 1)], one)
+    for copy in others[12:]:
+        copy.wait()
+    sweeps(WIDE, work, [rim_rows(rows, k) for k in (2, 3, 4)], keeper(t0, ub))
     hand_on(ub, rims)
+
+
+def rim_rows(rows, k):
+    return [(k, 3 * H - k), (rows - 3 * H + k, rows - k)]
+
+
+def rest_rows(rows, k):
+    return [(3 * H - k, rows - 3 * H + k)]
+
+
+def first_row(total_rows, place, own, shift, state, work, matrix):
+    t0, conduct, capacity, act, pre, dep = state
+    ua, cs, cd = work[:3]
+
+    def one(r):
+        for lo, hi in chunks(WIDE):
+            source, inverse, side, down = linearise(
+                r, place[0] * own + r + shift, total_rows, (lo, hi), t0, None, (conduct, capacity, act, pre), matrix
+            )
+            ua[r, lo:hi] = (source + dep[r, lo:hi]) * inverse
+            cs[r, lo:hi] = side
+            cd[r, lo:hi] = down
+
+    return one
+
+
+def first_rest_kernel(total_rows, scalars, reads, updates, makes, scratch):
+    (place,), state, (matrix,) = scalars, reads, scratch
+    rows = state[0].shape[0]
+    suffix_matrix(matrix)
+    over(rest_rows(rows, 1), first_row(total_rows, place, rows - 2 * H, -H, state, updates, matrix))
+    sweeps(WIDE, updates, [rest_rows(rows, k) for k in (2, 3, 4)], keeper(state[0], updates[3]))
 
 
 def later_kernel(outer, last, total_rows, scalars, reads, updates, makes, scratch):
@@ -490,24 +532,31 @@
     arrived = [lax.all_to_all(sent(first), "depth", 0, 0) for first in (True, False)]
     rims = [(n_depth, len(rim_planes(side)), layers, LANES) for side in (1, 0)]
     top, bottom = call(rims_kernel, "rims", [], arrived[:1], [], rims, kept=False)
+    own_rims = call(
+        unpack_own_kernel, "unpack_own", [tables], arrived[:1], [], [(2 * H, SPAN, LANES)] * 6
+    )
     outer = (4 * H, SPAN, LANES)
     came = call(
-        rims_in_kernel, "rims_in", [], [arrived[0], up(top), down(bottom)], [], [outer] * 4,
-        [pltpu.VMEM(outer, jnp.float32)] * 4 + [pltpu.SemaphoreType.DMA((4, 2))],
-        out_space=pltpu.HBM, limit=16,
+        functools.partial(outer_kernel, total_rows, own), "newton1_outer",
+        [place, tables], [up(top), down(bottom), *own_rims], [], [outer] * 9,
+        [pltpu.VMEM((4 * H, FULL, LANES), jnp.float32)] * 9 + matrix + [pltpu.SemaphoreType.DMA((9,))],
+        out_space=pltpu.HBM, limit=24,
     )
     came = [pltpu.with_memory_space_constraint(x, pltpu.HBM) for x in [arrived[1], *came]]
     *arrays, top, bottom = call(
         functools.partial(first_kernel, total_rows), "newton1",
-        [place, tables], came, [], [extended] * 7 + [rim] * 2,
+        [place, tables], came, [], [extended] * 11 + [rim] * 2,
         matrix
         + [pltpu.VMEM(came[0].shape, jnp.float32)]
-        + [pltpu.VMEM(extended, jnp.float32)] * 4
-        + [pltpu.SemaphoreType.DMA((2,)), pltpu.SemaphoreType.DMA((4, 2))],
-        space=pltpu.HBM, limit=14,
-    )
-    t0, conduct, capacity, act, pre, dep = arrays[:6]
-    t = arrays[6]
+        + [pltpu.SemaphoreType.DMA((2,)), pltpu.SemaphoreType.DMA((9, 2))],
+        space=pltpu.HBM, limit=8,
+    )
+    state, work = arrays[:6], arrays[6:]
+    work = call(
+        functools.partial(first_rest_kernel, total_rows), "newton1_rest", [place], state, work, [], matrix
+    )
+    t0, conduct, capacity, act, pre, dep = state
+    t = work[3]
     for last in (False, True):
         above, below = up(top), down(bottom)
         fixed = [t0, conduct, capacity, act, pre, dep]

time: 149 us -> 146 us (0.980)
  starting transfers between devices: 40.3 us -> 37.1 us
  waiting for transfers between devices: 49.5 us -> 46.6 us
  Pallas kernels: 37.4 us -> 40.2 us
    ppermute x3, starting transfers between devices: 17.8 us -> 14.4 us  [up(): return lax.ppermute(x, 'axial', [(i, i + 1) for i in range(n_axial - 1)])]
    pallas_call x9 -> x11, Pallas kernels: 34.8 us -> 37.6 us  [call(): pl.pallas_call(body, out_shape=[pltpu.VMEM(u.shape, jnp.float32) for u in...]
    ppermute x3, waiting for transfers between devices: 9.41 us -> 7.87 us  [up(): return lax.ppermute(x, 'axial', [(i, i + 1) for i in range(n_axial - 1)])]
  transfers between devices with their start and end apart: 9 -> 9, of which waited for: 6 -> 5; matrix products, arithmetic and copies ran while one was open for 0% -> 0% of each run, Pallas kernels for 10% -> 15%
where the time goes in v5:
time: 146 us; the launch traced here: 145 us
  waiting for transfers between devices  46.6 us (32%)
  Pallas kernels  40.2 us (28%)
  starting transfers between devices  37.1 us (25%)
  blocking collectives  19.4 us (13%)
    pallas_call x11, Pallas kernels, call(): pl.pallas_call(body, out_shape=[pltpu.VMEM(u.shape, jnp.float32) for u in...  37.6 us
    all_to_all x2, waiting for transfers between devices, shards(): lax.all_to_all(sent(first), 'depth', 0, 0)  29.9 us
    all_gather x1, blocking collectives, shards(): gathered = lax.all_gather(faces, 'axial')  19.4 us
    ppermute x3, starting transfers between devices, up(): return lax.ppermute(x, 'axial', [(i, i + 1) for i in range(n_axial - 1)])  14.4 us
    all_to_all x2, starting transfers between devices, shards(): lax.all_to_all(sent(first), 'depth', 0, 0)  12.1 us
    ppermute x3, waiting for transfers between devices, down(): return lax.ppermute(x, 'axial', [(i + 1, i) for i in range(n_axial - 1)])  8.85 us
    ppermute x3, waiting for transfers between devices, up(): return lax.ppermute(x, 'axial', [(i, i + 1) for i in range(n_axial - 1)])  7.87 us
    ppermute x3, starting transfers between devices, down(): return lax.ppermute(x, 'axial', [(i + 1, i) for i in range(n_axial - 1)])  6.66 us
  transfers between devices with their start and end apart: 9, of which 5 were waited for; matrix products, arithmetic and copies ran while one was open for 0% of the time, Pallas kernels for 15%

profile of v5, /device:TPU:1, one launch (start us, length us, event | category | flops | bytes accessed | tf_op | source)
XLA Modules:
  0.0 145.0 jit_solution(3562171449335501845)
XLA Ops:
  0.6 3.1 %pack1.1 = f32[16,38,8,128]{3,2,1,0:T(8,128)} custom-call(f32[16,8,2048]{2,1,0:T(8,128)} %refs_0_.3, s32[16,8,2048]{2,1,0:T(8,128)} %refs_1_.3, f32[16,8,2048]{2,1,0:T(8,128)} %refs_2_.3, f32[16,8,2048]{2,1,0:T(8,128)} %refs_3_.3), custom_call_target="tpu_custom_call" | custom-call | tf_op jit(solution)/shard_map/pack1/pallas_call | solution.py:42
  3.7 7.6 %all-to-all-start.1 = ((f32[16,38,8,128]{3,2,1,0:T(8,128)}), f32[16,38,8,128]{3,2,1,0:T(8,128)S(1)}, u32[]{:S(2)}, u32[]{:S(2)}) async-start(f32[16,38,8,128]{3,2,1,0:T(8,128)} %pack1.1), calls=%async_computation.1 | async-start | bytes 4980736 | tf_op jit(solution)/shard_map/all_to_all | solution.py:532
  11.3 3.4 %pack2.1 = f32[16,38,8,128]{3,2,1,0:T(8,128)} custom-call(f32[16,8,2048]{2,1,0:T(8,128)} %refs_0_.3, s32[16,8,2048]{2,1,0:T(8,128)} %refs_1_.3, f32[16,8,2048]{2,1,0:T(8,128)} %refs_2_.3, f32[16,8,2048]{2,1,0:T(8,128)} %refs_3_.3), custom_call_target="tpu_custom_call" | custom-call | tf_op jit(solution)/shard_map/pack2/pallas_call | solution.py:42
  14.7 29.9 %all-to-all-done.1.refs_0_.refs_1_ = f32[16,38,8,128]{3,2,1,0:T(8,128)S(1)} async-done(((f32[16,38,8,128]{3,2,1,0:T(8,128)}), f32[16,38,8,128]{3,2,1,0:T(8,128)S(1)}, u32[]{:S(2)}, u32[]{:S(2)}) %all-to-all-start.1) | async-done | bytes 2490400 | tf_op jit(solution)/shard_map/all_to_all | solution.py:532
  44.6 4.5 %all-to-all-start = ((f32[16,38,8,128]{3,2,1,0:T(8,128)}), f32[16,38,8,128]{3,2,1,0:T(8,128)}, u32[]{:S(2)}, u32[]{:S(2)}) async-start(f32[16,38,8,128]{3,2,1,0:T(8,128)} %pack2.1), calls=%async_computation | async-start | bytes 4980736 | tf_op jit(solution)/shard_map/all_to_all | solution.py:532
  49.1 0.0 copy-start.2
  49.1 0.0 copy-start.3
  49.1 0.0 copy-start.4
  49.1 1.5 %rims.1 = (f32[16,16,8,128]{3,2,1,0:T(8,128)}, f32[16,16,8,128]{3,2,1,0:T(8,128)}) custom-call(f32[16,38,8,128]{3,2,1,0:T(8,128)S(1)} %all-to-all-done.1.refs_0_.refs_1_), custom_call_target="tpu_custom_call" | custom-call | tf_op jit(solution)/shard_map/rims/pallas_call | solution.py:42
  50.6 6.5 %collective-permute-start = (f32[16,16,8,128]{3,2,1,0:T(8,128)}, f32[16,16,8,128]{3,2,1,0:T(8,128)S(1)}, u32[]{:S(2)}, u32[]{:S(2)}) collective-permute-start(f32[16,16,8,128]{3,2,1,0:T(8,128)} %get-tuple-element.52), channel_id=1, source_target_pairs={{0,16},{16,32},{32,48},{48,64},{64,80},{80,96},{96,112},{112,128},... | collective-permute-start | bytes 3145736 | tf_op jit(solution)/shard_map/ppermute | solution.py:513
  57.1 1.9 %collective-permute-start.1 = (f32[16,16,8,128]{3,2,1,0:T(8,128)}, f32[16,16,8,128]{3,2,1,0:T(8,128)}, u32[]{:S(2)}, u32[]{:S(2)}) collective-permute-start(f32[16,16,8,128]{3,2,1,0:T(8,128)} %get-tuple-element.53), channel_id=1, source_target_pairs={{16,0},{32,16},{48,32},{64,48},{80,64},{96,80},{112,96},{128,112},... | collective-permute-start | bytes 3145736 | tf_op jit(solution)/shard_map/ppermute | solution.py:516
  59.1 0.0 copy-done.2
  59.1 0.0 copy-done.3
  59.1 0.0 copy-done.4
  59.1 0.7 pad_maximum_fusion.1.refs_0_.refs_1_
  59.8 1.5 %unpack_own.1 = (f32[8,160,128]{2,1,0:T(8,128)S(1)}, f32[8,160,128]{2,1,0:T(8,128)S(1)}, f32[8,160,128]{2,1,0:T(8,128)S(1)}, f32[8,160,128]{2,1,0:T(8,128)S(1)},...) custom-call(f32[4,8]{1,0:T(4,128)S(1)} %pad_maximum_fusion.1.refs_0_.refs_1_, ...), custom_call_target="tpu_custom_call" | custom-call | tf_op jit(solution)/shard_map/unpack_own/pallas_call | solution.py:42
  61.3 7.9 %collective-permute-done.refs_2_ = f32[16,16,8,128]{3,2,1,0:T(8,128)S(1)} collective-permute-done((f32[16,16,8,128]{3,2,1,0:T(8,128)}, f32[16,16,8,128]{3,2,1,0:T(8,128)S(1)}, u32[]{:S(2)}, u32[]{:S(2)}) %collective-permute-start) | collective-permute-done | bytes 1048608 | tf_op jit(solution)/shard_map/ppermute | solution.py:513
  69.2 4.7 %collective-permute-done.1.refs_3_ = f32[16,16,8,128]{3,2,1,0:T(8,128)} collective-permute-done((f32[16,16,8,128]{3,2,1,0:T(8,128)}, f32[16,16,8,128]{3,2,1,0:T(8,128)}, u32[]{:S(2)}, u32[]{:S(2)}) %collective-permute-start.1) | collective-permute-done | bytes 1048608 | tf_op jit(solution)/shard_map/ppermute | solution.py:516
  73.9 7.7 %newton1_outer.1 = (f32[16,160,128]{2,1,0:T(8,128)}, f32[16,160,128]{2,1,0:T(8,128)}, f32[16,160,128]{2,1,0:T(8,128)}, f32[16,160,128]{2,1,0:T(8,128)}, f32[16,1...) custom-call(s32[1]{0:T(128)} %bitcast.refs_0_.place, ...), custom_call_target="tpu_custom_call" | custom-call | tf_op jit(solution)/shard_map/newton1_outer/pallas_call | solution.py:42
  81.6 0.0 all-to-all-done.refs_2_
  81.6 7.7 %newton1.1 = (f32[24,176,128]{2,1,0:T(8,128)S(1)}, f32[24,176,128]{2,1,0:T(8,128)S(1)}, f32[24,176,128]{2,1,0:T(8,128)S(1)}, f32[24,176,128]{2,1,0:T(8,128)S(1)}...) custom-call(s32[1]{0:T(128)} %bitcast.refs_0_.place, ...), custom_call_target="tpu_custom_call" | custom-call | tf_op jit(solution)/shard_map/newton1/pallas_call | solution.py:42
  89.3 6.0 %collective-permute-start.2 = (f32[4,144,128]{2,1,0:T(8,128)S(1)}, f32[4,144,128]{2,1,0:T(8,128)S(1)}, u32[]{:S(2)}, u32[]{:S(2)}) collective-permute-start(f32[4,144,128]{2,1,0:T(8,128)S(1)} %get-tuple-element.69), channel_id=1, source_target_pairs={{0,16},{16,32},{32,48},{48,64},{64,80},{80,96},{96,112},{112,128},... | collective-permute-start | bytes 884744 | tf_op jit(solution)/shard_map/ppermute | solution.py:513
  95.3 2.1 %collective-permute-start.3 = (f32[4,144,128]{2,1,0:T(8,128)S(1)}, f32[4,144,128]{2,1,0:T(8,128)S(1)}, u32[]{:S(2)}, u32[]{:S(2)}) collective-permute-start(f32[4,144,128]{2,1,0:T(8,128)S(1)} %get-tuple-element.70), channel_id=1, source_target_pairs={{16,0},{32,16},{48,32},{64,48},{80,64},{96,80},{112,96},{128,112},... | collective-permute-start | bytes 884744 | tf_op jit(solution)/shard_map/ppermute | solution.py:516
  97.4 1.0 newton1_rest.1
  98.5 3.0 %newton2_inner.1 = (f32[24,176,128]{2,1,0:T(8,128)S(1)}, f32[24,176,128]{2,1,0:T(8,128)S(1)}, f32[24,176,128]{2,1,0:T(8,128)S(1)}, f32[24,176,128]{2,1,0:T(8,128)S(1)}, f32[24,176,128]{2,1,0:T(8,128)S(1)}) custom-call(s32[1]{0:T(128)} %bitcast.refs_0_.place, f32[24,176,128]{2,1,0:T(8,128)S(1)} %get-tuple-element.82.refs_1_.refs_9_, ...), custom_call_target="tpu_custom_call" | custom-call | tf_op jit(solution)/shard_map/newton2_inner/pallas_call | solution.py:42
  101.5 0.0 collective-permute-done.2.refs_1_
  101.5 1.8 %collective-permute-done.3.refs_2_ = f32[4,144,128]{2,1,0:T(8,128)S(1)} collective-permute-done((f32[4,144,128]{2,1,0:T(8,128)S(1)}, f32[4,144,128]{2,1,0:T(8,128)S(1)}, u32[]{:S(2)}, u32[]{:S(2)}) %collective-permute-start.3) | collective-permute-done | bytes 294944 | tf_op jit(solution)/shard_map/ppermute | solution.py:516
  103.4 2.0 %newton2_outer.1 = (f32[24,176,128]{2,1,0:T(8,128)S(1)}, f32[24,176,128]{2,1,0:T(8,128)S(1)}, f32[24,176,128]{2,1,0:T(8,128)S(1)}, f32[24,176,128]{2,1,0:T(8,128...) custom-call(s32[1]{0:T(128)} %bitcast.refs_0_.place, ...), custom_call_target="tpu_custom_call", output_to_operand_aliasing={{0}: (9, {}), {1}: (10, {}), {2}: (11, {}), {3}: (12, {}), ... | custom-call | tf_op jit(solution)/shard_map/newton2_outer/pallas_call | solution.py:42
  105.4 1.9 %collective-permute-start.4 = (f32[4,144,128]{2,1,0:T(8,128)S(1)}, f32[4,144,128]{2,1,0:T(8,128)S(1)}, u32[]{:S(2)}, u32[]{:S(2)}) collective-permute-start(f32[4,144,128]{2,1,0:T(8,128)S(1)} %get-tuple-element.88), channel_id=1, source_target_pairs={{0,16},{16,32},{32,48},{48,64},{64,80},{80,96},{96,112},{112,128},... | collective-permute-start | bytes 884744 | tf_op jit(solution)/shard_map/ppermute | solution.py:513
  107.3 2.6 %collective-permute-start.5 = (f32[4,144,128]{2,1,0:T(8,128)S(1)}, f32[4,144,128]{2,1,0:T(8,128)S(1)}, u32[]{:S(2)}, u32[]{:S(2)}) collective-permute-start(f32[4,144,128]{2,1,0:T(8,128)S(1)} %get-tuple-element.89), channel_id=1, source_target_pairs={{16,0},{32,16},{48,32},{64,48},{80,64},{96,80},{112,96},{128,112},... | collective-permute-start | bytes 884744 | tf_op jit(solution)/shard_map/ppermute | solution.py:516
  109.9 3.3 %newton3_inner.1 = (f32[24,176,128]{2,1,0:T(8,128)S(1)}, f32[24,176,128]{2,1,0:T(8,128)S(1)}, f32[24,176,128]{2,1,0:T(8,128)S(1)}, f32[24,176,128]{2,1,0:T(8,128...) custom-call(s32[1]{0:T(128)} %bitcast.refs_0_.place, ...), custom_call_target="tpu_custom_call" | custom-call | tf_op jit(solution)/shard_map/newton3_inner/pallas_call | solution.py:42
  113.3 0.0 collective-permute-done.4.refs_1_
  113.3 2.3 %collective-permute-done.5.refs_2_ = f32[4,144,128]{2,1,0:T(8,128)S(1)} collective-permute-done((f32[4,144,128]{2,1,0:T(8,128)S(1)}, f32[4,144,128]{2,1,0:T(8,128)S(1)}, u32[]{:S(2)}, u32[]{:S(2)}) %collective-permute-start.5) | collective-permute-done | bytes 294944 | tf_op jit(solution)/shard_map/ppermute | solution.py:516
  115.6 0.0 copy-start
  115.6 0.0 copy-start.1
  115.6 3.2 %newton3_outer.1 = (f32[24,176,128]{2,1,0:T(8,128)S(1)}, f32[24,176,128]{2,1,0:T(8,128)S(1)}, f32[24,176,128]{2,1,0:T(8,128)S(1)}, f32[24,176,128]{2,1,0:T(8,128...) custom-call(s32[1]{0:T(128)} %bitcast.refs_0_.place, ...), custom_call_target="tpu_custom_call", output_to_operand_aliasing={{0}: (11, {}), {1}: (12, {}), {2}: (13, {}), {3}: (14, {}),... | custom-call | tf_op jit(solution)/shard_map/newton3_outer/pallas_call | solution.py:42
  118.8 4.0 %all-to-all-start.2 = ((f32[16,16,8,128]{3,2,1,0:T(8,128)}), f32[16,16,8,128]{3,2,1,0:T(8,128)S(1)}, u32[]{:S(2)}, u32[]{:S(2)}) async-start(f32[16,16,8,128]{3,2,1,0:T(8,128)} %get-tuple-element.99), calls=%async_computation.2 | async-start | bytes 2097152 | tf_op jit(solution)/shard_map/all_to_all | solution.py:577
  122.8 0.0 copy-done
  122.9 0.0 copy-done.1
  122.9 19.4 %all-gather = f32[768,128]{1,0:T(8,128)S(1)} all-gather(f32[48,128]{1,0:T(8,128)S(1)} %pad_maximum_fusion), channel_id=2, replica_groups=mesh['axial'=16,'depth'=16] {'axial'}, dimensions={0}, use_global_device_ids=true | all-gather | bytes 417792 | tf_op jit(solution)/shard_map/all_gather | solution.py:582
  142.3 0.0 all-to-all-done.2.refs_1_
  142.3 2.5 %deliver.1 = (f32[32,128]{1,0:T(8,128)}, f32[16,8,2048]{2,1,0:T(8,128)}) custom-call(s32[1]{0:T(128)} %bitcast.refs_0_.place, f32[16,48,128]{2,1,0:T(8,128)S(1)} %bitcast.7, f32[16,16,8,128]{3,2,1,0:T(8,128)S(1)} %all-to-all-done.2.refs_1_), custom_call_target="tpu_custom_call" | custom-call | tf_op jit(solution)/shard_map/deliver/pallas_call | solution.py:585
  (3 shorter events, 0.0 us)
Async XLA Ops:
  3.7 40.9 %all-to-all-start.1 = ((f32[16,38,8,128]{3,2,1,0:T(8,128)}), f32[16,38,8,128]{3,2,1,0:T(8,128)S(1)}, u32[]{:S(2)}, u32[]{:S(2)}) async-start(f32[16,38,8,128]{3,2,1,0:T(8,128)} %pack1.1), calls=%async_computation.1 | async-start | bytes 4980736 | tf_op jit(solution)/shard_map/all_to_all | solution.py:532
  44.6 37.0 %all-to-all-start = ((f32[16,38,8,128]{3,2,1,0:T(8,128)}), f32[16,38,8,128]{3,2,1,0:T(8,128)}, u32[]{:S(2)}, u32[]{:S(2)}) async-start(f32[16,38,8,128]{3,2,1,0:T(8,128)} %pack2.1), calls=%async_computation | async-start | bytes 4980736 | tf_op jit(solution)/shard_map/all_to_all | solution.py:532
  49.1 10.0 %copy-start.2 = (f32[8]{0:T(128)S(1)}, f32[8]{0:T(128)}, u32[]{:S(2)}) copy-start(f32[8]{0:T(128)} %param.17) | copy-start | bytes 100
  49.1 10.0 %copy-start.3 = (f32[8]{0:T(128)S(1)}, f32[8]{0:T(128)}, u32[]{:S(2)}) copy-start(f32[8]{0:T(128)} %param.16) | copy-start | bytes 100
  49.1 10.0 %copy-start.4 = (f32[8]{0:T(128)S(1)}, f32[8]{0:T(128)}, u32[]{:S(2)}) copy-start(f32[8]{0:T(128)} %param.15) | copy-start | bytes 100
  50.6 18.5 %collective-permute-start = (f32[16,16,8,128]{3,2,1,0:T(8,128)}, f32[16,16,8,128]{3,2,1,0:T(8,128)S(1)}, u32[]{:S(2)}, u32[]{:S(2)}) collective-permute-start(f32[16,16,8,128]{3,2,1,0:T(8,128)} %get-tuple-element.52), channel_id=1, source_target_pairs={{0,16},{16,32},{32,48},{48,64},{64,80},{80,96},{96,112},{112,128},... | collective-permute-start | bytes 3145736 | tf_op jit(solution)/shard_map/ppermute | solution.py:513
  57.1 16.7 %collective-permute-start.1 = (f32[16,16,8,128]{3,2,1,0:T(8,128)}, f32[16,16,8,128]{3,2,1,0:T(8,128)}, u32[]{:S(2)}, u32[]{:S(2)}) collective-permute-start(f32[16,16,8,128]{3,2,1,0:T(8,128)} %get-tuple-element.53), channel_id=1, source_target_pairs={{16,0},{32,16},{48,32},{64,48},{80,64},{96,80},{112,96},{128,112},... | collective-permute-start | bytes 3145736 | tf_op jit(solution)/shard_map/ppermute | solution.py:516
  89.3 12.2 %collective-permute-start.2 = (f32[4,144,128]{2,1,0:T(8,128)S(1)}, f32[4,144,128]{2,1,0:T(8,128)S(1)}, u32[]{:S(2)}, u32[]{:S(2)}) collective-permute-start(f32[4,144,128]{2,1,0:T(8,128)S(1)} %get-tuple-element.69), channel_id=1, source_target_pairs={{0,16},{16,32},{32,48},{48,64},{64,80},{80,96},{96,112},{112,128},... | collective-permute-start | bytes 884744 | tf_op jit(solution)/shard_map/ppermute | solution.py:513
  95.3 8.0 %collective-permute-start.3 = (f32[4,144,128]{2,1,0:T(8,128)S(1)}, f32[4,144,128]{2,1,0:T(8,128)S(1)}, u32[]{:S(2)}, u32[]{:S(2)}) collective-permute-start(f32[4,144,128]{2,1,0:T(8,128)S(1)} %get-tuple-element.70), channel_id=1, source_target_pairs={{16,0},{32,16},{48,32},{64,48},{80,64},{96,80},{112,96},{128,112},... | collective-permute-start | bytes 884744 | tf_op jit(solution)/shard_map/ppermute | solution.py:516
  105.4 7.9 %collective-permute-start.4 = (f32[4,144,128]{2,1,0:T(8,128)S(1)}, f32[4,144,128]{2,1,0:T(8,128)S(1)}, u32[]{:S(2)}, u32[]{:S(2)}) collective-permute-start(f32[4,144,128]{2,1,0:T(8,128)S(1)} %get-tuple-element.88), channel_id=1, source_target_pairs={{0,16},{16,32},{32,48},{48,64},{64,80},{80,96},{96,112},{112,128},... | collective-permute-start | bytes 884744 | tf_op jit(solution)/shard_map/ppermute | solution.py:513
  107.3 8.3 %collective-permute-start.5 = (f32[4,144,128]{2,1,0:T(8,128)S(1)}, f32[4,144,128]{2,1,0:T(8,128)S(1)}, u32[]{:S(2)}, u32[]{:S(2)}) collective-permute-start(f32[4,144,128]{2,1,0:T(8,128)S(1)} %get-tuple-element.89), channel_id=1, source_target_pairs={{16,0},{32,16},{48,32},{64,48},{80,64},{96,80},{112,96},{128,112},... | collective-permute-start | bytes 884744 | tf_op jit(solution)/shard_map/ppermute | solution.py:516
  115.6 7.2 %copy-start = (s32[16,128]{1,0:T(8,128)S(1)}, s32[16,128]{1,0:T(8,128)}, u32[]{:S(2)}) copy-start(s32[16,128]{1,0:T(8,128)} %param.19) | copy-start | bytes 24580
  115.6 7.2 %copy-start.1 = (s32[16,128]{1,0:T(8,128)S(1)}, s32[16,128]{1,0:T(8,128)}, u32[]{:S(2)}) copy-start(s32[16,128]{1,0:T(8,128)} %param.18) | copy-start | bytes 24580
  118.8 23.4 %all-to-all-start.2 = ((f32[16,16,8,128]{3,2,1,0:T(8,128)}), f32[16,16,8,128]{3,2,1,0:T(8,128)S(1)}, u32[]{:S(2)}, u32[]{:S(2)}) async-start(f32[16,16,8,128]{3,2,1,0:T(8,128)} %get-tuple-element.99), calls=%async_computation.2 | async-start | bytes 2097152 | tf_op jit(solution)/shard_map/all_to_all | solution.py:577

commit v6 on v5

--- a/solution.py
+++ b/solution.py
@@ -39,14 +39,15 @@
         kernel(groups[0], groups[1], groups[3], groups[4], groups[5])
 
     first = len(scalars) + len(reads)
+    out_spaces = out_space if isinstance(out_space, list) else [out_space] * len(makes)
     results = pl.pallas_call(
         body,
         out_shape=[pltpu.VMEM(u.shape, jnp.float32) for u in updates]
-        + [out_space(s, jnp.float32) if kept else f32(*s) for s in makes],
+        + [x(s, jnp.float32) if kept else f32(*s) for x, s in zip(out_spaces, makes)],
         in_specs=[SM] * len(scalars)
         + [pl.BlockSpec(memory_space=space)] * len(reads)
         + [VM] * len(updates),
-        out_specs=[VM] * len(updates) + [pl.BlockSpec(memory_space=out_space)] * len(makes),
+        out_specs=[VM] * len(updates) + [pl.BlockSpec(memory_space=x) for x in out_spaces],
         input_output_aliases={first + i: i for i in range(len(updates))},
         scratch_shapes=list(scratch),
         compiler_params=pltpu.CompilerParams(vmem_limit_bytes=limit * 1024 * 1024),
@@ -424,20 +425,35 @@
     if last:
         out, blowing = makes[-2:]
         if outer:
-            out[...], blowing[...] = reads[8][...], reads[9][...]
+            part, sems = scratch[1:]
+            copies = [
+                pltpu.make_async_copy(reads[8], out.at[:, H : own - H], sems.at[0]),
+                pltpu.make_async_copy(part.at[:, :H], out.at[:, :H], sems.at[1]),
+                pltpu.make_async_copy(part.at[:, H:], out.at[:, own - H :], sems.at[2]),
+            ]
+            copies[0].start()
+            blowing[...] = reads[9][...]
+        else:
+            part = out
         core = slice(*CORE)
 
         def finish(r, update):
             value = t[r, core] + update(*CORE)
-            out[:, r - H] = value.T.reshape(out.shape[0], 8, LANES)
+            at = r - 2 * H if not outer else r - H if r < 2 * H else r - own + H
+            part[:, at] = value.T.reshape(part.shape[0], 8, LANES)
             p = pre[r, core] * jnp.exp(act[r, core] * value / (1.0 + jnp.abs(value)))
             blowing[pl.ds(r - H, 1), :] = jnp.sum(p.T, axis=0, keepdims=True) * (1.0 / LANES)
+            if outer and r in (2 * H - 1, own + H - 1):
+                copies[1 if r < own else 2].start()
 
     else:
         finish = keeper(t, ub)
     ranges = outer_rows if outer else inner_rows
     over(ranges(rows, 1), one)
     sweeps(NEAR, (ua, cs, cd, ub, uc), [ranges(rows, k) for k in (2, 3, 4)], finish)
+    if outer and last:
+        for copy in copies:
+            copy.wait()
     if outer and not last:
         hand_on(ub, rims)
 
@@ -462,7 +478,8 @@
     first = jnp.minimum(first, groups * rows - most)
     high_of = lax.broadcasted_iota(jnp.int32, (most, LANES), 0)
     low_of = lax.broadcasted_iota(jnp.int32, (LANES, LANES), 0)
-    for i in range(most):
+
+    def one(i, _):
         at = first + i
         group, r = at // rows, at % rows
         value = gathered[group, pl.ds(r, 1), :]
@@ -470,13 +487,16 @@
         owner = gathered[group, pl.ds(2 * rows + r, 1), :].astype(jnp.int32)
         high = jnp.where(owner == me, slot >> 7, -1)
         low = slot & (LANES - 1)
-        here = slice(LANES * i, LANES * (i + 1))
+        here = pl.ds(pl.multiple_of(LANES * i, LANES), LANES)
         hit = high_of == high
         for k, part in enumerate(split3(value)):
             left[most * k : most * (k + 1), here] = jnp.where(hit, part.astype(jnp.float32), 0.0).astype(
                 jnp.bfloat16
             )
         right[:, here] = jnp.where(low_of == low, 1.0, 0.0).astype(jnp.bfloat16)
+        return 0
+
+    lax.fori_loop(0, most, one, 0, unroll=4)
     parts = lax.dot_general(
         left[...], right[...], (((1,), (1,)), ((), ())), preferred_element_type=jnp.float32
     )
@@ -560,15 +580,21 @@
     for last in (False, True):
         above, below = up(top), down(bottom)
         fixed = [t0, conduct, capacity, act, pre, dep]
-        results = [(n_depth, own, layers, LANES), (own, LANES)] if last else []
+        part = (n_depth, own - 2 * H, layers, LANES)
+        results = [part, (own, LANES)] if last else []
         work = call(
             functools.partial(later_kernel, False, last, total_rows), "newton3_inner" if last else "newton2_inner",
             [place], [t] + fixed, [], [extended] * 5 + results, matrix,
         )
+        kwargs = dict(
+            makes=[(n_depth, own, layers, LANES), (own, LANES)],
+            scratch=matrix
+            + [pltpu.VMEM((n_depth, 2 * H, layers, LANES), jnp.float32), pltpu.SemaphoreType.DMA((3,))],
+            out_space=[pltpu.HBM, pltpu.VMEM],
+        ) if last else dict(makes=[rim] * 2, scratch=matrix)
         work = call(
             functools.partial(later_kernel, True, last, total_rows), "newton3_outer" if last else "newton2_outer",
-            [place], [above, below] + fixed + work[5:], [t] + work[:5], results if last else [rim] * 2, matrix,
-            kept=not last,
+            [place], [above, below] + fixed + work[5:], [t] + work[:5], **kwargs,
         )
         if not last:
             t, top, bottom = work[4], *work[6:]

time: 146 us -> 145 us (level)
  no operation moved by 1% of the time
where the time goes in v6:
time: 145 us; the launch traced here: 144 us
  waiting for transfers between devices  46.6 us (32%)
  Pallas kernels  39.5 us (27%)
  starting transfers between devices  37.1 us (26%)
  blocking collectives  19.4 us (13%)
    pallas_call x11, Pallas kernels, call(): pl.pallas_call(body, out_shape=[pltpu.VMEM(u.shape, jnp.float32) for u in...  37.4 us
    all_to_all x2, waiting for transfers between devices, shards(): lax.all_to_all(sent(first), 'depth', 0, 0)  29.9 us
    all_gather x1, blocking collectives, shards(): gathered = lax.all_gather(faces, 'axial')  19.4 us
    ppermute x3, starting transfers between devices, up(): return lax.ppermute(x, 'axial', [(i, i + 1) for i in range(n_axial - 1)])  14.4 us
    all_to_all x2, starting transfers between devices, shards(): lax.all_to_all(sent(first), 'depth', 0, 0)  12.1 us
    ppermute x3, waiting for transfers between devices, down(): return lax.ppermute(x, 'axial', [(i + 1, i) for i in range(n_axial - 1)])  8.85 us
    ppermute x3, waiting for transfers between devices, up(): return lax.ppermute(x, 'axial', [(i, i + 1) for i in range(n_axial - 1)])  7.87 us
    ppermute x3, starting transfers between devices, down(): return lax.ppermute(x, 'axial', [(i + 1, i) for i in range(n_axial - 1)])  6.66 us
  transfers between devices with their start and end apart: 9, of which 5 were waited for; matrix products, arithmetic and copies ran while one was open for 0% of the time, Pallas kernels for 15%

profile of v6, /device:TPU:1, one launch (start us, length us, event | category | flops | bytes accessed | tf_op | source)
XLA Modules:
  0.0 144.3 jit_solution(3760866203470312625)
XLA Ops:
  0.6 3.1 %pack1.1 = f32[16,38,8,128]{3,2,1,0:T(8,128)} custom-call(f32[16,8,2048]{2,1,0:T(8,128)} %refs_0_.3, s32[16,8,2048]{2,1,0:T(8,128)} %refs_1_.3, f32[16,8,2048]{2,1,0:T(8,128)} %refs_2_.3, f32[16,8,2048]{2,1,0:T(8,128)} %refs_3_.3), custom_call_target="tpu_custom_call" | custom-call | tf_op jit(solution)/shard_map/pack1/pallas_call | solution.py:43
  3.7 7.6 %all-to-all-start.1 = ((f32[16,38,8,128]{3,2,1,0:T(8,128)}), f32[16,38,8,128]{3,2,1,0:T(8,128)S(1)}, u32[]{:S(2)}, u32[]{:S(2)}) async-start(f32[16,38,8,128]{3,2,1,0:T(8,128)} %pack1.1), calls=%async_computation.1 | async-start | bytes 4980736 | tf_op jit(solution)/shard_map/all_to_all | solution.py:552
  11.3 3.4 %pack2.1 = f32[16,38,8,128]{3,2,1,0:T(8,128)} custom-call(f32[16,8,2048]{2,1,0:T(8,128)} %refs_0_.3, s32[16,8,2048]{2,1,0:T(8,128)} %refs_1_.3, f32[16,8,2048]{2,1,0:T(8,128)} %refs_2_.3, f32[16,8,2048]{2,1,0:T(8,128)} %refs_3_.3), custom_call_target="tpu_custom_call" | custom-call | tf_op jit(solution)/shard_map/pack2/pallas_call | solution.py:43
  14.7 29.9 %all-to-all-done.1.refs_0_.refs_1_ = f32[16,38,8,128]{3,2,1,0:T(8,128)S(1)} async-done(((f32[16,38,8,128]{3,2,1,0:T(8,128)}), f32[16,38,8,128]{3,2,1,0:T(8,128)S(1)}, u32[]{:S(2)}, u32[]{:S(2)}) %all-to-all-start.1) | async-done | bytes 2490400 | tf_op jit(solution)/shard_map/all_to_all | solution.py:552
  44.6 4.5 %all-to-all-start = ((f32[16,38,8,128]{3,2,1,0:T(8,128)}), f32[16,38,8,128]{3,2,1,0:T(8,128)}, u32[]{:S(2)}, u32[]{:S(2)}) async-start(f32[16,38,8,128]{3,2,1,0:T(8,128)} %pack2.1), calls=%async_computation | async-start | bytes 4980736 | tf_op jit(solution)/shard_map/all_to_all | solution.py:552
  49.1 0.0 copy-start.2
  49.1 0.0 copy-start.3
  49.1 0.0 copy-start.4
  49.1 1.5 %rims.1 = (f32[16,16,8,128]{3,2,1,0:T(8,128)}, f32[16,16,8,128]{3,2,1,0:T(8,128)}) custom-call(f32[16,38,8,128]{3,2,1,0:T(8,128)S(1)} %all-to-all-done.1.refs_0_.refs_1_), custom_call_target="tpu_custom_call" | custom-call | tf_op jit(solution)/shard_map/rims/pallas_call | solution.py:43
  50.6 6.5 %collective-permute-start = (f32[16,16,8,128]{3,2,1,0:T(8,128)}, f32[16,16,8,128]{3,2,1,0:T(8,128)S(1)}, u32[]{:S(2)}, u32[]{:S(2)}) collective-permute-start(f32[16,16,8,128]{3,2,1,0:T(8,128)} %get-tuple-element.52), channel_id=1, source_target_pairs={{0,16},{16,32},{32,48},{48,64},{64,80},{80,96},{96,112},{112,128},... | collective-permute-start | bytes 3145736 | tf_op jit(solution)/shard_map/ppermute | solution.py:533
  57.1 1.9 %collective-permute-start.1 = (f32[16,16,8,128]{3,2,1,0:T(8,128)}, f32[16,16,8,128]{3,2,1,0:T(8,128)}, u32[]{:S(2)}, u32[]{:S(2)}) collective-permute-start(f32[16,16,8,128]{3,2,1,0:T(8,128)} %get-tuple-element.53), channel_id=1, source_target_pairs={{16,0},{32,16},{48,32},{64,48},{80,64},{96,80},{112,96},{128,112},... | collective-permute-start | bytes 3145736 | tf_op jit(solution)/shard_map/ppermute | solution.py:536
  59.1 0.0 copy-done.2
  59.1 0.0 copy-done.3
  59.1 0.0 copy-done.4
  59.1 0.7 pad_maximum_fusion.1.refs_0_.refs_1_
  59.8 1.5 %unpack_own.1 = (f32[8,160,128]{2,1,0:T(8,128)S(1)}, f32[8,160,128]{2,1,0:T(8,128)S(1)}, f32[8,160,128]{2,1,0:T(8,128)S(1)}, f32[8,160,128]{2,1,0:T(8,128)S(1)},...) custom-call(f32[4,8]{1,0:T(4,128)S(1)} %pad_maximum_fusion.1.refs_0_.refs_1_, ...), custom_call_target="tpu_custom_call" | custom-call | tf_op jit(solution)/shard_map/unpack_own/pallas_call | solution.py:43
  61.3 7.9 %collective-permute-done.refs_2_ = f32[16,16,8,128]{3,2,1,0:T(8,128)S(1)} collective-permute-done((f32[16,16,8,128]{3,2,1,0:T(8,128)}, f32[16,16,8,128]{3,2,1,0:T(8,128)S(1)}, u32[]{:S(2)}, u32[]{:S(2)}) %collective-permute-start) | collective-permute-done | bytes 1048608 | tf_op jit(solution)/shard_map/ppermute | solution.py:533
  69.2 4.7 %collective-permute-done.1.refs_3_ = f32[16,16,8,128]{3,2,1,0:T(8,128)} collective-permute-done((f32[16,16,8,128]{3,2,1,0:T(8,128)}, f32[16,16,8,128]{3,2,1,0:T(8,128)}, u32[]{:S(2)}, u32[]{:S(2)}) %collective-permute-start.1) | collective-permute-done | bytes 1048608 | tf_op jit(solution)/shard_map/ppermute | solution.py:536
  73.9 7.7 %newton1_outer.1 = (f32[16,160,128]{2,1,0:T(8,128)}, f32[16,160,128]{2,1,0:T(8,128)}, f32[16,160,128]{2,1,0:T(8,128)}, f32[16,160,128]{2,1,0:T(8,128)}, f32[16,1...) custom-call(s32[1]{0:T(128)} %bitcast.refs_0_.place, ...), custom_call_target="tpu_custom_call" | custom-call | tf_op jit(solution)/shard_map/newton1_outer/pallas_call | solution.py:43
  81.6 0.0 all-to-all-done.refs_2_
  81.6 7.7 %newton1.1 = (f32[24,176,128]{2,1,0:T(8,128)S(1)}, f32[24,176,128]{2,1,0:T(8,128)S(1)}, f32[24,176,128]{2,1,0:T(8,128)S(1)}, f32[24,176,128]{2,1,0:T(8,128)S(1)}...) custom-call(s32[1]{0:T(128)} %bitcast.refs_0_.place, ...), custom_call_target="tpu_custom_call" | custom-call | tf_op jit(solution)/shard_map/newton1/pallas_call | solution.py:43
  89.3 6.0 %collective-permute-start.2 = (f32[4,144,128]{2,1,0:T(8,128)S(1)}, f32[4,144,128]{2,1,0:T(8,128)S(1)}, u32[]{:S(2)}, u32[]{:S(2)}) collective-permute-start(f32[4,144,128]{2,1,0:T(8,128)S(1)} %get-tuple-element.69), channel_id=1, source_target_pairs={{0,16},{16,32},{32,48},{48,64},{64,80},{80,96},{96,112},{112,128},... | collective-permute-start | bytes 884744 | tf_op jit(solution)/shard_map/ppermute | solution.py:533
  95.3 2.1 %collective-permute-start.3 = (f32[4,144,128]{2,1,0:T(8,128)S(1)}, f32[4,144,128]{2,1,0:T(8,128)S(1)}, u32[]{:S(2)}, u32[]{:S(2)}) collective-permute-start(f32[4,144,128]{2,1,0:T(8,128)S(1)} %get-tuple-element.70), channel_id=1, source_target_pairs={{16,0},{32,16},{48,32},{64,48},{80,64},{96,80},{112,96},{128,112},... | collective-permute-start | bytes 884744 | tf_op jit(solution)/shard_map/ppermute | solution.py:536
  97.4 1.0 newton1_rest.1
  98.5 3.0 %newton2_inner.1 = (f32[24,176,128]{2,1,0:T(8,128)S(1)}, f32[24,176,128]{2,1,0:T(8,128)S(1)}, f32[24,176,128]{2,1,0:T(8,128)S(1)}, f32[24,176,128]{2,1,0:T(8,128)S(1)}, f32[24,176,128]{2,1,0:T(8,128)S(1)}) custom-call(s32[1]{0:T(128)} %bitcast.refs_0_.place, f32[24,176,128]{2,1,0:T(8,128)S(1)} %get-tuple-element.82.refs_1_.refs_9_, ...), custom_call_target="tpu_custom_call" | custom-call | tf_op jit(solution)/shard_map/newton2_inner/pallas_call | solution.py:43
  101.5 0.0 collective-permute-done.2.refs_1_
  101.5 1.8 %collective-permute-done.3.refs_2_ = f32[4,144,128]{2,1,0:T(8,128)S(1)} collective-permute-done((f32[4,144,128]{2,1,0:T(8,128)S(1)}, f32[4,144,128]{2,1,0:T(8,128)S(1)}, u32[]{:S(2)}, u32[]{:S(2)}) %collective-permute-start.3) | collective-permute-done | bytes 294944 | tf_op jit(solution)/shard_map/ppermute | solution.py:536
  103.4 2.0 %newton2_outer.1 = (f32[24,176,128]{2,1,0:T(8,128)S(1)}, f32[24,176,128]{2,1,0:T(8,128)S(1)}, f32[24,176,128]{2,1,0:T(8,128)S(1)}, f32[24,176,128]{2,1,0:T(8,128...) custom-call(s32[1]{0:T(128)} %bitcast.refs_0_.place, ...), custom_call_target="tpu_custom_call", output_to_operand_aliasing={{0}: (9, {}), {1}: (10, {}), {2}: (11, {}), {3}: (12, {}), ... | custom-call | tf_op jit(solution)/shard_map/newton2_outer/pallas_call | solution.py:43
  105.4 1.9 %collective-permute-start.4 = (f32[4,144,128]{2,1,0:T(8,128)S(1)}, f32[4,144,128]{2,1,0:T(8,128)S(1)}, u32[]{:S(2)}, u32[]{:S(2)}) collective-permute-start(f32[4,144,128]{2,1,0:T(8,128)S(1)} %get-tuple-element.88), channel_id=1, source_target_pairs={{0,16},{16,32},{32,48},{48,64},{64,80},{80,96},{96,112},{112,128},... | collective-permute-start | bytes 884744 | tf_op jit(solution)/shard_map/ppermute | solution.py:533
  107.3 2.6 %collective-permute-start.5 = (f32[4,144,128]{2,1,0:T(8,128)S(1)}, f32[4,144,128]{2,1,0:T(8,128)S(1)}, u32[]{:S(2)}, u32[]{:S(2)}) collective-permute-start(f32[4,144,128]{2,1,0:T(8,128)S(1)} %get-tuple-element.89), channel_id=1, source_target_pairs={{16,0},{32,16},{48,32},{64,48},{80,64},{96,80},{112,96},{128,112},... | collective-permute-start | bytes 884744 | tf_op jit(solution)/shard_map/ppermute | solution.py:536
  109.9 3.3 %newton3_inner.1 = (f32[24,176,128]{2,1,0:T(8,128)S(1)}, f32[24,176,128]{2,1,0:T(8,128)S(1)}, f32[24,176,128]{2,1,0:T(8,128)S(1)}, f32[24,176,128]{2,1,0:T(8,128...) custom-call(s32[1]{0:T(128)} %bitcast.refs_0_.place, ...), custom_call_target="tpu_custom_call" | custom-call | tf_op jit(solution)/shard_map/newton3_inner/pallas_call | solution.py:43
  113.3 0.0 collective-permute-done.4.refs_1_
  113.3 2.3 %collective-permute-done.5.refs_2_ = f32[4,144,128]{2,1,0:T(8,128)S(1)} collective-permute-done((f32[4,144,128]{2,1,0:T(8,128)S(1)}, f32[4,144,128]{2,1,0:T(8,128)S(1)}, u32[]{:S(2)}, u32[]{:S(2)}) %collective-permute-start.5) | collective-permute-done | bytes 294944 | tf_op jit(solution)/shard_map/ppermute | solution.py:536
  115.6 0.0 copy-start
  115.6 0.0 copy-start.1
  115.6 3.0 %newton3_outer.1 = (f32[24,176,128]{2,1,0:T(8,128)S(1)}, f32[24,176,128]{2,1,0:T(8,128)S(1)}, f32[24,176,128]{2,1,0:T(8,128)S(1)}, f32[24,176,128]{2,1,0:T(8,128...) custom-call(s32[1]{0:T(128)} %bitcast.refs_0_.place, ...), custom_call_target="tpu_custom_call", output_to_operand_aliasing={{0}: (11, {}), {1}: (12, {}), {2}: (13, {}), {3}: (14, {}),... | custom-call | tf_op jit(solution)/shard_map/newton3_outer/pallas_call | solution.py:43
  118.6 4.0 %all-to-all-start.2 = ((f32[16,16,8,128]{3,2,1,0:T(8,128)}), f32[16,16,8,128]{3,2,1,0:T(8,128)S(1)}, u32[]{:S(2)}, u32[]{:S(2)}) async-start(f32[16,16,8,128]{3,2,1,0:T(8,128)} %get-tuple-element.99), calls=%async_computation.2 | async-start | bytes 2097152 | tf_op jit(solution)/shard_map/all_to_all | solution.py:603
  122.6 0.0 copy-done
  122.6 0.0 copy-done.1
  122.7 19.4 %all-gather = f32[768,128]{1,0:T(8,128)S(1)} all-gather(f32[48,128]{1,0:T(8,128)S(1)} %pad_maximum_fusion), channel_id=2, replica_groups=mesh['axial'=16,'depth'=16] {'axial'}, dimensions={0}, use_global_device_ids=true | all-gather | bytes 417792 | tf_op jit(solution)/shard_map/all_gather | solution.py:608
  142.0 0.0 all-to-all-done.2.refs_1_
  142.0 2.1 %deliver.1 = (f32[32,128]{1,0:T(8,128)}, f32[16,8,2048]{2,1,0:T(8,128)}) custom-call(s32[1]{0:T(128)} %bitcast.refs_0_.place, f32[16,48,128]{2,1,0:T(8,128)S(1)} %bitcast.7, f32[16,16,8,128]{3,2,1,0:T(8,128)S(1)} %all-to-all-done.2.refs_1_), custom_call_target="tpu_custom_call" | custom-call | tf_op jit(solution)/shard_map/deliver/pallas_call | solution.py:611
  (3 shorter events, 0.0 us)
Async XLA Ops:
  3.7 40.9 %all-to-all-start.1 = ((f32[16,38,8,128]{3,2,1,0:T(8,128)}), f32[16,38,8,128]{3,2,1,0:T(8,128)S(1)}, u32[]{:S(2)}, u32[]{:S(2)}) async-start(f32[16,38,8,128]{3,2,1,0:T(8,128)} %pack1.1), calls=%async_computation.1 | async-start | bytes 4980736 | tf_op jit(solution)/shard_map/all_to_all | solution.py:552
  44.6 37.0 %all-to-all-start = ((f32[16,38,8,128]{3,2,1,0:T(8,128)}), f32[16,38,8,128]{3,2,1,0:T(8,128)}, u32[]{:S(2)}, u32[]{:S(2)}) async-start(f32[16,38,8,128]{3,2,1,0:T(8,128)} %pack2.1), calls=%async_computation | async-start | bytes 4980736 | tf_op jit(solution)/shard_map/all_to_all | solution.py:552
  49.1 10.0 %copy-start.2 = (f32[8]{0:T(128)S(1)}, f32[8]{0:T(128)}, u32[]{:S(2)}) copy-start(f32[8]{0:T(128)} %param.17) | copy-start | bytes 100
  49.1 10.0 %copy-start.3 = (f32[8]{0:T(128)S(1)}, f32[8]{0:T(128)}, u32[]{:S(2)}) copy-start(f32[8]{0:T(128)} %param.16) | copy-start | bytes 100
  49.1 10.0 %copy-start.4 = (f32[8]{0:T(128)S(1)}, f32[8]{0:T(128)}, u32[]{:S(2)}) copy-start(f32[8]{0:T(128)} %param.15) | copy-start | bytes 100
  50.6 18.5 %collective-permute-start = (f32[16,16,8,128]{3,2,1,0:T(8,128)}, f32[16,16,8,128]{3,2,1,0:T(8,128)S(1)}, u32[]{:S(2)}, u32[]{:S(2)}) collective-permute-start(f32[16,16,8,128]{3,2,1,0:T(8,128)} %get-tuple-element.52), channel_id=1, source_target_pairs={{0,16},{16,32},{32,48},{48,64},{64,80},{80,96},{96,112},{112,128},... | collective-permute-start | bytes 3145736 | tf_op jit(solution)/shard_map/ppermute | solution.py:533
  57.1 16.7 %collective-permute-start.1 = (f32[16,16,8,128]{3,2,1,0:T(8,128)}, f32[16,16,8,128]{3,2,1,0:T(8,128)}, u32[]{:S(2)}, u32[]{:S(2)}) collective-permute-start(f32[16,16,8,128]{3,2,1,0:T(8,128)} %get-tuple-element.53), channel_id=1, source_target_pairs={{16,0},{32,16},{48,32},{64,48},{80,64},{96,80},{112,96},{128,112},... | collective-permute-start | bytes 3145736 | tf_op jit(solution)/shard_map/ppermute | solution.py:536
  89.3 12.2 %collective-permute-start.2 = (f32[4,144,128]{2,1,0:T(8,128)S(1)}, f32[4,144,128]{2,1,0:T(8,128)S(1)}, u32[]{:S(2)}, u32[]{:S(2)}) collective-permute-start(f32[4,144,128]{2,1,0:T(8,128)S(1)} %get-tuple-element.69), channel_id=1, source_target_pairs={{0,16},{16,32},{32,48},{48,64},{64,80},{80,96},{96,112},{112,128},... | collective-permute-start | bytes 884744 | tf_op jit(solution)/shard_map/ppermute | solution.py:533
  95.3 8.0 %collective-permute-start.3 = (f32[4,144,128]{2,1,0:T(8,128)S(1)}, f32[4,144,128]{2,1,0:T(8,128)S(1)}, u32[]{:S(2)}, u32[]{:S(2)}) collective-permute-start(f32[4,144,128]{2,1,0:T(8,128)S(1)} %get-tuple-element.70), channel_id=1, source_target_pairs={{16,0},{32,16},{48,32},{64,48},{80,64},{96,80},{112,96},{128,112},... | collective-permute-start | bytes 884744 | tf_op jit(solution)/shard_map/ppermute | solution.py:536
  105.4 7.9 %collective-permute-start.4 = (f32[4,144,128]{2,1,0:T(8,128)S(1)}, f32[4,144,128]{2,1,0:T(8,128)S(1)}, u32[]{:S(2)}, u32[]{:S(2)}) collective-permute-start(f32[4,144,128]{2,1,0:T(8,128)S(1)} %get-tuple-element.88), channel_id=1, source_target_pairs={{0,16},{16,32},{32,48},{48,64},{64,80},{80,96},{96,112},{112,128},... | collective-permute-start | bytes 884744 | tf_op jit(solution)/shard_map/ppermute | solution.py:533
  107.3 8.3 %collective-permute-start.5 = (f32[4,144,128]{2,1,0:T(8,128)S(1)}, f32[4,144,128]{2,1,0:T(8,128)S(1)}, u32[]{:S(2)}, u32[]{:S(2)}) collective-permute-start(f32[4,144,128]{2,1,0:T(8,128)S(1)} %get-tuple-element.89), channel_id=1, source_target_pairs={{16,0},{32,16},{48,32},{64,48},{80,64},{96,80},{112,96},{128,112},... | collective-permute-start | bytes 884744 | tf_op jit(solution)/shard_map/ppermute | solution.py:536
  115.6 7.0 %copy-start = (s32[16,128]{1,0:T(8,128)S(1)}, s32[16,128]{1,0:T(8,128)}, u32[]{:S(2)}) copy-start(s32[16,128]{1,0:T(8,128)} %param.19) | copy-start | bytes 24580
  115.6 7.0 %copy-start.1 = (s32[16,128]{1,0:T(8,128)S(1)}, s32[16,128]{1,0:T(8,128)}, u32[]{:S(2)}) copy-start(s32[16,128]{1,0:T(8,128)} %param.18) | copy-start | bytes 24580
  118.6 23.4 %all-to-all-start.2 = ((f32[16,16,8,128]{3,2,1,0:T(8,128)}), f32[16,16,8,128]{3,2,1,0:T(8,128)S(1)}, u32[]{:S(2)}, u32[]{:S(2)}) async-start(f32[16,16,8,128]{3,2,1,0:T(8,128)} %get-tuple-element.99), calls=%async_computation.2 | async-start | bytes 2097152 | tf_op jit(solution)/shard_map/all_to_all | solution.py:603

commit v7 on v6

--- a/solution.py
+++ b/solution.py
@@ -146,10 +146,24 @@
 
 
 def rims_kernel(scalars, reads, updates, makes, scratch):
-    (arrived,), (top, bottom) = reads, makes
+    (arrived,), (top, bottom), (sems,) = reads, makes, scratch
+    copies = []
     for side, ref in enumerate((bottom, top)):
-        for p, plane in enumerate(rim_planes(side)):
-            ref[:, p] = arrived[:, side * GROUP + plane]
+        order = rim_planes(side)
+        begin = 0
+        for p in range(1, len(order) + 1):
+            if p < len(order) and order[p] == order[p - 1] + 1:
+                continue
+            low = side * GROUP + order[begin]
+            copies.append(
+                pltpu.make_async_copy(
+                    arrived.at[:, low : low + p - begin], ref.at[:, begin:p], sems.at[len(copies)]
+                )
+            )
+            copies[-1].start()
+            begin = p
+    for copy in copies:
+        copy.wait()
 
 
 def suffix_matrix(m_ref):
@@ -551,7 +565,10 @@
 
     arrived = [lax.all_to_all(sent(first), "depth", 0, 0) for first in (True, False)]
     rims = [(n_depth, len(rim_planes(side)), layers, LANES) for side in (1, 0)]
-    top, bottom = call(rims_kernel, "rims", [], arrived[:1], [], rims, kept=False)
+    top, bottom = call(
+        rims_kernel, "rims", [], arrived[:1], [], rims, [pltpu.SemaphoreType.DMA((10,))],
+        space=pl.ANY, out_space=pltpu.HBM,
+    )
     own_rims = call(
         unpack_own_kernel, "unpack_own", [tables], arrived[:1], [], [(2 * H, SPAN, LANES)] * 6
     )

time: 145 us -> 145 us (level)
  no operation moved by 1% of the time
where the time goes in v7:
time: 145 us; the launch traced here: 144 us
  waiting for transfers between devices  46.6 us (32%)
  Pallas kernels  39.3 us (27%)
  starting transfers between devices  37.2 us (26%)
  blocking collectives  19.2 us (13%)
    pallas_call x11, Pallas kernels, call(): pl.pallas_call(body, out_shape=[pltpu.VMEM(u.shape, jnp.float32) for u in...  37.2 us
    all_to_all x2, waiting for transfers between devices, shards(): lax.all_to_all(sent(first), 'depth', 0, 0)  29.9 us
    all_gather x1, blocking collectives, shards(): gathered = lax.all_gather(faces, 'axial')  19.2 us
    ppermute x3, starting transfers between devices, up(): return lax.ppermute(x, 'axial', [(i, i + 1) for i in range(n_axial - 1)])  14.5 us
    all_to_all x2, starting transfers between devices, shards(): lax.all_to_all(sent(first), 'depth', 0, 0)  12.1 us
    ppermute x3, waiting for transfers between devices, down(): return lax.ppermute(x, 'axial', [(i + 1, i) for i in range(n_axial - 1)])  8.85 us
    ppermute x3, waiting for transfers between devices, up(): return lax.ppermute(x, 'axial', [(i, i + 1) for i in range(n_axial - 1)])  7.87 us
    ppermute x3, starting transfers between devices, down(): return lax.ppermute(x, 'axial', [(i + 1, i) for i in range(n_axial - 1)])  6.66 us
  transfers between devices with their start and end apart: 9, of which 5 were waited for; matrix products, arithmetic and copies ran while one was open for 0% of the time, Pallas kernels for 15%

profile of v7, /device:TPU:1, one launch (start us, length us, event | category | flops | bytes accessed | tf_op | source)
XLA Modules:
  0.0 144.2 jit_solution(1175947108626260266)
XLA Ops:
  0.6 3.1 %pack1.1 = f32[16,38,8,128]{3,2,1,0:T(8,128)} custom-call(f32[16,8,2048]{2,1,0:T(8,128)} %refs_0_.3, s32[16,8,2048]{2,1,0:T(8,128)} %refs_1_.3, f32[16,8,2048]{2,1,0:T(8,128)} %refs_2_.3, f32[16,8,2048]{2,1,0:T(8,128)} %refs_3_.3), custom_call_target="tpu_custom_call" | custom-call | tf_op jit(solution)/shard_map/pack1/pallas_call | solution.py:43
  3.7 7.6 %all-to-all-start.1 = ((f32[16,38,8,128]{3,2,1,0:T(8,128)}), f32[16,38,8,128]{3,2,1,0:T(8,128)S(1)}, u32[]{:S(2)}, u32[]{:S(2)}) async-start(f32[16,38,8,128]{3,2,1,0:T(8,128)} %pack1.1), calls=%async_computation.1 | async-start | bytes 4980736 | tf_op jit(solution)/shard_map/all_to_all | solution.py:566
  11.3 3.4 %pack2.1 = f32[16,38,8,128]{3,2,1,0:T(8,128)} custom-call(f32[16,8,2048]{2,1,0:T(8,128)} %refs_0_.3, s32[16,8,2048]{2,1,0:T(8,128)} %refs_1_.3, f32[16,8,2048]{2,1,0:T(8,128)} %refs_2_.3, f32[16,8,2048]{2,1,0:T(8,128)} %refs_3_.3), custom_call_target="tpu_custom_call" | custom-call | tf_op jit(solution)/shard_map/pack2/pallas_call | solution.py:43
  14.7 29.9 %all-to-all-done.1.refs_0_.refs_1_ = f32[16,38,8,128]{3,2,1,0:T(8,128)S(1)} async-done(((f32[16,38,8,128]{3,2,1,0:T(8,128)}), f32[16,38,8,128]{3,2,1,0:T(8,128)S(1)}, u32[]{:S(2)}, u32[]{:S(2)}) %all-to-all-start.1) | async-done | bytes 2490400 | tf_op jit(solution)/shard_map/all_to_all | solution.py:566
  44.6 4.5 %all-to-all-start = ((f32[16,38,8,128]{3,2,1,0:T(8,128)}), f32[16,38,8,128]{3,2,1,0:T(8,128)}, u32[]{:S(2)}, u32[]{:S(2)}) async-start(f32[16,38,8,128]{3,2,1,0:T(8,128)} %pack2.1), calls=%async_computation | async-start | bytes 4980736 | tf_op jit(solution)/shard_map/all_to_all | solution.py:566
  49.1 0.0 copy-start.2
  49.1 0.0 copy-start.3
  49.1 0.0 copy-start.4
  49.1 1.4 rims.1
  50.5 6.5 %collective-permute-start = (f32[16,16,8,128]{3,2,1,0:T(8,128)}, f32[16,16,8,128]{3,2,1,0:T(8,128)S(1)}, u32[]{:S(2)}, u32[]{:S(2)}) collective-permute-start(f32[16,16,8,128]{3,2,1,0:T(8,128)} %get-tuple-element.52), channel_id=1, source_target_pairs={{0,16},{16,32},{32,48},{48,64},{64,80},{80,96},{96,112},{112,128},... | collective-permute-start | bytes 3145736 | tf_op jit(solution)/shard_map/ppermute | solution.py:547
  57.0 1.9 %collective-permute-start.1 = (f32[16,16,8,128]{3,2,1,0:T(8,128)}, f32[16,16,8,128]{3,2,1,0:T(8,128)}, u32[]{:S(2)}, u32[]{:S(2)}) collective-permute-start(f32[16,16,8,128]{3,2,1,0:T(8,128)} %get-tuple-element.53), channel_id=1, source_target_pairs={{16,0},{32,16},{48,32},{64,48},{80,64},{96,80},{112,96},{128,112},... | collective-permute-start | bytes 3145736 | tf_op jit(solution)/shard_map/ppermute | solution.py:550
  58.9 0.0 copy-done.2
  58.9 0.0 copy-done.3
  59.0 0.0 copy-done.4
  59.0 0.7 pad_maximum_fusion.1.refs_0_.refs_1_
  59.6 1.5 %unpack_own.1 = (f32[8,160,128]{2,1,0:T(8,128)S(1)}, f32[8,160,128]{2,1,0:T(8,128)S(1)}, f32[8,160,128]{2,1,0:T(8,128)S(1)}, f32[8,160,128]{2,1,0:T(8,128)S(1)},...) custom-call(f32[4,8]{1,0:T(4,128)S(1)} %pad_maximum_fusion.1.refs_0_.refs_1_, ...), custom_call_target="tpu_custom_call" | custom-call | tf_op jit(solution)/shard_map/unpack_own/pallas_call | solution.py:43
  61.2 7.9 %collective-permute-done.refs_2_ = f32[16,16,8,128]{3,2,1,0:T(8,128)S(1)} collective-permute-done((f32[16,16,8,128]{3,2,1,0:T(8,128)}, f32[16,16,8,128]{3,2,1,0:T(8,128)S(1)}, u32[]{:S(2)}, u32[]{:S(2)}) %collective-permute-start) | collective-permute-done | bytes 1048608 | tf_op jit(solution)/shard_map/ppermute | solution.py:547
  69.0 4.7 %collective-permute-done.1.refs_3_ = f32[16,16,8,128]{3,2,1,0:T(8,128)} collective-permute-done((f32[16,16,8,128]{3,2,1,0:T(8,128)}, f32[16,16,8,128]{3,2,1,0:T(8,128)}, u32[]{:S(2)}, u32[]{:S(2)}) %collective-permute-start.1) | collective-permute-done | bytes 1048608 | tf_op jit(solution)/shard_map/ppermute | solution.py:550
  73.7 7.7 %newton1_outer.1 = (f32[16,160,128]{2,1,0:T(8,128)}, f32[16,160,128]{2,1,0:T(8,128)}, f32[16,160,128]{2,1,0:T(8,128)}, f32[16,160,128]{2,1,0:T(8,128)}, f32[16,1...) custom-call(s32[1]{0:T(128)} %bitcast.refs_0_.place, ...), custom_call_target="tpu_custom_call" | custom-call | tf_op jit(solution)/shard_map/newton1_outer/pallas_call | solution.py:43
  81.5 0.0 all-to-all-done.refs_2_
  81.5 7.7 %newton1.1 = (f32[24,176,128]{2,1,0:T(8,128)S(1)}, f32[24,176,128]{2,1,0:T(8,128)S(1)}, f32[24,176,128]{2,1,0:T(8,128)S(1)}, f32[24,176,128]{2,1,0:T(8,128)S(1)}...) custom-call(s32[1]{0:T(128)} %bitcast.refs_0_.place, ...), custom_call_target="tpu_custom_call" | custom-call | tf_op jit(solution)/shard_map/newton1/pallas_call | solution.py:43
  89.2 6.1 %collective-permute-start.2 = (f32[4,144,128]{2,1,0:T(8,128)S(1)}, f32[4,144,128]{2,1,0:T(8,128)S(1)}, u32[]{:S(2)}, u32[]{:S(2)}) collective-permute-start(f32[4,144,128]{2,1,0:T(8,128)S(1)} %get-tuple-element.69), channel_id=1, source_target_pairs={{0,16},{16,32},{32,48},{48,64},{64,80},{80,96},{96,112},{112,128},... | collective-permute-start | bytes 884744 | tf_op jit(solution)/shard_map/ppermute | solution.py:547
  95.3 2.1 %collective-permute-start.3 = (f32[4,144,128]{2,1,0:T(8,128)S(1)}, f32[4,144,128]{2,1,0:T(8,128)S(1)}, u32[]{:S(2)}, u32[]{:S(2)}) collective-permute-start(f32[4,144,128]{2,1,0:T(8,128)S(1)} %get-tuple-element.70), channel_id=1, source_target_pairs={{16,0},{32,16},{48,32},{64,48},{80,64},{96,80},{112,96},{128,112},... | collective-permute-start | bytes 884744 | tf_op jit(solution)/shard_map/ppermute | solution.py:550
  97.4 1.0 newton1_rest.1
  98.5 3.0 %newton2_inner.1 = (f32[24,176,128]{2,1,0:T(8,128)S(1)}, f32[24,176,128]{2,1,0:T(8,128)S(1)}, f32[24,176,128]{2,1,0:T(8,128)S(1)}, f32[24,176,128]{2,1,0:T(8,128)S(1)}, f32[24,176,128]{2,1,0:T(8,128)S(1)}) custom-call(s32[1]{0:T(128)} %bitcast.refs_0_.place, f32[24,176,128]{2,1,0:T(8,128)S(1)} %get-tuple-element.82.refs_1_.refs_9_, ...), custom_call_target="tpu_custom_call" | custom-call | tf_op jit(solution)/shard_map/newton2_inner/pallas_call | solution.py:43
  101.5 0.0 collective-permute-done.2.refs_1_
  101.5 1.8 %collective-permute-done.3.refs_2_ = f32[4,144,128]{2,1,0:T(8,128)S(1)} collective-permute-done((f32[4,144,128]{2,1,0:T(8,128)S(1)}, f32[4,144,128]{2,1,0:T(8,128)S(1)}, u32[]{:S(2)}, u32[]{:S(2)}) %collective-permute-start.3) | collective-permute-done | bytes 294944 | tf_op jit(solution)/shard_map/ppermute | solution.py:550
  103.4 2.0 %newton2_outer.1 = (f32[24,176,128]{2,1,0:T(8,128)S(1)}, f32[24,176,128]{2,1,0:T(8,128)S(1)}, f32[24,176,128]{2,1,0:T(8,128)S(1)}, f32[24,176,128]{2,1,0:T(8,128...) custom-call(s32[1]{0:T(128)} %bitcast.refs_0_.place, ...), custom_call_target="tpu_custom_call", output_to_operand_aliasing={{0}: (9, {}), {1}: (10, {}), {2}: (11, {}), {3}: (12, {}), ... | custom-call | tf_op jit(solution)/shard_map/newton2_outer/pallas_call | solution.py:43
  105.4 1.9 %collective-permute-start.4 = (f32[4,144,128]{2,1,0:T(8,128)S(1)}, f32[4,144,128]{2,1,0:T(8,128)S(1)}, u32[]{:S(2)}, u32[]{:S(2)}) collective-permute-start(f32[4,144,128]{2,1,0:T(8,128)S(1)} %get-tuple-element.88), channel_id=1, source_target_pairs={{0,16},{16,32},{32,48},{48,64},{64,80},{80,96},{96,112},{112,128},... | collective-permute-start | bytes 884744 | tf_op jit(solution)/shard_map/ppermute | solution.py:547
  107.3 2.6 %collective-permute-start.5 = (f32[4,144,128]{2,1,0:T(8,128)S(1)}, f32[4,144,128]{2,1,0:T(8,128)S(1)}, u32[]{:S(2)}, u32[]{:S(2)}) collective-permute-start(f32[4,144,128]{2,1,0:T(8,128)S(1)} %get-tuple-element.89), channel_id=1, source_target_pairs={{16,0},{32,16},{48,32},{64,48},{80,64},{96,80},{112,96},{128,112},... | collective-permute-start | bytes 884744 | tf_op jit(solution)/shard_map/ppermute | solution.py:550
  109.9 3.3 %newton3_inner.1 = (f32[24,176,128]{2,1,0:T(8,128)S(1)}, f32[24,176,128]{2,1,0:T(8,128)S(1)}, f32[24,176,128]{2,1,0:T(8,128)S(1)}, f32[24,176,128]{2,1,0:T(8,128...) custom-call(s32[1]{0:T(128)} %bitcast.refs_0_.place, ...), custom_call_target="tpu_custom_call" | custom-call | tf_op jit(solution)/shard_map/newton3_inner/pallas_call | solution.py:43
  113.3 0.0 collective-permute-done.4.refs_1_
  113.3 2.3 %collective-permute-done.5.refs_2_ = f32[4,144,128]{2,1,0:T(8,128)S(1)} collective-permute-done((f32[4,144,128]{2,1,0:T(8,128)S(1)}, f32[4,144,128]{2,1,0:T(8,128)S(1)}, u32[]{:S(2)}, u32[]{:S(2)}) %collective-permute-start.5) | collective-permute-done | bytes 294944 | tf_op jit(solution)/shard_map/ppermute | solution.py:550
  115.6 0.0 copy-start
  115.6 0.0 copy-start.1
  115.6 3.0 %newton3_outer.1 = (f32[24,176,128]{2,1,0:T(8,128)S(1)}, f32[24,176,128]{2,1,0:T(8,128)S(1)}, f32[24,176,128]{2,1,0:T(8,128)S(1)}, f32[24,176,128]{2,1,0:T(8,128...) custom-call(s32[1]{0:T(128)} %bitcast.refs_0_.place, ...), custom_call_target="tpu_custom_call", output_to_operand_aliasing={{0}: (11, {}), {1}: (12, {}), {2}: (13, {}), {3}: (14, {}),... | custom-call | tf_op jit(solution)/shard_map/newton3_outer/pallas_call | solution.py:43
  118.6 4.0 %all-to-all-start.2 = ((f32[16,16,8,128]{3,2,1,0:T(8,128)}), f32[16,16,8,128]{3,2,1,0:T(8,128)S(1)}, u32[]{:S(2)}, u32[]{:S(2)}) async-start(f32[16,16,8,128]{3,2,1,0:T(8,128)} %get-tuple-element.99), calls=%async_computation.2 | async-start | bytes 2097152 | tf_op jit(solution)/shard_map/all_to_all | solution.py:620
  122.6 0.0 copy-done
  122.6 0.0 copy-done.1
  122.7 19.2 %all-gather = f32[768,128]{1,0:T(8,128)S(1)} all-gather(f32[48,128]{1,0:T(8,128)S(1)} %pad_maximum_fusion), channel_id=2, replica_groups=mesh['axial'=16,'depth'=16] {'axial'}, dimensions={0}, use_global_device_ids=true | all-gather | bytes 417792 | tf_op jit(solution)/shard_map/all_gather | solution.py:625
  141.9 0.0 all-to-all-done.2.refs_1_
  141.9 2.1 %deliver.1 = (f32[32,128]{1,0:T(8,128)}, f32[16,8,2048]{2,1,0:T(8,128)}) custom-call(s32[1]{0:T(128)} %bitcast.refs_0_.place, f32[16,48,128]{2,1,0:T(8,128)S(1)} %bitcast.7, f32[16,16,8,128]{3,2,1,0:T(8,128)S(1)} %all-to-all-done.2.refs_1_), custom_call_target="tpu_custom_call" | custom-call | tf_op jit(solution)/shard_map/deliver/pallas_call | solution.py:628
  (3 shorter events, 0.0 us)
Async XLA Ops:
  3.7 40.9 %all-to-all-start.1 = ((f32[16,38,8,128]{3,2,1,0:T(8,128)}), f32[16,38,8,128]{3,2,1,0:T(8,128)S(1)}, u32[]{:S(2)}, u32[]{:S(2)}) async-start(f32[16,38,8,128]{3,2,1,0:T(8,128)} %pack1.1), calls=%async_computation.1 | async-start | bytes 4980736 | tf_op jit(solution)/shard_map/all_to_all | solution.py:566
  44.6 36.9 %all-to-all-start = ((f32[16,38,8,128]{3,2,1,0:T(8,128)}), f32[16,38,8,128]{3,2,1,0:T(8,128)}, u32[]{:S(2)}, u32[]{:S(2)}) async-start(f32[16,38,8,128]{3,2,1,0:T(8,128)} %pack2.1), calls=%async_computation | async-start | bytes 4980736 | tf_op jit(solution)/shard_map/all_to_all | solution.py:566
  49.1 9.9 %copy-start.2 = (f32[8]{0:T(128)S(1)}, f32[8]{0:T(128)}, u32[]{:S(2)}) copy-start(f32[8]{0:T(128)} %param.17) | copy-start | bytes 100
  49.1 9.9 %copy-start.3 = (f32[8]{0:T(128)S(1)}, f32[8]{0:T(128)}, u32[]{:S(2)}) copy-start(f32[8]{0:T(128)} %param.16) | copy-start | bytes 100
  49.1 9.9 %copy-start.4 = (f32[8]{0:T(128)S(1)}, f32[8]{0:T(128)}, u32[]{:S(2)}) copy-start(f32[8]{0:T(128)} %param.15) | copy-start | bytes 100
  50.5 18.5 %collective-permute-start = (f32[16,16,8,128]{3,2,1,0:T(8,128)}, f32[16,16,8,128]{3,2,1,0:T(8,128)S(1)}, u32[]{:S(2)}, u32[]{:S(2)}) collective-permute-start(f32[16,16,8,128]{3,2,1,0:T(8,128)} %get-tuple-element.52), channel_id=1, source_target_pairs={{0,16},{16,32},{32,48},{48,64},{64,80},{80,96},{96,112},{112,128},... | collective-permute-start | bytes 3145736 | tf_op jit(solution)/shard_map/ppermute | solution.py:547
  57.0 16.7 %collective-permute-start.1 = (f32[16,16,8,128]{3,2,1,0:T(8,128)}, f32[16,16,8,128]{3,2,1,0:T(8,128)}, u32[]{:S(2)}, u32[]{:S(2)}) collective-permute-start(f32[16,16,8,128]{3,2,1,0:T(8,128)} %get-tuple-element.53), channel_id=1, source_target_pairs={{16,0},{32,16},{48,32},{64,48},{80,64},{96,80},{112,96},{128,112},... | collective-permute-start | bytes 3145736 | tf_op jit(solution)/shard_map/ppermute | solution.py:550
  89.2 12.3 %collective-permute-start.2 = (f32[4,144,128]{2,1,0:T(8,128)S(1)}, f32[4,144,128]{2,1,0:T(8,128)S(1)}, u32[]{:S(2)}, u32[]{:S(2)}) collective-permute-start(f32[4,144,128]{2,1,0:T(8,128)S(1)} %get-tuple-element.69), channel_id=1, source_target_pairs={{0,16},{16,32},{32,48},{48,64},{64,80},{80,96},{96,112},{112,128},... | collective-permute-start | bytes 884744 | tf_op jit(solution)/shard_map/ppermute | solution.py:547
  95.3 8.0 %collective-permute-start.3 = (f32[4,144,128]{2,1,0:T(8,128)S(1)}, f32[4,144,128]{2,1,0:T(8,128)S(1)}, u32[]{:S(2)}, u32[]{:S(2)}) collective-permute-start(f32[4,144,128]{2,1,0:T(8,128)S(1)} %get-tuple-element.70), channel_id=1, source_target_pairs={{16,0},{32,16},{48,32},{64,48},{80,64},{96,80},{112,96},{128,112},... | collective-permute-start | bytes 884744 | tf_op jit(solution)/shard_map/ppermute | solution.py:550
  105.4 7.9 %collective-permute-start.4 = (f32[4,144,128]{2,1,0:T(8,128)S(1)}, f32[4,144,128]{2,1,0:T(8,128)S(1)}, u32[]{:S(2)}, u32[]{:S(2)}) collective-permute-start(f32[4,144,128]{2,1,0:T(8,128)S(1)} %get-tuple-element.88), channel_id=1, source_target_pairs={{0,16},{16,32},{32,48},{48,64},{64,80},{80,96},{96,112},{112,128},... | collective-permute-start | bytes 884744 | tf_op jit(solution)/shard_map/ppermute | solution.py:547
  107.3 8.3 %collective-permute-start.5 = (f32[4,144,128]{2,1,0:T(8,128)S(1)}, f32[4,144,128]{2,1,0:T(8,128)S(1)}, u32[]{:S(2)}, u32[]{:S(2)}) collective-permute-start(f32[4,144,128]{2,1,0:T(8,128)S(1)} %get-tuple-element.89), channel_id=1, source_target_pairs={{16,0},{32,16},{48,32},{64,48},{80,64},{96,80},{112,96},{128,112},... | collective-permute-start | bytes 884744 | tf_op jit(solution)/shard_map/ppermute | solution.py:550
  115.6 7.0 %copy-start = (s32[16,128]{1,0:T(8,128)S(1)}, s32[16,128]{1,0:T(8,128)}, u32[]{:S(2)}) copy-start(s32[16,128]{1,0:T(8,128)} %param.19) | copy-start | bytes 24580
  115.6 7.0 %copy-start.1 = (s32[16,128]{1,0:T(8,128)S(1)}, s32[16,128]{1,0:T(8,128)}, u32[]{:S(2)}) copy-start(s32[16,128]{1,0:T(8,128)} %param.18) | copy-start | bytes 24580
  118.6 23.3 %all-to-all-start.2 = ((f32[16,16,8,128]{3,2,1,0:T(8,128)}), f32[16,16,8,128]{3,2,1,0:T(8,128)S(1)}, u32[]{:S(2)}, u32[]{:S(2)}) async-start(f32[16,16,8,128]{3,2,1,0:T(8,128)} %get-tuple-element.99), calls=%async_computation.2 | async-start | bytes 2097152 | tf_op jit(solution)/shard_map/all_to_all | solution.py:620
